TPU v7x, 32 devices: a whole 2x2x4 slice. The times are simulated.
32 devices in a mesh: grp: 4 (over x, core), sub: 8 (over z, y).
Axes of the slice: x: 2, y: 2, z: 4, core: 2. Of those that a mesh axis runs over, the one named last changes fastest.
Arguments:
- embeddings: bfloat16 [24576, 1024], P(('grp', 'sub')), may hold values from -6 to 6
- cluster_id: int32 [24576], P(('grp', 'sub')), may hold values from 0 to 3, as said below
- cluster_rank: int32 [24576], P(('grp', 'sub')), may hold values from 0 to 6143, as said below
Outputs:
- best_similarity: float32 [24576], P(('grp', 'sub'))
Inputs may be any that keep to these rules, and one draw needn't show every extreme that they name: `cluster_id`: every cluster 0 to 3 holds exactly 6144 documents. `cluster_rank`: within each cluster the ranks are a permutation of 0 to 6143. The documents of one device include at most 24 of one cluster whose ranks lie in one aligned block of 384 ranks, and some device has exactly 24.
All inputs are finite; a program needn't handle non-finite values.
Results may differ from a plain program's by a relative error of at most 0.0013.
Values may be sent and summed in bfloat16 or wider, within the bound.
No kernel may reach another device: no remote copies, remote signals or barrier semaphores. Data moves between devices by JAX's collectives and lax.ppermute only.
A program may use at most 128 MiB of HBM per device.

v0:
```python
import jax
import jax.numpy as jnp
from jax import lax
from jax.sharding import PartitionSpec as P


def from_behind(block, axis, distance):
    devices = range(lax.axis_size(axis))
    route = [((i - distance) % len(devices), i) for i in devices]
    return lax.ppermute(block, axis, route)


def product(left, right):
    return lax.dot_general(
        left, right, (((1,), (1,)), ((), ())), preferred_element_type=jnp.float32
    )


def body(embeddings, cluster_id, cluster_rank):
    rows = embeddings.shape[0]
    width = embeddings.shape[1]
    half = rows // 2
    nsub = lax.axis_size("sub")
    ngrp = lax.axis_size("grp")
    ndev = nsub * ngrp
    capacity = rows // ndev
    total = 2 * ndev * capacity
    wide = embeddings.astype(jnp.float32)
    unit = (wide * lax.rsqrt(jnp.sum(wide * wide, axis=1, keepdims=True) + 1e-06)).astype(
        jnp.bfloat16
    )
    bucket = cluster_id * (2 * nsub) + cluster_rank // half
    onehot = (bucket[:, None] == jnp.arange(2 * ndev, dtype=jnp.int32)[None, :]).astype(
        jnp.bfloat16
    )
    index_rows = jnp.arange(rows, dtype=jnp.int32)
    lower = (index_rows[:, None] > index_rows[None, :]).astype(jnp.bfloat16)
    before = jnp.dot(lower, onehot, preferred_element_type=jnp.float32)
    slot = jnp.sum(before * onehot, axis=1).astype(jnp.int32)
    place = bucket * capacity + slot
    send_rows = jnp.zeros((total, width), jnp.bfloat16).at[place].set(unit)
    send_rank = jnp.full((total,), -1, jnp.int32).at[place].set(cluster_rank)
    recv_rows, recv_rank = (
        lax.all_to_all(
            send_rows.reshape(ndev, 2 * capacity, width),
            ("grp", "sub"),
            split_axis=0,
            concat_axis=0,
            tiled=True,
        ),
        lax.all_to_all(
            send_rank.reshape(ndev, 2 * capacity),
            ("grp", "sub"),
            split_axis=0,
            concat_axis=0,
            tiled=True,
        ),
    )
    recv_rows = recv_rows.reshape(total, width)
    recv_rank = recv_rank.reshape(total)
    member = lax.axis_index("sub")
    local_pos = jnp.where(recv_rank >= 0, recv_rank - member * rows, rows).astype(jnp.int32)
    local = jnp.zeros((rows, width), jnp.bfloat16).at[local_pos].set(recv_rows, mode="drop")
    own_rank = member * rows + index_rows
    lowest = jnp.float32(-1.0)
    sims = product(local, local)
    best = jnp.max(jnp.where(own_rank[None, :] < own_rank[:, None], sims, lowest), axis=1)
    column = jnp.full((nsub, rows), -1.0, jnp.float32)
    other = local
    members = jnp.arange(nsub, dtype=jnp.int32)
    for step in range(1, nsub // 2 + 1):
        other = from_behind(other, "sub", 1)
        peer = (member - step) % nsub
        their = peer * rows + index_rows
        sims = product(local, other)
        row_mask = their[None, :] < own_rank[:, None]
        best = jnp.maximum(best, jnp.max(jnp.where(row_mask, sims, lowest), axis=1))
        col_mask = own_rank[:, None] < their[None, :]
        col_best = jnp.max(jnp.where(col_mask, sims, lowest), axis=0)
        column = jnp.maximum(column, jnp.where(members[:, None] == peer, col_best[None, :], lowest))
    merged = lax.pmax(column, "sub")
    best = jnp.maximum(best, lax.dynamic_index_in_dim(merged, member, 0, keepdims=False))
    back = jnp.where(recv_rank >= 0, best[jnp.clip(local_pos, 0, rows - 1)], 0.0)
    returned = lax.all_to_all(
        back.reshape(ndev, 2 * capacity), ("grp", "sub"), split_axis=0, concat_axis=0, tiled=True
    )
    return returned.reshape(total)[place]


def solution(mesh):
    placed = (P(("grp", "sub"), None), P(("grp", "sub")), P(("grp", "sub")))
    return jax.shard_map(
        body, mesh=mesh, in_specs=placed, out_specs=P(("grp", "sub")), check_vma=False
    )
```

profile of v0, /device:TPU:0, one launch (start us, length us, event | category | flops | bytes accessed | tf_op | source)
XLA Modules:
  0.0 321.8 jit_solution(1389017039937995896)
XLA Ops:
  0.0 0.8 fusion.16
  1.2 3.5 %scatter_custom_fusion = s32[1536]{0:T(1024)S(1)} fusion(s32[768]{0:T(1024)S(1)} %compare_select_fusion.4, s32[768]{0:T(1024)} %param.5, s32[]{:T(128)} %constant.34.clone.1), kind=kCustom, calls=%fused_computation.52 | custom fusion | bytes 6656 | tf_op jit(solution)/shard_map/scatter | solution.py:42
  4.8 0.7 all_to_all.13
  5.5 7.3 %all-to-all-start = ((s32[32,1,48]{2,1,0:T(1,128)}), s32[32,1,48]{2,1,0:T(1,128)S(1)}, u32[]{:S(2)}, u32[]{:S(2)}) async-start(s32[32,1,48]{2,1,0:T(1,128)} %all_to_all.13), calls=%async_computation | async-start | bytes 32768 | tf_op jit(solution)/shard_map/all_to_all | solution.py:51
  12.8 1.8 fusion
  14.6 8.4 %scatter_custom_fusion.1 = bf16[1536,1024]{1,0:T(8,128)(2,1)} fusion(s32[768]{0:T(1024)S(1)} %compare_select_fusion.4, bf16[768,1024]{1,0:T(8,128)(2,1)S(1)} %copy-done, f32[768]{0:T(1024)S(1)} %add_rsqrt_fusion, bf16[]{:T(256)} %constant.71.clone.1), kind=kCustom, calls=%fused_computation.20 | custom fusion | flops 2359296 | bytes 4722690 | tf_op jit(solution)/shard_map/scatter | solution.py:41
  23.0 5.8 %all-to-all-start.1 = ((bf16[32,48,1024]{2,1,0:T(8,128)(2,1)}), bf16[32,48,1024]{2,1,0:T(8,128)(2,1)S(1)}, u32[]{:S(2)}, u32[]{:S(2)}) async-start(bf16[32,48,1024]{2,1,0:T(8,128)(2,1)} %bitcast), calls=%async_computation.1 | async-start | bytes 6291456 | tf_op jit(solution)/shard_map/all_to_all | solution.py:44
  29.1 72.9 %all-to-all-done.1 = bf16[32,48,1024]{2,1,0:T(8,128)(2,1)S(1)} async-done(((bf16[32,48,1024]{2,1,0:T(8,128)(2,1)}), bf16[32,48,1024]{2,1,0:T(8,128)(2,1)S(1)}, u32[]{:S(2)}, u32[]{:S(2)}) %all-to-all-start.1) | async-done | bytes 3145760 | tf_op jit(solution)/shard_map/all_to_all | solution.py:44
  101.9 8.8 %scatter_custom_fusion.2 = bf16[768,1024]{1,0:T(8,128)(2,1)} fusion(s32[1536]{0:T(1024)S(1)} %get-tuple-element.14, bf16[1536,1024]{1,0:T(8,128)(2,1)S(1)} %bitcast.15, bf16[]{:T(256)} %constant.71.clone.1), kind=kCustom, calls=%fused_computation.25 | custom fusion | bytes 1572866 | tf_op jit(solution)/shard_map/scatter | solution.py:63
  110.7 39.0 %collective-permute-done = bf16[768,1024]{1,0:T(8,128)(2,1)S(1)} collective-permute-done((bf16[768,1024]{1,0:T(8,128)(2,1)}, bf16[768,1024]{1,0:T(8,128)(2,1)S(1)}, u32[]{:S(2)}, u32[]{:S(2)}) %collective-permute-start) | collective-permute-done | bytes 1572896 | tf_op jit(solution)/shard_map/ppermute | solution.py:10
  149.8 38.1 %collective-permute-done.1 = bf16[768,1024]{1,0:T(8,128)(2,1)} collective-permute-done((bf16[768,1024]{1,0:T(8,128)(2,1)S(1)}, bf16[768,1024]{1,0:T(8,128)(2,1)}, u32[]{:S(2)}, u32[]{:S(2)}) %collective-permute-start.1) | collective-permute-done | bytes 1572896 | tf_op jit(solution)/shard_map/ppermute | solution.py:10
  187.9 37.3 %collective-permute-done.2 = bf16[768,1024]{1,0:T(8,128)(2,1)} collective-permute-done((bf16[768,1024]{1,0:T(8,128)(2,1)}, bf16[768,1024]{1,0:T(8,128)(2,1)}, u32[]{:S(2)}, u32[]{:S(2)}) %collective-permute-start.2) | collective-permute-done | bytes 1572896 | tf_op jit(solution)/shard_map/ppermute | solution.py:10
  225.2 3.4 %select_reduce_fusion.8 = f32[768]{0:T(1024)S(1)} fusion(bf16[768,1024]{1,0:T(8,128)(2,1)} %scatter_custom_fusion.2, s32[768]{0:T(1024)S(1)} %iota_add_fusion.4), kind=kOutput, calls=%fused_computation.17 | convolution fusion | flops 1209728256 | bytes 1579008 | tf_op jit(solution)/shard_map/dot_general | solution.py:14
  228.7 1.4 fusion.20
  230.2 2.8 fusion.21
  233.0 2.9 fusion.22
  235.9 25.7 %collective-permute-done.3 = bf16[768,1024]{1,0:T(8,128)(2,1)S(1)} collective-permute-done((bf16[768,1024]{1,0:T(8,128)(2,1)}, bf16[768,1024]{1,0:T(8,128)(2,1)S(1)}, u32[]{:S(2)}, u32[]{:S(2)}) %collective-permute-start.3) | collective-permute-done | bytes 1572896 | tf_op jit(solution)/shard_map/ppermute | solution.py:10
  261.6 3.4 %select_reduce_fusion.7 = (f32[768]{0:T(1024)S(1)}, f32[768]{0:T(1024)S(1)}, f32[768]{0:T(1024)S(1)}, f32[768]{0:T(1024)S(1)}, f32[768]{0:T(1024)S(1)}, /*index=...) fusion(f32[768,768]{0,1:T(8,128)S(1)} %fusion.20, s32[768]{0:T(1024)S(1)} %iota_add_fusion.4, ...), kind=kOutput, calls=%fused_computation.16 | convolution fusion | flops 1222109184 | bytes 10263552 | tf_op jit(solution)/shard_map/dot_general | solution.py:14
  265.0 33.0 %pmax.7 = f32[8,768]{1,0:T(8,128)S(1)} all-reduce(f32[8,768]{1,0:T(8,128)S(1)} %select_maximum_fusion), channel_id=1, replica_groups=mesh['grp'=4,'sub'=8] {'sub'}, use_global_device_ids=true, to_apply=%region_14.15 | all-reduce | flops 6144 | bytes 49152 | tf_op jit(solution)/shard_map/pmax | solution.py:81
  298.1 5.9 %gather_fusion = f32[1536]{0:T(1024)S(1)} fusion(f32[768]{0:T(1024)S(1)} %maximum_maximum_fusion, s32[2048]{0:T(1024)S(1)} %pad_clamp_fusion), kind=kCustom, calls=%fused_computation | custom fusion | bytes 18432 | tf_op jit(solution)/shard_map/gather | solution.py:83
  304.7 2.6 all-to-all-start.2
  307.3 7.1 %all-to-all-done.2 = f32[32,1,48]{2,1,0:T(1,128)S(1)} async-done(((f32[32,1,48]{2,1,0:T(1,128)}), f32[32,1,48]{2,1,0:T(1,128)S(1)}, u32[]{:S(2)}, u32[]{:S(2)}) %all-to-all-start.2) | async-done | bytes 6176 | tf_op jit(solution)/shard_map/all_to_all | solution.py:84
  314.9 0.7 reduce.13
  315.6 6.1 %gather_fusion.1 = f32[768]{0:T(1024)} fusion(f32[1536]{0:T(1024)S(1)} %reshape.135, s32[1024]{0:T(1024)S(1)} %pad_clamp_fusion.1), kind=kCustom, calls=%fused_computation.1 | custom fusion | bytes 9216 | tf_op jit(solution)/shard_map/gather | solution.py:87
  (29 shorter events, 2.0 us)
Async XLA Ops:
  0.0 14.6 %copy-start = (bf16[768,1024]{1,0:T(8,128)(2,1)S(1)}, bf16[768,1024]{1,0:T(8,128)(2,1)}, u32[]{:S(2)}) copy-start(bf16[768,1024]{1,0:T(8,128)(2,1)} %param.3) | copy-start | bytes 4718596
  5.5 17.5 %all-to-all-start = ((s32[32,1,48]{2,1,0:T(1,128)}), s32[32,1,48]{2,1,0:T(1,128)S(1)}, u32[]{:S(2)}, u32[]{:S(2)}) async-start(s32[32,1,48]{2,1,0:T(1,128)} %all_to_all.13), calls=%async_computation | async-start | bytes 32768 | tf_op jit(solution)/shard_map/all_to_all | solution.py:51
  23.0 78.9 %all-to-all-start.1 = ((bf16[32,48,1024]{2,1,0:T(8,128)(2,1)}), bf16[32,48,1024]{2,1,0:T(8,128)(2,1)S(1)}, u32[]{:S(2)}, u32[]{:S(2)}) async-start(bf16[32,48,1024]{2,1,0:T(8,128)(2,1)} %bitcast), calls=%async_computation.1 | async-start | bytes 6291456 | tf_op jit(solution)/shard_map/all_to_all | solution.py:44
  110.7 39.0 %collective-permute-start = (bf16[768,1024]{1,0:T(8,128)(2,1)}, bf16[768,1024]{1,0:T(8,128)(2,1)S(1)}, u32[]{:S(2)}, u32[]{:S(2)}) collective-permute-start(bf16[768,1024]{1,0:T(8,128)(2,1)} %scatter_custom_fusion.2), channel_id=1, source_target_pairs={{7,0},{0,1},{1,2},{2,3},{3,4},{4,5},{5,6},{6,7},{15,8},{8,9},{9,10... | collective-permute-start | bytes 4718600 | tf_op jit(solution)/shard_map/ppermute | solution.py:10
  149.8 38.1 %collective-permute-start.1 = (bf16[768,1024]{1,0:T(8,128)(2,1)S(1)}, bf16[768,1024]{1,0:T(8,128)(2,1)}, u32[]{:S(2)}, u32[]{:S(2)}) collective-permute-start(bf16[768,1024]{1,0:T(8,128)(2,1)S(1)} %collective-permute-done), channel_id=1, source_target_pairs={{7,0},{0,1},{1,2},{2,3},{3,4},{4,5},{5,6},{6,7},{15,8},{8,9},{9,10... | collective-permute-start | bytes 4718600 | tf_op jit(solution)/shard_map/ppermute | solution.py:10
  187.9 37.4 %collective-permute-start.2 = (bf16[768,1024]{1,0:T(8,128)(2,1)}, bf16[768,1024]{1,0:T(8,128)(2,1)}, u32[]{:S(2)}, u32[]{:S(2)}) collective-permute-start(bf16[768,1024]{1,0:T(8,128)(2,1)} %collective-permute-done.1), channel_id=1, source_target_pairs={{7,0},{0,1},{1,2},{2,3},{3,4},{4,5},{5,6},{6,7},{15,8},{8,9},{9,10... | collective-permute-start | bytes 4718600 | tf_op jit(solution)/shard_map/ppermute | solution.py:10
  225.2 36.3 %collective-permute-start.3 = (bf16[768,1024]{1,0:T(8,128)(2,1)}, bf16[768,1024]{1,0:T(8,128)(2,1)S(1)}, u32[]{:S(2)}, u32[]{:S(2)}) collective-permute-start(bf16[768,1024]{1,0:T(8,128)(2,1)} %collective-permute-done.2), channel_id=1, source_target_pairs={{7,0},{0,1},{1,2},{2,3},{3,4},{4,5},{5,6},{6,7},{15,8},{8,9},{9,10... | collective-permute-start | bytes 4718600 | tf_op jit(solution)/shard_map/ppermute | solution.py:10
  225.2 3.5 %copy-start.1 = (bf16[768,1024]{1,0:T(8,128)(2,1)S(1)}, bf16[768,1024]{1,0:T(8,128)(2,1)}, u32[]{:S(2)}) copy-start(bf16[768,1024]{1,0:T(8,128)(2,1)} %scatter_custom_fusion.2) | copy-start | bytes 4718596
  304.7 9.7 %all-to-all-start.2 = ((f32[32,1,48]{2,1,0:T(1,128)}), f32[32,1,48]{2,1,0:T(1,128)S(1)}, u32[]{:S(2)}, u32[]{:S(2)}) async-start(f32[32,1,48]{2,1,0:T(1,128)} %compare_select_fusion.2), calls=%async_computation.2 | async-start | bytes 32768 | tf_op jit(solution)/shard_map/all_to_all | solution.py:84
where the time goes:
time: 322 us
  waiting for transfers between devices  220 us (68%)
  blocking collectives  33 us (10%)
  local copies, waits for them, and re-layouts  25.8 us (8%)
  starting transfers between devices  15.7 us (5%)
  matrix products  14.3 us (4%)
  other arithmetic  12.6 us (4%)
    ppermute x4, waiting for transfers between devices, from_behind(): return lax.ppermute(block, axis, route)  140 us
    all_to_all x1, waiting for transfers between devices, body(): lax.all_to_all(send_rows.reshape(ndev, 2 * capacity, width), ('grp', 'sub...  72.9 us
    pmax x1, blocking collectives, body(): merged = lax.pmax(column, 'sub')  33 us
    dot_general x5, matrix products, product(): lax.dot_general(left, right, (((1,), (1,)), ((), ())), preferred_element_...  14 us
    scatter x1, local copies, waits for them, and re-layouts, body(): jnp.zeros((rows, width), jnp.bfloat16).at[local_pos]  8.82 us
    scatter x1, other arithmetic, body(): send_rows = jnp.zeros((total, width), jnp.bfloat16).at[place].set(unit)  8.41 us
    all_to_all x1, starting transfers between devices, body(): lax.all_to_all(send_rank.reshape(ndev, 2 * capacity), ('grp', 'sub'), spl...  7.3 us
    all_to_all x1, waiting for transfers between devices, body(): lax.all_to_all(back.reshape(ndev, 2 * capacity), ('grp', 'sub'), split_ax...  7.1 us
  transfers between devices with their start and end apart: 7, of which 6 were waited for; matrix products, arithmetic and copies ran while one was open for 7% of the time, Pallas kernels for 0%

commit v1 on v0

v1 whole, which is shorter than its diff:
```python
import functools

import jax
import jax.numpy as jnp
from jax import lax
from jax.experimental import pallas as pl
from jax.experimental.pallas import tpu as pltpu
from jax.sharding import PartitionSpec as P

AXES = ("grp", "sub")
LANES = 128
QUERY_TILE = 256
RADIX = 128
EMPTY = 255.0
VMEM = 56 * 1024 * 1024


def ceil_to(value, unit):
    return -(-value // unit) * unit


def nt_dot(left, right):
    return lax.dot_general(
        left, right, (((1,), (1,)), ((), ())), preferred_element_type=jnp.float32
    )


def dispatch_kernel(pieces, low, cap, flagged, emb, cid, rank, *refs):
    outs, place_ref, unit, slot_ref = refs[:pieces], refs[pieces], refs[pieces + 1], refs[pieces + 2]
    rows, width = emb.shape
    wide_lanes = ceil_to(cap, LANES)
    plane = lax.axis_index("sub") // low

    @pl.loop(0, rows // 64)
    def _(i):
        at = pl.ds(pl.multiple_of(i * 64, 64), 64)
        wide = emb[at, :].astype(jnp.float32)
        scale = lax.rsqrt(jnp.sum(wide * wide, axis=1, keepdims=True) + 1e-06)
        unit[at, :] = (wide * scale).astype(jnp.bfloat16)

    piece = cid[...] ^ plane
    which = lax.broadcasted_iota(jnp.int32, (16, LANES), 0)
    upper = (
        lax.broadcasted_iota(jnp.int32, (LANES, LANES), 0)
        < lax.broadcasted_iota(jnp.int32, (LANES, LANES), 1)
    ).astype(jnp.bfloat16)
    before = jnp.zeros((16, 1), jnp.float32)
    for b in range(rows // LANES):
        lanes = slice(b * LANES, (b + 1) * LANES)
        member = piece[:, lanes] == which
        ones = member.astype(jnp.float32)
        prefix = jnp.dot(ones.astype(jnp.bfloat16), upper, preferred_element_type=jnp.float32)
        slot = jnp.sum(jnp.where(member, prefix + before, 0.0), axis=0, keepdims=True)
        slot_ref[:, lanes] = slot.astype(jnp.int32)
        before = before + jnp.sum(ones, axis=1, keepdims=True)
    slot = slot_ref[...]
    place_ref[...] = piece * cap + slot
    full = jnp.max(before, axis=0, keepdims=True) > cap - 1
    full = full.astype(jnp.float32)

    target = piece * 1024 + slot
    r = rank[...]
    digits = jnp.concatenate(
        [
            (r // RADIX).astype(jnp.float32),
            (r % RADIX).astype(jnp.float32),
            jnp.ones((1, rows), jnp.float32),
            jnp.zeros((13, rows), jnp.float32),
        ],
        axis=0,
    ).astype(jnp.bfloat16)
    for s in range(pieces):
        slots = lax.broadcasted_iota(jnp.int32, (wide_lanes, rows), 0) + s * 1024
        pick = jnp.where(slots == target, 1.0, 0.0).astype(jnp.bfloat16)
        ranks = nt_dot(digits, pick)
        filled = ranks[2:3, :] > 0.5
        high = jnp.where(filled, ranks[0:1, :], EMPTY)
        parts = [high, ranks[1:2, :]]
        if flagged:
            parts.append(jnp.broadcast_to(full, (1, LANES)))
        used = 2 * wide_lanes + (LANES if flagged else 0)
        if used < width:
            parts.append(jnp.zeros((1, width - used), jnp.float32))
        note = jnp.concatenate(parts, axis=1)
        moved = jnp.dot(pick[:cap], unit[...], preferred_element_type=jnp.float32)
        outs[s][: cap - 16, :] = moved[: cap - 16].astype(jnp.bfloat16)
        last = lax.broadcasted_iota(jnp.int32, (16, 1), 0) == 15
        outs[s][cap - 16 :, :] = jnp.where(last, note, moved[cap - 16 :]).astype(jnp.bfloat16)


def dispatch(pieces, low, cap, flagged, emb, cid, rank):
    rows, width = emb.shape
    return pl.pallas_call(
        functools.partial(dispatch_kernel, pieces, low, cap, flagged),
        out_shape=[jax.ShapeDtypeStruct((cap, width), jnp.bfloat16)] * pieces
        + [jax.ShapeDtypeStruct((1, rows), jnp.int32)],
        scratch_shapes=[
            pltpu.VMEM((rows, width), jnp.bfloat16),
            pltpu.VMEM((1, rows), jnp.int32),
        ],
        compiler_params=pltpu.CompilerParams(vmem_limit_bytes=VMEM),
        name="dispatch",
    )(emb, cid.reshape(1, rows), rank.reshape(1, rows))


def similarity_kernel(pieces, ncross, cap, flagged, chunk, *refs):
    nblocks = pieces * (4 + ncross)
    blocks, refs = refs[:nblocks], refs[nblocks:]
    out_own, out_twin, out_near, out_far = refs[:4]
    home, away, cross, home_rank, away_rank, home_key, away_key, cross_key, best, sem = refs[4:]
    span = pieces * cap
    queries = home.shape[0]
    wide_lanes = ceil_to(cap, LANES)

    copies = []
    for i, block in enumerate(blocks):
        group, p = divmod(i, pieces)
        buffer, base = (
            (home, group * span) if group < 2 else
            (away, (group - 2) * span) if group < 4 else
            (cross, (group - 4) * span)
        )
        copies.append((group, p, buffer, base + p * cap))
        pltpu.make_async_copy(block, buffer.at[pl.ds(base + p * cap, cap), :], sem.at[i]).start()

    for buffer in (home, away):
        if queries > 2 * span:
            buffer[2 * span :, :] = jnp.zeros((queries - 2 * span, buffer.shape[1]), jnp.bfloat16)

    lane = lax.broadcasted_iota(jnp.int32, (1, wide_lanes), 1)
    square = lax.broadcasted_iota(jnp.int32, (cap, wide_lanes), 0) == lax.broadcasted_iota(
        jnp.int32, (cap, wide_lanes), 1
    )
    home_ranks = jnp.zeros((8, queries), jnp.float32)
    away_ranks = jnp.zeros((8, queries), jnp.float32)
    flag = jnp.zeros((1, LANES), jnp.float32)
    for i, (group, p, buffer, base) in enumerate(copies):
        pltpu.make_async_copy(blocks[i], buffer.at[pl.ds(base, cap), :], sem.at[i]).wait()
        note = buffer[base + cap - 16 : base + cap, :].astype(jnp.float32)[15:16, :]
        ranks = note[:, :wide_lanes] * RADIX + note[:, wide_lanes : 2 * wide_lanes]
        ranks = jnp.where(lane < cap - 1, ranks, EMPTY * RADIX)
        if flagged:
            flag = jnp.maximum(flag, note[:, 2 * wide_lanes : 2 * wide_lanes + LANES])
        if group < 4:
            kept = jnp.where(lane < cap, ranks, 0.0)
            row = jnp.concatenate(
                [kept, jnp.zeros((1, queries - wide_lanes), jnp.float32)], axis=1
            )
            row = pltpu.roll(jnp.broadcast_to(row, (8, queries)), base, 1)
            if group < 2:
                home_ranks = home_ranks + row
            else:
                away_ranks = away_ranks + row
        if group in (0, 2) or group >= 4:
            keys = home_key if group == 0 else away_key if group == 2 else cross_key
            column = jnp.sum(jnp.where(square, ranks, 0.0), axis=1, keepdims=True)
            keys[base : base + cap, :] = jnp.broadcast_to(column, (cap, LANES))
    home_rank[...] = home_ranks
    away_rank[...] = away_ranks

    def sweep(rows, row_rank, key_sets):
        @pl.loop(0, queries // QUERY_TILE)
        def _(t):
            at = pl.ds(pl.multiple_of(t * QUERY_TILE, QUERY_TILE), QUERY_TILE)
            query = rows[at, :]
            limit = row_rank[0:1, at]
            top = jnp.full((8, QUERY_TILE), -1.0, jnp.float32)
            for keys, key_rank, total in key_sets:
                for first in range(0, total, chunk):
                    sims = nt_dot(keys[first : first + chunk, :], query)
                    kr = key_rank[first : first + chunk, :]
                    kr = jnp.concatenate([kr] * (QUERY_TILE // LANES), axis=1)
                    sims = jnp.where(kr < limit, sims, -1.0)
                    top = jnp.maximum(
                        top, jnp.max(sims.reshape(chunk // 8, 8, QUERY_TILE), axis=0)
                    )
            best[:, at] = top

    def emit(first, second):
        got = jnp.broadcast_to(jnp.max(best[...], axis=0, keepdims=True), (8, queries))
        shown = first.shape[1] - LANES
        for out, moved in ((first, got), (second, pltpu.roll(got, queries - span, 1))):
            out[:, :shown] = moved[:, :shown]
            out[:, shown:] = jnp.broadcast_to(flag, (8, LANES))

    sweep(
        home,
        home_rank,
        [(home, home_key, span), (away, away_key, span), (cross, cross_key, ncross * span)],
    )
    emit(out_own, out_twin)
    sweep(away, away_rank, [(cross, cross_key, ncross * span)])
    emit(out_near, out_far)


def similarity(pieces, cap, flagged, own, twin, near, far, cross):
    ncross = len(cross)
    width = own[0].shape[1]
    span = pieces * cap
    queries = ceil_to(2 * span, QUERY_TILE)
    shown = ceil_to(span, LANES) + LANES
    chunk = cap * max(j for j in range(1, pieces + 1) if pieces % j == 0 and j * cap <= 832)
    groups = [own, twin, near, far] + cross
    blocks = [block for group in groups for block in group]
    f32 = jnp.float32
    return pl.pallas_call(
        functools.partial(similarity_kernel, pieces, ncross, cap, flagged, chunk),
        out_shape=[jax.ShapeDtypeStruct((8, shown), f32)] * 4,
        in_specs=[pl.BlockSpec(memory_space=pl.ANY)] * len(blocks),
        scratch_shapes=[
            pltpu.VMEM((queries, width), jnp.bfloat16),
            pltpu.VMEM((queries, width), jnp.bfloat16),
            pltpu.VMEM((ncross * span, width), jnp.bfloat16),
            pltpu.VMEM((8, queries), f32),
            pltpu.VMEM((8, queries), f32),
            pltpu.VMEM((span, LANES), f32),
            pltpu.VMEM((span, LANES), f32),
            pltpu.VMEM((ncross * span, LANES), f32),
            pltpu.VMEM((8, queries), f32),
            pltpu.SemaphoreType.DMA((len(blocks),)),
        ],
        compiler_params=pltpu.CompilerParams(vmem_limit_bytes=VMEM),
        name="similarity",
    )(*blocks)


def collect_kernel(pieces, cap, place, *refs):
    rows, out = refs[:pieces], refs[pieces]
    where = place[...]
    lane = lax.broadcasted_iota(jnp.int32, (8, LANES), 1)
    result = jnp.zeros((8, LANES), jnp.float32)
    for first in range(0, pieces * cap, LANES):
        back = rows[min(first // cap, pieces - 1)][:, first : first + LANES]
        for s in range(first // cap + 1, pieces):
            if s * cap < first + LANES:
                back = jnp.where(lane + first >= s * cap, rows[s][:, first : first + LANES], back)
        inside = where - first
        hit = (inside >= 0) & (inside < LANES)
        taken = jnp.take_along_axis(back, jnp.where(hit, inside, 0), axis=1)
        result = jnp.where(hit, taken, result)
    out[...] = result


def collect(pieces, cap, place, rows):
    return pl.pallas_call(
        functools.partial(collect_kernel, pieces, cap),
        out_shape=jax.ShapeDtypeStruct((8, LANES), jnp.float32),
        name="collect",
    )(place, *rows)


def solution(mesh):
    ngrp, nsub = mesh.shape["grp"], mesh.shape["sub"]
    low = nsub // ngrp
    pieces = ngrp
    chips = ngrp // 2

    def send(block, target):
        route = []
        for g in range(ngrp):
            for s in range(nsub):
                chip, core, plane, small = target(g // 2, g % 2, s // low, s % low)
                route.append((g * nsub + s, (chip * 2 + core) * nsub + plane * low + small))
        return lax.ppermute(block, AXES, route)

    def to_plane(block, s):
        return send(block, lambda x, c, z, y: (x, c, z ^ s, y))

    def to_twin(block):
        return send(block, lambda x, c, z, y: (x, 1 - c, z, y))

    def to_near(block):
        return send(block, lambda x, c, z, y: (x, c, z, 1 - y))

    def to_far(block):
        return send(block, lambda x, c, z, y: (x, 1 - c, z, 1 - y))

    def to_cross(block, j):
        return send(block, lambda x, c, z, y: (x ^ j, c, z, y))

    def attempt(cap, flagged, embeddings, cluster_id, cluster_rank):
        rows = embeddings.shape[0]
        *own, place = dispatch(pieces, low, cap, flagged, embeddings, cluster_id, cluster_rank)
        own = [own[0]] + [to_plane(own[s], s) for s in range(1, pieces)]
        twin = [to_twin(block) for block in own]
        near = [to_near(block) for block in own]
        far = [to_twin(block) for block in near]
        cross = [[to_cross(block, j) for block in own] for j in range(1, chips)]
        a, b, c, d = similarity(pieces, cap, flagged, own, twin, near, far, cross)
        a = jnp.maximum(jnp.maximum(a, to_twin(b)), jnp.maximum(to_near(c), to_far(d)))
        back = [a] + [to_plane(a, s) for s in range(1, pieces)]
        where = jnp.pad(place.reshape(rows // LANES, LANES), ((0, 8 - rows // LANES), (0, 0)))
        result = collect(pieces, cap, where, back)
        return result[: rows // LANES].reshape(rows), a[0, -1]

    def body(embeddings, cluster_id, cluster_rank):
        share = embeddings.shape[0] // ngrp
        usual = ceil_to(share + 1, 16)
        most = ceil_to(2 * share + 1, 16)
        result, over = attempt(usual, True, embeddings, cluster_id, cluster_rank)

        def again():
            return attempt(most, False, embeddings, cluster_id, cluster_rank)[0]

        return lax.cond(over > 0.5, again, lambda: result)

    placed = (P(AXES, None), P(AXES), P(AXES))
    return jax.shard_map(body, mesh=mesh, in_specs=placed, out_specs=P(AXES), check_vma=False)
```

time: 322 us -> 136 us (0.42)
  waiting for transfers between devices: 220 us -> 72.3 us
  blocking collectives: 33 us -> 0 us
  Pallas kernels: 0 us -> 26.3 us
  local copies, waits for them, and re-layouts: 25.8 us -> 6.76 us
  matrix products: 14.3 us -> 0 us
  starting transfers between devices: 15.7 us -> 28.5 us
  other arithmetic: 12.6 us -> 0.78 us
    all_to_all x3 -> x0, waiting for transfers between devices: 80 us -> none  [the longest x1 72.9 us: body(): lax.all_to_all(send_rows.reshape(ndev, 2 * capacity, width), ('grp', 'sub...]
    ppermute x4 -> x25, waiting for transfers between devices: 140 us -> 72.3 us  [send(): return lax.ppermute(block, AXES, route)]
    pmax x1 -> x0, blocking collectives: 33 us -> none  [body(): merged = lax.pmax(column, 'sub')]
    ppermute x4 -> x25, starting transfers between devices: 0.01 us -> 28.5 us  [send(): return lax.ppermute(block, AXES, route)]
    pallas_call x0 -> x3, Pallas kernels: none -> 26.3 us  [the longest x1 19.6 us: similarity(): pl.pallas_call(functools.partial(similarity_kernel, pieces, ncross, cap,...]
    all_to_all x3 -> x0, starting transfers between devices: 15.7 us -> none  [the longest x1 7.3 us: body(): lax.all_to_all(send_rank.reshape(ndev, 2 * capacity), ('grp', 'sub'), spl...]
    dot_general x6 -> x0, matrix products: 14.3 us -> none  [the longest x5 14 us: product(): lax.dot_general(left, right, (((1,), (1,)), ((), ())), preferred_element_...]
    scatter x2 -> x0, local copies, waits for them, and re-layouts: 12.4 us -> none  [the longest x1 8.82 us: body(): jnp.zeros((rows, width), jnp.bfloat16).at[local_pos]]
  transfers between devices with their start and end apart: 7 -> 25, of which waited for: 6 -> 12; matrix products, arithmetic and copies ran while one was open for 7% -> 1% of each run, Pallas kernels for 0% -> 0%
where the time goes in v1:
time: 136 us
  waiting for transfers between devices  72.3 us (53%)
  starting transfers between devices  28.5 us (21%)
  Pallas kernels  26.3 us (19%)
  local copies, waits for them, and re-layouts  6.76 us (5%)
    ppermute x25, waiting for transfers between devices, send(): return lax.ppermute(block, AXES, route)  72.3 us
    ppermute x25, starting transfers between devices, send(): return lax.ppermute(block, AXES, route)  28.5 us
    pallas_call x1, Pallas kernels, similarity(): pl.pallas_call(functools.partial(similarity_kernel, pieces, ncross, cap,...  19.6 us
    pallas_call x1, Pallas kernels, dispatch(): pl.pallas_call(functools.partial(dispatch_kernel, pieces, low, cap, flagg...  5.7 us
    unnamed x54, local copies, waits for them, and re-layouts  2.97 us
  transfers between devices with their start and end apart: 25, of which 12 were waited for; matrix products, arithmetic and copies ran while one was open for 1% of the time, Pallas kernels for 0%

profile of v1, /device:TPU:0, one launch (start us, length us, event | category | flops | bytes accessed | tf_op | source)
XLA Modules:
  0.0 135.7 jit_solution(10647306451316064067)
XLA Ops:
  1.3 1.3 reshape.32.rank
  2.5 5.7 %dispatch.3 = (bf16[208,1024]{1,0:T(8,128)(2,1)}, bf16[208,1024]{1,0:T(8,128)(2,1)}, bf16[208,1024]{1,0:T(8,128)(2,1)}, bf16[208,1024]{1,0:T(8,128)(2,1)}, s32[1,768]{1,0:T(1,128)}) custom-call(bf16[768,1024]{1,0:T(8,128)(2,1)} %emb.1, s32[1,768]{1,0:T(1,128)} %reshape.31.cid, s32[1,768]{1,0:T(1,128)} %reshape.32.rank), custom_call_target="tpu_custom_call" | custom-call | tf_op jit(solution)/shard_map/dispatch/pallas_call | solution.py:93
  8.2 3.0 %collective-permute-start.25 = (bf16[208,1024]{1,0:T(8,128)(2,1)}, bf16[208,1024]{1,0:T(8,128)(2,1)S(1)}, u32[]{:S(2)}, u32[]{:S(2)}) collective-permute-start(bf16[208,1024]{1,0:T(8,128)(2,1)} %get-tuple-element.40), channel_id=1, source_target_pairs={{0,2},{1,3},{2,0},{3,1},{4,6},{5,7},{6,4},{7,5},{8,10},{9,11},{10,... | collective-permute-start | bytes 1277960 | tf_op jit(solution)/shard_map/ppermute | solution.py:264
  11.3 2.6 %collective-permute-start.26 = (bf16[208,1024]{1,0:T(8,128)(2,1)}, bf16[208,1024]{1,0:T(8,128)(2,1)S(1)}, u32[]{:S(2)}, u32[]{:S(2)}) collective-permute-start(bf16[208,1024]{1,0:T(8,128)(2,1)} %get-tuple-element.41), channel_id=1, source_target_pairs={{0,4},{1,5},{2,6},{3,7},{4,0},{5,1},{6,2},{7,3},{8,12},{9,13},{10,... | collective-permute-start | bytes 1277960 | tf_op jit(solution)/shard_map/ppermute | solution.py:264
  13.9 1.8 %collective-permute-start.32 = (bf16[208,1024]{1,0:T(8,128)(2,1)}, bf16[208,1024]{1,0:T(8,128)(2,1)S(1)}, u32[]{:S(2)}, u32[]{:S(2)}) collective-permute-start(bf16[208,1024]{1,0:T(8,128)(2,1)} %get-tuple-element.39.refs_0_), channel_id=1, source_target_pairs={{0,1},{1,0},{2,3},{3,2},{4,5},{5,4},{6,7},{7,6},{8,9},{9,8},{10,11... | collective-permute-start | bytes 1277960 | tf_op jit(solution)/shard_map/ppermute | solution.py:264
  15.7 14.0 %collective-permute-done.25.refs_1_ = bf16[208,1024]{1,0:T(8,128)(2,1)S(1)} collective-permute-done((bf16[208,1024]{1,0:T(8,128)(2,1)}, bf16[208,1024]{1,0:T(8,128)(2,1)S(1)}, u32[]{:S(2)}, u32[]{:S(2)}) %collective-permute-start.25) | collective-permute-done | bytes 426016 | tf_op jit(solution)/shard_map/ppermute | solution.py:264
  29.7 1.7 %collective-permute-start.40 = (bf16[208,1024]{1,0:T(8,128)(2,1)}, bf16[208,1024]{1,0:T(8,128)(2,1)S(1)}, u32[]{:S(2)}, u32[]{:S(2)}) collective-permute-start(bf16[208,1024]{1,0:T(8,128)(2,1)} %get-tuple-element.39.refs_0_), channel_id=1, source_target_pairs={{0,16},{1,17},{2,18},{3,19},{4,20},{5,21},{6,22},{7,23},{8,24},{9,... | collective-permute-start | bytes 1277960 | tf_op jit(solution)/shard_map/ppermute | solution.py:264
  31.3 12.1 %collective-permute-done.26.refs_2_ = bf16[208,1024]{1,0:T(8,128)(2,1)S(1)} collective-permute-done((bf16[208,1024]{1,0:T(8,128)(2,1)}, bf16[208,1024]{1,0:T(8,128)(2,1)S(1)}, u32[]{:S(2)}, u32[]{:S(2)}) %collective-permute-start.26) | collective-permute-done | bytes 426016 | tf_op jit(solution)/shard_map/ppermute | solution.py:264
  43.4 1.5 %collective-permute-start.33 = (bf16[208,1024]{1,0:T(8,128)(2,1)S(1)}, bf16[208,1024]{1,0:T(8,128)(2,1)S(1)}, u32[]{:S(2)}, u32[]{:S(2)}) collective-permute-start(bf16[208,1024]{1,0:T(8,128)(2,1)S(1)} %collective-permute-done.25.refs_1_), channel_id=1, source_target_pairs={{0,1},{1,0},{2,3},{3,2},{4,5},{5,4},{6,7},{7,6},{8,9},{9,8},{10,11... | collective-permute-start | bytes 1277960 | tf_op jit(solution)/shard_map/ppermute | solution.py:264
  45.4 1.5 %collective-permute-start.35 = (bf16[208,1024]{1,0:T(8,128)(2,1)S(1)}, bf16[208,1024]{1,0:T(8,128)(2,1)S(1)}, u32[]{:S(2)}, u32[]{:S(2)}) collective-permute-start(bf16[208,1024]{1,0:T(8,128)(2,1)S(1)} %collective-permute-done.27.refs_3_), channel_id=1, source_target_pairs={{0,1},{1,0},{2,3},{3,2},{4,5},{5,4},{6,7},{7,6},{8,9},{9,8},{10,11... | collective-permute-start | bytes 1277960 | tf_op jit(solution)/shard_map/ppermute | solution.py:264
  47.5 8.7 %collective-permute-done.33.refs_9_ = bf16[208,1024]{1,0:T(8,128)(2,1)S(1)} collective-permute-done((bf16[208,1024]{1,0:T(8,128)(2,1)S(1)}, bf16[208,1024]{1,0:T(8,128)(2,1)S(1)}, u32[]{:S(2)}, u32[]{:S(2)}) %collective-permute-start.33) | collective-permute-done | bytes 426016 | tf_op jit(solution)/shard_map/ppermute | solution.py:264
  56.1 5.5 %collective-permute-done.34.refs_10_ = bf16[208,1024]{1,0:T(8,128)(2,1)S(1)} collective-permute-done((bf16[208,1024]{1,0:T(8,128)(2,1)S(1)}, bf16[208,1024]{1,0:T(8,128)(2,1)S(1)}, u32[]{:S(2)}, u32[]{:S(2)}) %collective-permute-start.34) | collective-permute-done | bytes 426016 | tf_op jit(solution)/shard_map/ppermute | solution.py:264
  61.6 4.6 %collective-permute-done.35.refs_11_ = bf16[208,1024]{1,0:T(8,128)(2,1)S(1)} collective-permute-done((bf16[208,1024]{1,0:T(8,128)(2,1)S(1)}, bf16[208,1024]{1,0:T(8,128)(2,1)S(1)}, u32[]{:S(2)}, u32[]{:S(2)}) %collective-permute-start.35) | collective-permute-done | bytes 426016 | tf_op jit(solution)/shard_map/ppermute | solution.py:264
  66.2 1.5 %collective-permute-start.41 = (bf16[208,1024]{1,0:T(8,128)(2,1)S(1)}, bf16[208,1024]{1,0:T(8,128)(2,1)S(1)}, u32[]{:S(2)}, u32[]{:S(2)}) collective-permute-start(bf16[208,1024]{1,0:T(8,128)(2,1)S(1)} %collective-permute-done.25.refs_1_), channel_id=1, source_target_pairs={{0,16},{1,17},{2,18},{3,19},{4,20},{5,21},{6,22},{7,23},{8,24},{9,... | collective-permute-start | bytes 1277960 | tf_op jit(solution)/shard_map/ppermute | solution.py:264
  68.2 1.5 %collective-permute-start.43 = (bf16[208,1024]{1,0:T(8,128)(2,1)S(1)}, bf16[208,1024]{1,0:T(8,128)(2,1)S(1)}, u32[]{:S(2)}, u32[]{:S(2)}) collective-permute-start(bf16[208,1024]{1,0:T(8,128)(2,1)S(1)} %collective-permute-done.27.refs_3_), channel_id=1, source_target_pairs={{0,16},{1,17},{2,18},{3,19},{4,20},{5,21},{6,22},{7,23},{8,24},{9,... | collective-permute-start | bytes 1277960 | tf_op jit(solution)/shard_map/ppermute | solution.py:264
  70.2 8.7 %collective-permute-done.41.refs_17_ = bf16[208,1024]{1,0:T(8,128)(2,1)S(1)} collective-permute-done((bf16[208,1024]{1,0:T(8,128)(2,1)S(1)}, bf16[208,1024]{1,0:T(8,128)(2,1)S(1)}, u32[]{:S(2)}, u32[]{:S(2)}) %collective-permute-start.41) | collective-permute-done | bytes 426016 | tf_op jit(solution)/shard_map/ppermute | solution.py:264
  78.9 8.6 %collective-permute-done.42.refs_18_ = bf16[208,1024]{1,0:T(8,128)(2,1)S(1)} collective-permute-done((bf16[208,1024]{1,0:T(8,128)(2,1)S(1)}, bf16[208,1024]{1,0:T(8,128)(2,1)S(1)}, u32[]{:S(2)}, u32[]{:S(2)}) %collective-permute-start.42) | collective-permute-done | bytes 426016 | tf_op jit(solution)/shard_map/ppermute | solution.py:264
  87.5 4.6 %collective-permute-done.43.refs_19_ = bf16[208,1024]{1,0:T(8,128)(2,1)S(1)} collective-permute-done((bf16[208,1024]{1,0:T(8,128)(2,1)S(1)}, bf16[208,1024]{1,0:T(8,128)(2,1)S(1)}, u32[]{:S(2)}, u32[]{:S(2)}) %collective-permute-start.43) | collective-permute-done | bytes 426016 | tf_op jit(solution)/shard_map/ppermute | solution.py:264
  93.9 19.6 %similarity.3 = (f32[8,1024]{1,0:T(8,128)}, f32[8,1024]{1,0:T(8,128)}, f32[8,1024]{1,0:T(8,128)}, f32[8,1024]{1,0:T(8,128)}) custom-call(bf16[208,1024]{1,0:T(8,128)(2,1)} %get-tuple-element.39.refs_0_, bf16[208,1024]{1,0:T(8,128)(2,1)} %copy-done.19, bf16[208,1024]{1,0:T(8,128)(2,1)} %copy-done.20, bf16[208,1024]{1,0:T(8,128)(2,1)} %copy-done.21, ...), custom_call_target="tpu_custom_call" | custom-call | tf_op jit(solution)/shard_map/similarity/pallas_call | solution.py:206
  113.7 1.6 %collective-permute-start.45 = (f32[8,1024]{1,0:T(8,128)}, f32[8,1024]{1,0:T(8,128)S(1)}, u32[]{:S(2)}, u32[]{:S(2)}) collective-permute-start(f32[8,1024]{1,0:T(8,128)} %get-tuple-element.45), channel_id=1, source_target_pairs={{0,1},{1,0},{2,3},{3,2},{4,5},{5,4},{6,7},{7,6},{8,9},{9,8},{10,11... | collective-permute-start | bytes 98312 | tf_op jit(solution)/shard_map/ppermute | solution.py:264
  115.5 2.3 %collective-permute-done.45 = f32[8,1024]{1,0:T(8,128)S(1)} collective-permute-done((f32[8,1024]{1,0:T(8,128)}, f32[8,1024]{1,0:T(8,128)S(1)}, u32[]{:S(2)}, u32[]{:S(2)}) %collective-permute-start.45) | collective-permute-done | bytes 32800 | tf_op jit(solution)/shard_map/ppermute | solution.py:264
  119.6 6.9 %collective-permute-start.47 = (f32[8,1024]{1,0:T(8,128)S(1)}, f32[8,1024]{1,0:T(8,128)S(1)}, u32[]{:S(2)}, u32[]{:S(2)}) collective-permute-start(f32[8,1024]{1,0:T(8,128)S(1)} %maximum_maximum_fusion.1.refs_0_), channel_id=1, source_target_pairs={{0,2},{1,3},{2,0},{3,1},{4,6},{5,7},{6,4},{7,5},{8,10},{9,11},{10,... | collective-permute-start | bytes 98312 | tf_op jit(solution)/shard_map/ppermute | solution.py:264
  127.6 1.4 %collective-permute-start.49 = (f32[8,1024]{1,0:T(8,128)S(1)}, f32[8,1024]{1,0:T(8,128)S(1)}, u32[]{:S(2)}, u32[]{:S(2)}) collective-permute-start(f32[8,1024]{1,0:T(8,128)S(1)} %maximum_maximum_fusion.1.refs_0_), channel_id=1, source_target_pairs={{0,6},{1,7},{2,4},{3,5},{4,2},{5,3},{6,0},{7,1},{8,14},{9,15},{10,... | collective-permute-start | bytes 98312 | tf_op jit(solution)/shard_map/ppermute | solution.py:264
  131.9 1.4 %collective-permute-done.49.refs_3_ = f32[8,1024]{1,0:T(8,128)S(1)} collective-permute-done((f32[8,1024]{1,0:T(8,128)S(1)}, f32[8,1024]{1,0:T(8,128)S(1)}, u32[]{:S(2)}, u32[]{:S(2)}) %collective-permute-start.49) | collective-permute-done | bytes 32800 | tf_op jit(solution)/shard_map/ppermute | solution.py:264
  (91 shorter events, 12.9 us)
Async XLA Ops:
  8.2 21.4 %collective-permute-start.25 = (bf16[208,1024]{1,0:T(8,128)(2,1)}, bf16[208,1024]{1,0:T(8,128)(2,1)S(1)}, u32[]{:S(2)}, u32[]{:S(2)}) collective-permute-start(bf16[208,1024]{1,0:T(8,128)(2,1)} %get-tuple-element.40), channel_id=1, source_target_pairs={{0,2},{1,3},{2,0},{3,1},{4,6},{5,7},{6,4},{7,5},{8,10},{9,11},{10,... | collective-permute-start | bytes 1277960 | tf_op jit(solution)/shard_map/ppermute | solution.py:264
  11.3 32.1 %collective-permute-start.26 = (bf16[208,1024]{1,0:T(8,128)(2,1)}, bf16[208,1024]{1,0:T(8,128)(2,1)S(1)}, u32[]{:S(2)}, u32[]{:S(2)}) collective-permute-start(bf16[208,1024]{1,0:T(8,128)(2,1)} %get-tuple-element.41), channel_id=1, source_target_pairs={{0,4},{1,5},{2,6},{3,7},{4,0},{5,1},{6,2},{7,3},{8,12},{9,13},{10,... | collective-permute-start | bytes 1277960 | tf_op jit(solution)/shard_map/ppermute | solution.py:264
  13.9 31.0 %collective-permute-start.27 = (bf16[208,1024]{1,0:T(8,128)(2,1)}, bf16[208,1024]{1,0:T(8,128)(2,1)S(1)}, u32[]{:S(2)}, u32[]{:S(2)}) collective-permute-start(bf16[208,1024]{1,0:T(8,128)(2,1)} %get-tuple-element.42), channel_id=1, source_target_pairs={{0,6},{1,7},{2,4},{3,5},{4,2},{5,3},{6,0},{7,1},{8,14},{9,15},{10,... | collective-permute-start | bytes 1277960 | tf_op jit(solution)/shard_map/ppermute | solution.py:264
  13.9 31.5 %collective-permute-start.32 = (bf16[208,1024]{1,0:T(8,128)(2,1)}, bf16[208,1024]{1,0:T(8,128)(2,1)S(1)}, u32[]{:S(2)}, u32[]{:S(2)}) collective-permute-start(bf16[208,1024]{1,0:T(8,128)(2,1)} %get-tuple-element.39.refs_0_), channel_id=1, source_target_pairs={{0,1},{1,0},{2,3},{3,2},{4,5},{5,4},{6,7},{7,6},{8,9},{9,8},{10,11... | collective-permute-start | bytes 1277960 | tf_op jit(solution)/shard_map/ppermute | solution.py:264
  15.7 31.3 %collective-permute-start.28 = (bf16[208,1024]{1,0:T(8,128)(2,1)}, bf16[208,1024]{1,0:T(8,128)(2,1)S(1)}, u32[]{:S(2)}, u32[]{:S(2)}) collective-permute-start(bf16[208,1024]{1,0:T(8,128)(2,1)} %get-tuple-element.39.refs_0_), channel_id=1, source_target_pairs={{0,8},{1,9},{2,10},{3,11},{4,12},{5,13},{6,14},{7,15},{8,0},{9,1},... | collective-permute-start | bytes 1277960 | tf_op jit(solution)/shard_map/ppermute | solution.py:264
  29.7 17.3 %collective-permute-start.40 = (bf16[208,1024]{1,0:T(8,128)(2,1)}, bf16[208,1024]{1,0:T(8,128)(2,1)S(1)}, u32[]{:S(2)}, u32[]{:S(2)}) collective-permute-start(bf16[208,1024]{1,0:T(8,128)(2,1)} %get-tuple-element.39.refs_0_), channel_id=1, source_target_pairs={{0,16},{1,17},{2,18},{3,19},{4,20},{5,21},{6,22},{7,23},{8,24},{9,... | collective-permute-start | bytes 1277960 | tf_op jit(solution)/shard_map/ppermute | solution.py:264
  43.4 12.8 %collective-permute-start.33 = (bf16[208,1024]{1,0:T(8,128)(2,1)S(1)}, bf16[208,1024]{1,0:T(8,128)(2,1)S(1)}, u32[]{:S(2)}, u32[]{:S(2)}) collective-permute-start(bf16[208,1024]{1,0:T(8,128)(2,1)S(1)} %collective-permute-done.25.refs_1_), channel_id=1, source_target_pairs={{0,1},{1,0},{2,3},{3,2},{4,5},{5,4},{6,7},{7,6},{8,9},{9,8},{10,11... | collective-permute-start | bytes 1277960 | tf_op jit(solution)/shard_map/ppermute | solution.py:264
  44.9 16.7 %collective-permute-start.34 = (bf16[208,1024]{1,0:T(8,128)(2,1)S(1)}, bf16[208,1024]{1,0:T(8,128)(2,1)S(1)}, u32[]{:S(2)}, u32[]{:S(2)}) collective-permute-start(bf16[208,1024]{1,0:T(8,128)(2,1)S(1)} %collective-permute-done.26.refs_2_), channel_id=1, source_target_pairs={{0,1},{1,0},{2,3},{3,2},{4,5},{5,4},{6,7},{7,6},{8,9},{9,8},{10,11... | collective-permute-start | bytes 1277960 | tf_op jit(solution)/shard_map/ppermute | solution.py:264
  45.4 20.7 %collective-permute-start.35 = (bf16[208,1024]{1,0:T(8,128)(2,1)S(1)}, bf16[208,1024]{1,0:T(8,128)(2,1)S(1)}, u32[]{:S(2)}, u32[]{:S(2)}) collective-permute-start(bf16[208,1024]{1,0:T(8,128)(2,1)S(1)} %collective-permute-done.27.refs_3_), channel_id=1, source_target_pairs={{0,1},{1,0},{2,3},{3,2},{4,5},{5,4},{6,7},{7,6},{8,9},{9,8},{10,11... | collective-permute-start | bytes 1277960 | tf_op jit(solution)/shard_map/ppermute | solution.py:264
  47.0 20.7 %collective-permute-start.36 = (bf16[208,1024]{1,0:T(8,128)(2,1)S(1)}, bf16[208,1024]{1,0:T(8,128)(2,1)S(1)}, u32[]{:S(2)}, u32[]{:S(2)}) collective-permute-start(bf16[208,1024]{1,0:T(8,128)(2,1)S(1)} %collective-permute-done.32.refs_8_), channel_id=1, source_target_pairs={{0,8},{1,9},{2,10},{3,11},{4,12},{5,13},{6,14},{7,15},{8,0},{9,1},... | collective-permute-start | bytes 1277960 | tf_op jit(solution)/shard_map/ppermute | solution.py:264
  47.0 21.2 %collective-permute-start.29 = (bf16[208,1024]{1,0:T(8,128)(2,1)S(1)}, bf16[208,1024]{1,0:T(8,128)(2,1)S(1)}, u32[]{:S(2)}, u32[]{:S(2)}) collective-permute-start(bf16[208,1024]{1,0:T(8,128)(2,1)S(1)} %collective-permute-done.25.refs_1_), channel_id=1, source_target_pairs={{0,8},{1,9},{2,10},{3,11},{4,12},{5,13},{6,14},{7,15},{8,0},{9,1},... | collective-permute-start | bytes 1277960 | tf_op jit(solution)/shard_map/ppermute | solution.py:264
  56.1 13.6 %collective-permute-start.30 = (bf16[208,1024]{1,0:T(8,128)(2,1)S(1)}, bf16[208,1024]{1,0:T(8,128)(2,1)S(1)}, u32[]{:S(2)}, u32[]{:S(2)}) collective-permute-start(bf16[208,1024]{1,0:T(8,128)(2,1)S(1)} %collective-permute-done.26.refs_2_), channel_id=1, source_target_pairs={{0,8},{1,9},{2,10},{3,11},{4,12},{5,13},{6,14},{7,15},{8,0},{9,1},... | collective-permute-start | bytes 1277960 | tf_op jit(solution)/shard_map/ppermute | solution.py:264
  61.6 8.1 %collective-permute-start.31 = (bf16[208,1024]{1,0:T(8,128)(2,1)S(1)}, bf16[208,1024]{1,0:T(8,128)(2,1)S(1)}, u32[]{:S(2)}, u32[]{:S(2)}) collective-permute-start(bf16[208,1024]{1,0:T(8,128)(2,1)S(1)} %collective-permute-done.27.refs_3_), channel_id=1, source_target_pairs={{0,8},{1,9},{2,10},{3,11},{4,12},{5,13},{6,14},{7,15},{8,0},{9,1},... | collective-permute-start | bytes 1277960 | tf_op jit(solution)/shard_map/ppermute | solution.py:264
  66.2 12.8 %collective-permute-start.41 = (bf16[208,1024]{1,0:T(8,128)(2,1)S(1)}, bf16[208,1024]{1,0:T(8,128)(2,1)S(1)}, u32[]{:S(2)}, u32[]{:S(2)}) collective-permute-start(bf16[208,1024]{1,0:T(8,128)(2,1)S(1)} %collective-permute-done.25.refs_1_), channel_id=1, source_target_pairs={{0,16},{1,17},{2,18},{3,19},{4,20},{5,21},{6,22},{7,23},{8,24},{9,... | collective-permute-start | bytes 1277960 | tf_op jit(solution)/shard_map/ppermute | solution.py:264
  67.7 19.9 %collective-permute-start.42 = (bf16[208,1024]{1,0:T(8,128)(2,1)S(1)}, bf16[208,1024]{1,0:T(8,128)(2,1)S(1)}, u32[]{:S(2)}, u32[]{:S(2)}) collective-permute-start(bf16[208,1024]{1,0:T(8,128)(2,1)S(1)} %collective-permute-done.26.refs_2_), channel_id=1, source_target_pairs={{0,16},{1,17},{2,18},{3,19},{4,20},{5,21},{6,22},{7,23},{8,24},{9,... | collective-permute-start | bytes 1277960 | tf_op jit(solution)/shard_map/ppermute | solution.py:264
  68.2 23.9 %collective-permute-start.43 = (bf16[208,1024]{1,0:T(8,128)(2,1)S(1)}, bf16[208,1024]{1,0:T(8,128)(2,1)S(1)}, u32[]{:S(2)}, u32[]{:S(2)}) collective-permute-start(bf16[208,1024]{1,0:T(8,128)(2,1)S(1)} %collective-permute-done.27.refs_3_), channel_id=1, source_target_pairs={{0,16},{1,17},{2,18},{3,19},{4,20},{5,21},{6,22},{7,23},{8,24},{9,... | collective-permute-start | bytes 1277960 | tf_op jit(solution)/shard_map/ppermute | solution.py:264
  69.7 22.4 %collective-permute-start.37 = (bf16[208,1024]{1,0:T(8,128)(2,1)S(1)}, bf16[208,1024]{1,0:T(8,128)(2,1)S(1)}, u32[]{:S(2)}, u32[]{:S(2)}) collective-permute-start(bf16[208,1024]{1,0:T(8,128)(2,1)S(1)} %collective-permute-done.33.refs_9_), channel_id=1, source_target_pairs={{0,8},{1,9},{2,10},{3,11},{4,12},{5,13},{6,14},{7,15},{8,0},{9,1},... | collective-permute-start | bytes 1277960 | tf_op jit(solution)/shard_map/ppermute | solution.py:264
  69.7 22.4 %collective-permute-start.38 = (bf16[208,1024]{1,0:T(8,128)(2,1)S(1)}, bf16[208,1024]{1,0:T(8,128)(2,1)S(1)}, u32[]{:S(2)}, u32[]{:S(2)}) collective-permute-start(bf16[208,1024]{1,0:T(8,128)(2,1)S(1)} %collective-permute-done.34.refs_10_), channel_id=1, source_target_pairs={{0,8},{1,9},{2,10},{3,11},{4,12},{5,13},{6,14},{7,15},{8,0},{9,1},... | collective-permute-start | bytes 1277960 | tf_op jit(solution)/shard_map/ppermute | solution.py:264
  78.9 14.9 %collective-permute-start.39 = (bf16[208,1024]{1,0:T(8,128)(2,1)S(1)}, bf16[208,1024]{1,0:T(8,128)(2,1)}, u32[]{:S(2)}, u32[]{:S(2)}) collective-permute-start(bf16[208,1024]{1,0:T(8,128)(2,1)S(1)} %collective-permute-done.35.refs_11_), channel_id=1, source_target_pairs={{0,8},{1,9},{2,10},{3,11},{4,12},{5,13},{6,14},{7,15},{8,0},{9,1},... | collective-permute-start | bytes 1277960 | tf_op jit(solution)/shard_map/ppermute | solution.py:264
  113.7 4.2 %collective-permute-start.45 = (f32[8,1024]{1,0:T(8,128)}, f32[8,1024]{1,0:T(8,128)S(1)}, u32[]{:S(2)}, u32[]{:S(2)}) collective-permute-start(f32[8,1024]{1,0:T(8,128)} %get-tuple-element.45), channel_id=1, source_target_pairs={{0,1},{1,0},{2,3},{3,2},{4,5},{5,4},{6,7},{7,6},{8,9},{9,8},{10,11... | collective-permute-start | bytes 98312 | tf_op jit(solution)/shard_map/ppermute | solution.py:264
  115.3 3.6 %collective-permute-start.46 = (f32[8,1024]{1,0:T(8,128)}, f32[8,1024]{1,0:T(8,128)S(1)}, u32[]{:S(2)}, u32[]{:S(2)}) collective-permute-start(f32[8,1024]{1,0:T(8,128)} %get-tuple-element.46), channel_id=1, source_target_pairs={{0,9},{1,8},{2,11},{3,10},{4,13},{5,12},{6,15},{7,14},{8,1},{9,0},... | collective-permute-start | bytes 98312 | tf_op jit(solution)/shard_map/ppermute | solution.py:264
  119.6 11.3 %collective-permute-start.47 = (f32[8,1024]{1,0:T(8,128)S(1)}, f32[8,1024]{1,0:T(8,128)S(1)}, u32[]{:S(2)}, u32[]{:S(2)}) collective-permute-start(f32[8,1024]{1,0:T(8,128)S(1)} %maximum_maximum_fusion.1.refs_0_), channel_id=1, source_target_pairs={{0,2},{1,3},{2,0},{3,1},{4,6},{5,7},{6,4},{7,5},{8,10},{9,11},{10,... | collective-permute-start | bytes 98312 | tf_op jit(solution)/shard_map/ppermute | solution.py:264
  126.5 5.4 %collective-permute-start.48 = (f32[8,1024]{1,0:T(8,128)S(1)}, f32[8,1024]{1,0:T(8,128)S(1)}, u32[]{:S(2)}, u32[]{:S(2)}) collective-permute-start(f32[8,1024]{1,0:T(8,128)S(1)} %maximum_maximum_fusion.1.refs_0_), channel_id=1, source_target_pairs={{0,4},{1,5},{2,6},{3,7},{4,0},{5,1},{6,2},{7,3},{8,12},{9,13},{10,... | collective-permute-start | bytes 98312 | tf_op jit(solution)/shard_map/ppermute | solution.py:264
  127.6 5.7 %collective-permute-start.49 = (f32[8,1024]{1,0:T(8,128)S(1)}, f32[8,1024]{1,0:T(8,128)S(1)}, u32[]{:S(2)}, u32[]{:S(2)}) collective-permute-start(f32[8,1024]{1,0:T(8,128)S(1)} %maximum_maximum_fusion.1.refs_0_), channel_id=1, source_target_pairs={{0,6},{1,7},{2,4},{3,5},{4,2},{5,3},{6,0},{7,1},{8,14},{9,15},{10,... | collective-permute-start | bytes 98312 | tf_op jit(solution)/shard_map/ppermute | solution.py:264
  (28 other events, 1026.3 us)

commit v2 on v1

v2 whole, which is shorter than its diff:
```python
import functools

import jax
import jax.numpy as jnp
from jax import lax
from jax.experimental import pallas as pl
from jax.experimental.pallas import tpu as pltpu
from jax.sharding import PartitionSpec as P

AXES = ("grp", "sub")
LANES = 128
RADIX = 128
EMPTY = 255.0
VMEM = 16 * 1024 * 1024


def ceil_to(value, unit):
    return -(-value // unit) * unit


def nt_dot(left, right):
    return lax.dot_general(
        left, right, (((1,), (1,)), ((), ())), preferred_element_type=jnp.float32
    )


def flat(ref):
    return jnp.concatenate([ref[b : b + 1, :] for b in range(ref.shape[0])], axis=1)


def dispatch_kernel(pieces, low, cap, flagged, emb, cid, rank, *refs):
    outs, place_ref, unit, slot_ref = refs[:pieces], refs[pieces], refs[pieces + 1], refs[pieces + 2]
    rows, width = emb.shape
    wide_lanes = ceil_to(cap, LANES)
    plane = lax.axis_index("sub") // low

    @pl.loop(0, rows // 64)
    def _(i):
        at = pl.ds(pl.multiple_of(i * 64, 64), 64)
        wide = emb[at, :].astype(jnp.float32)
        scale = lax.rsqrt(jnp.sum(wide * wide, axis=1, keepdims=True) + 1e-06)
        unit[at, :] = (wide * scale).astype(jnp.bfloat16)

    piece = flat(cid) ^ plane
    which = lax.broadcasted_iota(jnp.int32, (16, LANES), 0)
    upper = (
        lax.broadcasted_iota(jnp.int32, (LANES, LANES), 0)
        < lax.broadcasted_iota(jnp.int32, (LANES, LANES), 1)
    ).astype(jnp.bfloat16)
    before = jnp.zeros((16, 1), jnp.float32)
    for b in range(rows // LANES):
        lanes = slice(b * LANES, (b + 1) * LANES)
        member = piece[:, lanes] == which
        ones = member.astype(jnp.float32)
        prefix = jnp.dot(ones.astype(jnp.bfloat16), upper, preferred_element_type=jnp.float32)
        slot = jnp.sum(jnp.where(member, prefix + before, 0.0), axis=0, keepdims=True)
        slot_ref[:, lanes] = slot.astype(jnp.int32)
        before = before + jnp.sum(ones, axis=1, keepdims=True)
    slot = slot_ref[...]
    place_ref[...] = piece * wide_lanes + slot
    full = jnp.max(before, axis=0, keepdims=True) > cap - 1
    full = full.astype(jnp.float32)

    target = piece * 1024 + slot
    r = flat(rank)
    digits = jnp.concatenate(
        [
            (r // RADIX).astype(jnp.float32),
            (r % RADIX).astype(jnp.float32),
            jnp.ones((1, rows), jnp.float32),
            jnp.zeros((13, rows), jnp.float32),
        ],
        axis=0,
    ).astype(jnp.bfloat16)
    for s in range(pieces):
        slots = lax.broadcasted_iota(jnp.int32, (wide_lanes, rows), 0) + s * 1024
        pick = jnp.where(slots == target, 1.0, 0.0).astype(jnp.bfloat16)
        ranks = nt_dot(digits, pick)
        filled = ranks[2:3, :] > 0.5
        high = jnp.where(filled, ranks[0:1, :], EMPTY)
        parts = [high, ranks[1:2, :]]
        if flagged:
            parts.append(jnp.broadcast_to(full, (1, LANES)))
        used = 2 * wide_lanes + (LANES if flagged else 0)
        if used < width:
            parts.append(jnp.zeros((1, width - used), jnp.float32))
        note = jnp.concatenate(parts, axis=1)
        moved = jnp.dot(pick[:cap], unit[...], preferred_element_type=jnp.float32)
        outs[s][: cap - 16, :] = moved[: cap - 16].astype(jnp.bfloat16)
        last = lax.broadcasted_iota(jnp.int32, (16, 1), 0) == 15
        outs[s][cap - 16 :, :] = jnp.where(last, note, moved[cap - 16 :]).astype(jnp.bfloat16)


def dispatch(pieces, low, cap, flagged, emb, cid, rank):
    rows, width = emb.shape
    return pl.pallas_call(
        functools.partial(dispatch_kernel, pieces, low, cap, flagged),
        out_shape=[jax.ShapeDtypeStruct((cap, width), jnp.bfloat16)] * pieces
        + [jax.ShapeDtypeStruct((1, rows), jnp.int32)],
        scratch_shapes=[
            pltpu.VMEM((rows, width), jnp.bfloat16),
            pltpu.VMEM((1, rows), jnp.int32),
        ],
        compiler_params=pltpu.CompilerParams(vmem_limit_bytes=VMEM),
        name="dispatch",
    )(emb, cid.reshape(rows // LANES, LANES), rank.reshape(rows // LANES, LANES))


def stage_kernel(p, pieces, groups, cap, flagged, chunk, *refs):
    blocks, refs = refs[:groups], refs[groups:]
    if p:
        refs = refs[4:]
    store, keys, limits, best, refs = *refs[:4], refs[4:]
    sem = refs[-1]
    lanes_per = ceil_to(cap, LANES)
    per = groups * cap
    base = p * per

    copies = []
    for g in range(groups):
        copy = pltpu.make_async_copy(blocks[g], store.at[pl.ds(base + g * cap, cap), :], sem.at[g])
        copy.start()
        copies.append(copy)

    lane = lax.broadcasted_iota(jnp.int32, (1, lanes_per), 1)
    square = lax.broadcasted_iota(jnp.int32, (cap, lanes_per), 0) == lax.broadcasted_iota(
        jnp.int32, (cap, lanes_per), 1
    )
    flag = jnp.zeros((1, LANES), jnp.float32)
    if p == 0:
        limits[...] = jnp.zeros(limits.shape, jnp.float32)
        best[...] = jnp.full(best.shape, -1.0, jnp.float32)
    for g in range(groups):
        copies[g].wait()
        end = base + (g + 1) * cap
        note = store[end - 16 : end, :].astype(jnp.float32)[15:16, :]
        ranks = note[:, :lanes_per] * RADIX + note[:, lanes_per : 2 * lanes_per]
        ranks = jnp.where(lane < cap - 1, ranks, EMPTY * RADIX)
        if flagged:
            flag = jnp.maximum(flag, note[:, 2 * lanes_per : 2 * lanes_per + LANES])
        if g in (0, 2):
            at = (2 * p + g // 2) * lanes_per
            limits[:, at : at + lanes_per] = jnp.broadcast_to(ranks, (8, lanes_per))
        column = jnp.sum(jnp.where(square, ranks, 0.0), axis=1, keepdims=True)
        keys[end - cap : end, :] = jnp.broadcast_to(column, (cap, LANES))
    if flagged:
        at = 2 * pieces * lanes_per
        best[:, at:] = jnp.maximum(best[:, at:], jnp.broadcast_to(flag, (8, LANES)))

    @pl.loop(0, 2 * p + 1)
    def _(t):
        old = t > p
        first = jnp.where(old, t - p - 1, p)
        second = jnp.where(old, p, t)
        for group, start, total in ((0, 0, per), (2, 4 * cap, per - 4 * cap)):
            query = store[pl.ds(pl.multiple_of(first * per + group * cap, 16), lanes_per), :]
            at = pl.ds(pl.multiple_of((first * 2 + group // 2) * lanes_per, LANES), lanes_per)
            limit = limits[0:1, at]
            top = best[:, at]
            for offset in range(start, start + total, chunk):
                rows = pl.ds(pl.multiple_of(second * per + offset, 16), chunk)
                sims = nt_dot(store[rows, :], query)
                kr = jnp.concatenate([keys[rows, :]] * (lanes_per // LANES), axis=1)
                sims = jnp.where(kr < limit, sims, -1.0)
                top = jnp.maximum(top, jnp.max(sims.reshape(chunk // 8, 8, lanes_per), axis=0))
            best[:, at] = top

    if p == pieces - 1:
        for group, out in enumerate(refs[:2]):
            for s in range(pieces):
                at = (2 * s + group) * lanes_per
                row = jnp.max(best[:, at : at + lanes_per], axis=0, keepdims=True)
                out[:, s * lanes_per : (s + 1) * lanes_per] = jnp.broadcast_to(row, (8, lanes_per))
            out[:, pieces * lanes_per :] = best[:, 2 * pieces * lanes_per :]


def stage(p, pieces, cap, flagged, blocks, carried):
    groups = len(blocks)
    width = blocks[0].shape[1]
    lanes_per = ceil_to(cap, LANES)
    per = groups * cap
    f32 = jnp.float32
    chunk = 2 * cap
    kept = [
        pltpu.VMEM((pieces * per, width), jnp.bfloat16),
        pltpu.VMEM((pieces * per, LANES), f32),
        pltpu.VMEM((8, 2 * pieces * lanes_per), f32),
        pltpu.VMEM((8, 2 * pieces * lanes_per + LANES), f32),
    ]
    ends = [jax.ShapeDtypeStruct((8, pieces * lanes_per + LANES), f32)] * 2
    last = p == pieces - 1
    pairs = (2 * p + 1) * (2 * per - 4 * cap) * cap
    got = pl.pallas_call(
        functools.partial(stage_kernel, p, pieces, groups, cap, flagged, chunk),
        out_shape=kept + (ends if last else []),
        in_specs=[pl.BlockSpec(memory_space=pl.ANY)] * groups
        + [pl.BlockSpec(memory_space=pltpu.VMEM)] * len(carried),
        out_specs=[pl.BlockSpec(memory_space=pltpu.VMEM)] * (4 + 2 * last),
        scratch_shapes=[pltpu.SemaphoreType.DMA((groups,))],
        input_output_aliases={groups + i: i for i in range(len(carried))},
        cost_estimate=pl.CostEstimate(
            flops=2 * pairs * width, bytes_accessed=2 * per * width, transcendentals=0
        ),
        compiler_params=pltpu.CompilerParams(vmem_limit_bytes=VMEM),
        name="stage" + str(p),
    )(*blocks, *[pltpu.with_memory_space_constraint(x, pltpu.VMEM) for x in carried])
    return got[:4], got[4:]


def collect_kernel(pieces, per, place, *refs):
    rows, out = refs[:pieces], refs[pieces]
    where = place[...]
    result = jnp.zeros((8, LANES), jnp.float32)
    for first in range(0, pieces * per, LANES):
        back = rows[first // per][:, first : first + LANES]
        inside = where - first
        hit = (inside >= 0) & (inside < LANES)
        taken = jnp.take_along_axis(back, jnp.where(hit, inside, 0), axis=1)
        result = jnp.where(hit, taken, result)
    out[...] = result


def collect(pieces, cap, place, rows):
    return pl.pallas_call(
        functools.partial(collect_kernel, pieces, ceil_to(cap, LANES)),
        out_shape=jax.ShapeDtypeStruct((8, LANES), jnp.float32),
        name="collect",
    )(place, *rows)


def solution(mesh):
    ngrp, nsub = mesh.shape["grp"], mesh.shape["sub"]
    low = nsub // ngrp
    pieces = ngrp
    chips = ngrp // 2

    def send(block, target):
        route = []
        for g in range(ngrp):
            for s in range(nsub):
                chip, core, plane, small = target(g // 2, g % 2, s // low, s % low)
                route.append((g * nsub + s, (chip * 2 + core) * nsub + plane * low + small))
        return lax.ppermute(block, AXES, route)

    def to_plane(block, s):
        return send(block, lambda x, c, z, y: (x, c, z ^ s, y))

    def to_twin(block):
        return send(block, lambda x, c, z, y: (x, 1 - c, z, y))

    def to_near(block):
        return send(block, lambda x, c, z, y: (x, c, z, 1 - y))

    def to_cross(block, j):
        return send(block, lambda x, c, z, y: (x ^ j, c, z, y))

    def attempt(cap, flagged, embeddings, cluster_id, cluster_rank):
        rows = embeddings.shape[0]
        *own, place = dispatch(pieces, low, cap, flagged, embeddings, cluster_id, cluster_rank)
        own = [own[0]] + [to_plane(own[s], s) for s in range(1, pieces)]
        carried = []
        for p in range(pieces):
            near = to_near(own[p])
            cross = [to_cross(own[p], j) for j in range(1, chips)]
            blocks = [own[p], to_twin(own[p]), near, to_twin(near)]
            blocks += cross + [to_twin(block) for block in cross]
            carried, ends = stage(p, pieces, cap, flagged, blocks, carried)
        a = jnp.maximum(ends[0], to_near(ends[1]))
        back = [a] + [to_plane(a, s) for s in range(1, pieces)]
        where = jnp.pad(place.reshape(rows // LANES, LANES), ((0, 8 - rows // LANES), (0, 0)))
        result = collect(pieces, cap, where, back)
        return result[: rows // LANES].reshape(rows), a[0, -1]

    def body(embeddings, cluster_id, cluster_rank):
        share = embeddings.shape[0] // ngrp
        usual = ceil_to(share + 1, 16)
        most = ceil_to(2 * share + 1, 16)
        result, over = attempt(usual, True, embeddings, cluster_id, cluster_rank)

        def again():
            return attempt(most, False, embeddings, cluster_id, cluster_rank)[0]

        return lax.cond(over > 0.5, again, lambda: result)

    placed = (P(AXES, None), P(AXES), P(AXES))
    return jax.shard_map(body, mesh=mesh, in_specs=placed, out_specs=P(AXES), check_vma=False)
```

time: 136 us -> 114 us (0.84)
  waiting for transfers between devices: 72.3 us -> 50.6 us
  Pallas kernels: 26.3 us -> 31.4 us
  local copies, waits for them, and re-layouts: 6.76 us -> 2.38 us
    ppermute x25 -> x27, waiting for transfers between devices: 72.3 us -> 50.6 us  [send(): return lax.ppermute(block, AXES, route)]
    pallas_call x2 -> x5, Pallas kernels: 20.6 us -> 26.5 us  [the longest x4 25.6 us: stage(): pl.pallas_call(functools.partial(stage_kernel, p, pieces, groups, cap, fl...]
    reshape x2 -> x0, local copies, waits for them, and re-layouts: 2.55 us -> none  [the longest x1 1.28 us: dispatch(): rank.reshape(1, rows)]
    unnamed x54 -> x16, local copies, waits for them, and re-layouts: 2.97 us -> 1.21 us
    ppermute x25 -> x27, starting transfers between devices: 28.5 us -> 27.9 us  [send(): return lax.ppermute(block, AXES, route)]
  transfers between devices with their start and end apart: 25 -> 27, of which waited for: 12 -> 10; matrix products, arithmetic and copies ran while one was open for 1% -> 1% of each run, Pallas kernels for 0% -> 14%
where the time goes in v2:
time: 114 us; the launch traced here: 113 us
  waiting for transfers between devices  50.6 us (44%)
  Pallas kernels  31.4 us (28%)
  starting transfers between devices  27.9 us (24%)
  local copies, waits for them, and re-layouts  2.38 us (2%)
    ppermute x27, waiting for transfers between devices, send(): return lax.ppermute(block, AXES, route)  50.6 us
    ppermute x27, starting transfers between devices, send(): return lax.ppermute(block, AXES, route)  27.9 us
    pallas_call x4, Pallas kernels, stage(): pl.pallas_call(functools.partial(stage_kernel, p, pieces, groups, cap, fl...  25.6 us
    pallas_call x1, Pallas kernels, dispatch(): pl.pallas_call(functools.partial(dispatch_kernel, pieces, low, cap, flagg...  4.91 us
  transfers between devices with their start and end apart: 27, of which 10 were waited for; matrix products, arithmetic and copies ran while one was open for 1% of the time, Pallas kernels for 14%

profile of v2, /device:TPU:0, one launch (start us, length us, event | category | flops | bytes accessed | tf_op | source)
XLA Modules:
  0.0 113.4 jit_solution(4189945279601188436)
XLA Ops:
  0.0 4.9 %dispatch.3 = (bf16[208,1024]{1,0:T(8,128)(2,1)S(1)}, bf16[208,1024]{1,0:T(8,128)(2,1)S(1)}, bf16[208,1024]{1,0:T(8,128)(2,1)S(1)}, bf16[208,1024]{1,0:T(8,128)(2,1)S(1)}, s32[1,768]{1,0:T(1,128)S(1)}) custom-call(bf16[768,1024]{1,0:T(8,128)(2,1)} %emb.1, s32[6,128]{1,0:T(8,128)} %bitcast.11, s32[6,128]{1,0:T(8,128)} %bitcast.13), custom_call_target="tpu_custom_call" | custom-call | tf_op jit(solution)/shard_map/dispatch/pallas_call | solution.py:96
  4.9 3.0 %collective-permute-start.46 = (bf16[208,1024]{1,0:T(8,128)(2,1)S(1)}, bf16[208,1024]{1,0:T(8,128)(2,1)S(1)}, u32[]{:S(2)}, u32[]{:S(2)}) collective-permute-start(bf16[208,1024]{1,0:T(8,128)(2,1)S(1)} %get-tuple-element.62.refs_0_), channel_id=1, source_target_pairs={{0,1},{1,0},{2,3},{3,2},{4,5},{5,4},{6,7},{7,6},{8,9},{9,8},{10,11... | collective-permute-start | bytes 1277960 | tf_op jit(solution)/shard_map/ppermute | solution.py:243
  8.0 1.5 %collective-permute-start.48 = (bf16[208,1024]{1,0:T(8,128)(2,1)S(1)}, bf16[208,1024]{1,0:T(8,128)(2,1)S(1)}, u32[]{:S(2)}, u32[]{:S(2)}) collective-permute-start(bf16[208,1024]{1,0:T(8,128)(2,1)S(1)} %get-tuple-element.62.refs_0_), channel_id=1, source_target_pairs={{0,16},{1,17},{2,18},{3,19},{4,20},{5,21},{6,22},{7,23},{8,24},{9,... | collective-permute-start | bytes 1277960 | tf_op jit(solution)/shard_map/ppermute | solution.py:243
  9.4 1.6 %collective-permute-start.39 = (bf16[208,1024]{1,0:T(8,128)(2,1)S(1)}, bf16[208,1024]{1,0:T(8,128)(2,1)S(1)}, u32[]{:S(2)}, u32[]{:S(2)}) collective-permute-start(bf16[208,1024]{1,0:T(8,128)(2,1)S(1)} %get-tuple-element.61), channel_id=1, source_target_pairs={{0,2},{1,3},{2,0},{3,1},{4,6},{5,7},{6,4},{7,5},{8,10},{9,11},{10,... | collective-permute-start | bytes 1277960 | tf_op jit(solution)/shard_map/ppermute | solution.py:243
  11.0 2.6 %collective-permute-start.33 = (bf16[208,1024]{1,0:T(8,128)(2,1)S(1)}, bf16[208,1024]{1,0:T(8,128)(2,1)S(1)}, u32[]{:S(2)}, u32[]{:S(2)}) collective-permute-start(bf16[208,1024]{1,0:T(8,128)(2,1)S(1)} %get-tuple-element.60), channel_id=1, source_target_pairs={{0,4},{1,5},{2,6},{3,7},{4,0},{5,1},{6,2},{7,3},{8,12},{9,13},{10,... | collective-permute-start | bytes 1277960 | tf_op jit(solution)/shard_map/ppermute | solution.py:243
  13.6 4.2 %collective-permute-done.46.refs_2_ = bf16[208,1024]{1,0:T(8,128)(2,1)S(1)} collective-permute-done((bf16[208,1024]{1,0:T(8,128)(2,1)S(1)}, bf16[208,1024]{1,0:T(8,128)(2,1)S(1)}, u32[]{:S(2)}, u32[]{:S(2)}) %collective-permute-start.46) | collective-permute-done | bytes 426016 | tf_op jit(solution)/shard_map/ppermute | solution.py:243
  17.8 3.8 %collective-permute-start.27 = (bf16[208,1024]{1,0:T(8,128)(2,1)S(1)}, bf16[208,1024]{1,0:T(8,128)(2,1)S(1)}, u32[]{:S(2)}, u32[]{:S(2)}) collective-permute-start(bf16[208,1024]{1,0:T(8,128)(2,1)S(1)} %get-tuple-element.59), channel_id=1, source_target_pairs={{0,6},{1,7},{2,4},{3,5},{4,2},{5,3},{6,0},{7,1},{8,14},{9,15},{10,... | collective-permute-start | bytes 1277960 | tf_op jit(solution)/shard_map/ppermute | solution.py:243
  22.1 8.3 %collective-permute-done.39.refs_0_ = bf16[208,1024]{1,0:T(8,128)(2,1)S(1)} collective-permute-done((bf16[208,1024]{1,0:T(8,128)(2,1)S(1)}, bf16[208,1024]{1,0:T(8,128)(2,1)S(1)}, u32[]{:S(2)}, u32[]{:S(2)}) %collective-permute-start.39) | collective-permute-done | bytes 426016 | tf_op jit(solution)/shard_map/ppermute | solution.py:243
  30.9 12.0 %collective-permute-done.33.refs_0_ = bf16[208,1024]{1,0:T(8,128)(2,1)S(1)} collective-permute-done((bf16[208,1024]{1,0:T(8,128)(2,1)S(1)}, bf16[208,1024]{1,0:T(8,128)(2,1)S(1)}, u32[]{:S(2)}, u32[]{:S(2)}) %collective-permute-start.33) | collective-permute-done | bytes 426016 | tf_op jit(solution)/shard_map/ppermute | solution.py:243
  44.0 1.5 %collective-permute-start.37 = (bf16[208,1024]{1,0:T(8,128)(2,1)S(1)}, bf16[208,1024]{1,0:T(8,128)(2,1)S(1)}, u32[]{:S(2)}, u32[]{:S(2)}) collective-permute-start(bf16[208,1024]{1,0:T(8,128)(2,1)S(1)} %collective-permute-done.33.refs_0_), channel_id=1, source_target_pairs={{0,16},{1,17},{2,18},{3,19},{4,20},{5,21},{6,22},{7,23},{8,24},{9,... | collective-permute-start | bytes 1277960 | tf_op jit(solution)/shard_map/ppermute | solution.py:243
  45.5 9.8 %collective-permute-done.43.refs_4_ = bf16[208,1024]{1,0:T(8,128)(2,1)S(1)} collective-permute-done((bf16[208,1024]{1,0:T(8,128)(2,1)S(1)}, bf16[208,1024]{1,0:T(8,128)(2,1)S(1)}, u32[]{:S(2)}, u32[]{:S(2)}) %collective-permute-start.43) | collective-permute-done | bytes 426016 | tf_op jit(solution)/shard_map/ppermute | solution.py:243
  56.1 8.3 %collective-permute-done.37.refs_4_ = bf16[208,1024]{1,0:T(8,128)(2,1)S(1)} collective-permute-done((bf16[208,1024]{1,0:T(8,128)(2,1)S(1)}, bf16[208,1024]{1,0:T(8,128)(2,1)S(1)}, u32[]{:S(2)}, u32[]{:S(2)}) %collective-permute-start.37) | collective-permute-done | bytes 426016 | tf_op jit(solution)/shard_map/ppermute | solution.py:243
  65.0 3.0 %stage0.3 = (bf16[4992,1024]{1,0:T(8,128)(2,1)S(1)}, f32[4992,128]{1,0:T(8,128)S(1)}, f32[8,2048]{1,0:T(8,128)S(1)}, f32[8,2176]{1,0:T(8,128)S(1)}) custom-call(bf16[208,1024]{1,0:T(8,128)(2,1)S(1)} %get-tuple-element.62.refs_0_, bf16[208,1024]{1,0:T(8,128)(2,1)S(1)} %collective-permute-done.45.refs_1_, ...), custom_call_target="tpu_custom_call" | custom-call | flops 708837376 | bytes 2555904 | tf_op jit(solution)/shard_map/stage0/pallas_call | solution.py:193
  68.0 1.2 %collective-permute-done.31.refs_4_ = bf16[208,1024]{1,0:T(8,128)(2,1)S(1)} collective-permute-done((bf16[208,1024]{1,0:T(8,128)(2,1)S(1)}, bf16[208,1024]{1,0:T(8,128)(2,1)S(1)}, u32[]{:S(2)}, u32[]{:S(2)}) %collective-permute-start.31) | collective-permute-done | bytes 426016 | tf_op jit(solution)/shard_map/ppermute | solution.py:243
  69.9 5.3 %stage1.3 = (bf16[4992,1024]{1,0:T(8,128)(2,1)S(1)}, f32[4992,128]{1,0:T(8,128)S(1)}, f32[8,2048]{1,0:T(8,128)S(1)}, f32[8,2176]{1,0:T(8,128)S(1)}) custom-call(bf16[208,1024]{1,0:T(8,128)(2,1)S(1)} %collective-permute-done.39.refs_0_, ...), custom_call_target="tpu_custom_call", output_to_operand_aliasing={{0}: (6, {}), {1}: (7, {}), {2}: (8, {}), {3}: (9, {})} | custom-call | flops 2126512128 | bytes 2555904 | tf_op jit(solution)/shard_map/stage1/pallas_call | solution.py:193
  75.2 7.5 %stage2.3 = (bf16[4992,1024]{1,0:T(8,128)(2,1)S(1)}, f32[4992,128]{1,0:T(8,128)S(1)}, f32[8,2048]{1,0:T(8,128)S(1)}, f32[8,2176]{1,0:T(8,128)S(1)}) custom-call(bf16[208,1024]{1,0:T(8,128)(2,1)S(1)} %collective-permute-done.33.refs_0_, ...), custom_call_target="tpu_custom_call", output_to_operand_aliasing={{0}: (6, {}), {1}: (7, {}), {2}: (8, {}), {3}: (9, {})} | custom-call | flops 3544186880 | bytes 2555904 | tf_op jit(solution)/shard_map/stage2/pallas_call | solution.py:193
  82.8 9.7 %stage3.3 = (bf16[4992,1024]{1,0:T(8,128)(2,1)S(1)}, f32[4992,128]{1,0:T(8,128)S(1)}, f32[8,2048]{1,0:T(8,128)S(1)}, f32[8,2176]{1,0:T(8,128)S(1)}, f32[8,1152]{1,0:T(8,128)S(1)}, /*index=5*/f32[8,1152]{1,0:T(8,128)S(1)}) custom-call(bf16[208,1024]{1,0:T(8,128)(2,1)S(1)} %collective-permute-d, ...), custom_call_target="tpu_custom_call", output_to_operand_aliasing={{0}: (6, {}), {1}: (7, {}), {2}: (8, {}), {3}: (9, {})} | custom-call | flops 4961861632 | bytes 2555904 | tf_op jit(solution)/shard_map/stage3/pallas_call | solution.py:193
  93.1 3.5 %collective-permute-done.50 = f32[8,1152]{1,0:T(8,128)S(1)} collective-permute-done((f32[8,1152]{1,0:T(8,128)S(1)}, f32[8,1152]{1,0:T(8,128)S(1)}, u32[]{:S(2)}, u32[]{:S(2)}) %collective-permute-start.50) | collective-permute-done | bytes 36896 | tf_op jit(solution)/shard_map/ppermute | solution.py:243
  96.5 7.6 %collective-permute-start.51 = (f32[8,1152]{1,0:T(8,128)S(1)}, f32[8,1152]{1,0:T(8,128)S(1)}, u32[]{:S(2)}, u32[]{:S(2)}) collective-permute-start(f32[8,1152]{1,0:T(8,128)S(1)} %max.6.refs_0_), channel_id=1, source_target_pairs={{0,2},{1,3},{2,0},{3,1},{4,6},{5,7},{6,4},{7,5},{8,10},{9,11},{10,... | collective-permute-start | bytes 110600 | tf_op jit(solution)/shard_map/ppermute | solution.py:243
  104.2 1.1 collective-permute-start.52
  105.2 1.4 %collective-permute-start.53 = (f32[8,1152]{1,0:T(8,128)S(1)}, f32[8,1152]{1,0:T(8,128)S(1)}, u32[]{:S(2)}, u32[]{:S(2)}) collective-permute-start(f32[8,1152]{1,0:T(8,128)S(1)} %max.6.refs_0_), channel_id=1, source_target_pairs={{0,6},{1,7},{2,4},{3,5},{4,2},{5,3},{6,0},{7,1},{8,14},{9,15},{10,... | collective-permute-start | bytes 110600 | tf_op jit(solution)/shard_map/ppermute | solution.py:243
  108.4 1.2 %collective-permute-done.52.refs_2_ = f32[8,1152]{1,0:T(8,128)S(1)} collective-permute-done((f32[8,1152]{1,0:T(8,128)S(1)}, f32[8,1152]{1,0:T(8,128)S(1)}, u32[]{:S(2)}, u32[]{:S(2)}) %collective-permute-start.52) | collective-permute-done | bytes 36896 | tf_op jit(solution)/shard_map/ppermute | solution.py:243
  109.6 1.3 %collective-permute-done.53.refs_3_ = f32[8,1152]{1,0:T(8,128)S(1)} collective-permute-done((f32[8,1152]{1,0:T(8,128)S(1)}, f32[8,1152]{1,0:T(8,128)S(1)}, u32[]{:S(2)}, u32[]{:S(2)}) %collective-permute-start.53) | collective-permute-done | bytes 36896 | tf_op jit(solution)/shard_map/ppermute | solution.py:243
  111.6 0.9 collect.3
  (58 shorter events, 7.4 us)
Async XLA Ops:
  4.9 12.8 %collective-permute-start.46 = (bf16[208,1024]{1,0:T(8,128)(2,1)S(1)}, bf16[208,1024]{1,0:T(8,128)(2,1)S(1)}, u32[]{:S(2)}, u32[]{:S(2)}) collective-permute-start(bf16[208,1024]{1,0:T(8,128)(2,1)S(1)} %get-tuple-element.62.refs_0_), channel_id=1, source_target_pairs={{0,1},{1,0},{2,3},{3,2},{4,5},{5,4},{6,7},{7,6},{8,9},{9,8},{10,11... | collective-permute-start | bytes 1277960 | tf_op jit(solution)/shard_map/ppermute | solution.py:243
  8.0 13.6 %collective-permute-start.48 = (bf16[208,1024]{1,0:T(8,128)(2,1)S(1)}, bf16[208,1024]{1,0:T(8,128)(2,1)S(1)}, u32[]{:S(2)}, u32[]{:S(2)}) collective-permute-start(bf16[208,1024]{1,0:T(8,128)(2,1)S(1)} %get-tuple-element.62.refs_0_), channel_id=1, source_target_pairs={{0,16},{1,17},{2,18},{3,19},{4,20},{5,21},{6,22},{7,23},{8,24},{9,... | collective-permute-start | bytes 1277960 | tf_op jit(solution)/shard_map/ppermute | solution.py:243
  9.4 12.2 %collective-permute-start.45 = (bf16[208,1024]{1,0:T(8,128)(2,1)S(1)}, bf16[208,1024]{1,0:T(8,128)(2,1)S(1)}, u32[]{:S(2)}, u32[]{:S(2)}) collective-permute-start(bf16[208,1024]{1,0:T(8,128)(2,1)S(1)} %get-tuple-element.62.refs_0_), channel_id=1, source_target_pairs={{0,8},{1,9},{2,10},{3,11},{4,12},{5,13},{6,14},{7,15},{8,0},{9,1},... | collective-permute-start | bytes 1277960 | tf_op jit(solution)/shard_map/ppermute | solution.py:243
  9.4 20.9 %collective-permute-start.39 = (bf16[208,1024]{1,0:T(8,128)(2,1)S(1)}, bf16[208,1024]{1,0:T(8,128)(2,1)S(1)}, u32[]{:S(2)}, u32[]{:S(2)}) collective-permute-start(bf16[208,1024]{1,0:T(8,128)(2,1)S(1)} %get-tuple-element.61), channel_id=1, source_target_pairs={{0,2},{1,3},{2,0},{3,1},{4,6},{5,7},{6,4},{7,5},{8,10},{9,11},{10,... | collective-permute-start | bytes 1277960 | tf_op jit(solution)/shard_map/ppermute | solution.py:243
  11.0 31.9 %collective-permute-start.33 = (bf16[208,1024]{1,0:T(8,128)(2,1)S(1)}, bf16[208,1024]{1,0:T(8,128)(2,1)S(1)}, u32[]{:S(2)}, u32[]{:S(2)}) collective-permute-start(bf16[208,1024]{1,0:T(8,128)(2,1)S(1)} %get-tuple-element.60), channel_id=1, source_target_pairs={{0,4},{1,5},{2,6},{3,7},{4,0},{5,1},{6,2},{7,3},{8,12},{9,13},{10,... | collective-permute-start | bytes 1277960 | tf_op jit(solution)/shard_map/ppermute | solution.py:243
  17.8 25.6 %collective-permute-start.27 = (bf16[208,1024]{1,0:T(8,128)(2,1)S(1)}, bf16[208,1024]{1,0:T(8,128)(2,1)S(1)}, u32[]{:S(2)}, u32[]{:S(2)}) collective-permute-start(bf16[208,1024]{1,0:T(8,128)(2,1)S(1)} %get-tuple-element.59), channel_id=1, source_target_pairs={{0,6},{1,7},{2,4},{3,5},{4,2},{5,3},{6,0},{7,1},{8,14},{9,15},{10,... | collective-permute-start | bytes 1277960 | tf_op jit(solution)/shard_map/ppermute | solution.py:243
  21.6 21.8 %collective-permute-start.47 = (bf16[208,1024]{1,0:T(8,128)(2,1)S(1)}, bf16[208,1024]{1,0:T(8,128)(2,1)S(1)}, u32[]{:S(2)}, u32[]{:S(2)}) collective-permute-start(bf16[208,1024]{1,0:T(8,128)(2,1)S(1)} %collective-permute-done.46.refs_2_), channel_id=1, source_target_pairs={{0,8},{1,9},{2,10},{3,11},{4,12},{5,13},{6,14},{7,15},{8,0},{9,1},... | collective-permute-start | bytes 1277960 | tf_op jit(solution)/shard_map/ppermute | solution.py:243
  21.6 22.4 %collective-permute-start.49 = (bf16[208,1024]{1,0:T(8,128)(2,1)S(1)}, bf16[208,1024]{1,0:T(8,128)(2,1)S(1)}, u32[]{:S(2)}, u32[]{:S(2)}) collective-permute-start(bf16[208,1024]{1,0:T(8,128)(2,1)S(1)} %collective-permute-done.48.refs_4_), channel_id=1, source_target_pairs={{0,8},{1,9},{2,10},{3,11},{4,12},{5,13},{6,14},{7,15},{8,0},{9,1},... | collective-permute-start | bytes 1277960 | tf_op jit(solution)/shard_map/ppermute | solution.py:243
  30.4 15.1 %collective-permute-start.41 = (bf16[208,1024]{1,0:T(8,128)(2,1)S(1)}, bf16[208,1024]{1,0:T(8,128)(2,1)S(1)}, u32[]{:S(2)}, u32[]{:S(2)}) collective-permute-start(bf16[208,1024]{1,0:T(8,128)(2,1)S(1)} %collective-permute-done.39.refs_0_), channel_id=1, source_target_pairs={{0,1},{1,0},{2,3},{3,2},{4,5},{5,4},{6,7},{7,6},{8,9},{9,8},{10,11... | collective-permute-start | bytes 1277960 | tf_op jit(solution)/shard_map/ppermute | solution.py:243
  42.9 12.4 %collective-permute-start.43 = (bf16[208,1024]{1,0:T(8,128)(2,1)S(1)}, bf16[208,1024]{1,0:T(8,128)(2,1)S(1)}, u32[]{:S(2)}, u32[]{:S(2)}) collective-permute-start(bf16[208,1024]{1,0:T(8,128)(2,1)S(1)} %collective-permute-done.39.refs_0_), channel_id=1, source_target_pairs={{0,16},{1,17},{2,18},{3,19},{4,20},{5,21},{6,22},{7,23},{8,24},{9,... | collective-permute-start | bytes 1277960 | tf_op jit(solution)/shard_map/ppermute | solution.py:243
  43.4 11.8 %collective-permute-start.40 = (bf16[208,1024]{1,0:T(8,128)(2,1)S(1)}, bf16[208,1024]{1,0:T(8,128)(2,1)S(1)}, u32[]{:S(2)}, u32[]{:S(2)}) collective-permute-start(bf16[208,1024]{1,0:T(8,128)(2,1)S(1)} %collective-permute-done.39.refs_0_), channel_id=1, source_target_pairs={{0,8},{1,9},{2,10},{3,11},{4,12},{5,13},{6,14},{7,15},{8,0},{9,1},... | collective-permute-start | bytes 1277960 | tf_op jit(solution)/shard_map/ppermute | solution.py:243
  43.4 12.7 %collective-permute-start.35 = (bf16[208,1024]{1,0:T(8,128)(2,1)S(1)}, bf16[208,1024]{1,0:T(8,128)(2,1)S(1)}, u32[]{:S(2)}, u32[]{:S(2)}) collective-permute-start(bf16[208,1024]{1,0:T(8,128)(2,1)S(1)} %collective-permute-done.33.refs_0_), channel_id=1, source_target_pairs={{0,1},{1,0},{2,3},{3,2},{4,5},{5,4},{6,7},{7,6},{8,9},{9,8},{10,11... | collective-permute-start | bytes 1277960 | tf_op jit(solution)/shard_map/ppermute | solution.py:243
  44.0 20.4 %collective-permute-start.37 = (bf16[208,1024]{1,0:T(8,128)(2,1)S(1)}, bf16[208,1024]{1,0:T(8,128)(2,1)S(1)}, u32[]{:S(2)}, u32[]{:S(2)}) collective-permute-start(bf16[208,1024]{1,0:T(8,128)(2,1)S(1)} %collective-permute-done.33.refs_0_), channel_id=1, source_target_pairs={{0,16},{1,17},{2,18},{3,19},{4,20},{5,21},{6,22},{7,23},{8,24},{9,... | collective-permute-start | bytes 1277960 | tf_op jit(solution)/shard_map/ppermute | solution.py:243
  45.5 18.9 %collective-permute-start.34 = (bf16[208,1024]{1,0:T(8,128)(2,1)S(1)}, bf16[208,1024]{1,0:T(8,128)(2,1)S(1)}, u32[]{:S(2)}, u32[]{:S(2)}) collective-permute-start(bf16[208,1024]{1,0:T(8,128)(2,1)S(1)} %collective-permute-done.33.refs_0_), channel_id=1, source_target_pairs={{0,8},{1,9},{2,10},{3,11},{4,12},{5,13},{6,14},{7,15},{8,0},{9,1},... | collective-permute-start | bytes 1277960 | tf_op jit(solution)/shard_map/ppermute | solution.py:243
  55.3 9.6 %collective-permute-start.29 = (bf16[208,1024]{1,0:T(8,128)(2,1)S(1)}, bf16[208,1024]{1,0:T(8,128)(2,1)S(1)}, u32[]{:S(2)}, u32[]{:S(2)}) collective-permute-start(bf16[208,1024]{1,0:T(8,128)(2,1)S(1)} %collective-permute-done.27.refs_0_), channel_id=1, source_target_pairs={{0,1},{1,0},{2,3},{3,2},{4,5},{5,4},{6,7},{7,6},{8,9},{9,8},{10,11... | collective-permute-start | bytes 1277960 | tf_op jit(solution)/shard_map/ppermute | solution.py:243
  55.3 14.0 %collective-permute-start.31 = (bf16[208,1024]{1,0:T(8,128)(2,1)S(1)}, bf16[208,1024]{1,0:T(8,128)(2,1)S(1)}, u32[]{:S(2)}, u32[]{:S(2)}) collective-permute-start(bf16[208,1024]{1,0:T(8,128)(2,1)S(1)} %collective-permute-done.27.refs_0_), channel_id=1, source_target_pairs={{0,16},{1,17},{2,18},{3,19},{4,20},{5,21},{6,22},{7,23},{8,24},{9,... | collective-permute-start | bytes 1277960 | tf_op jit(solution)/shard_map/ppermute | solution.py:243
  56.1 13.2 %collective-permute-start.42 = (bf16[208,1024]{1,0:T(8,128)(2,1)S(1)}, bf16[208,1024]{1,0:T(8,128)(2,1)S(1)}, u32[]{:S(2)}, u32[]{:S(2)}) collective-permute-start(bf16[208,1024]{1,0:T(8,128)(2,1)S(1)} %collective-permute-done.41.refs_2_), channel_id=1, source_target_pairs={{0,8},{1,9},{2,10},{3,11},{4,12},{5,13},{6,14},{7,15},{8,0},{9,1},... | collective-permute-start | bytes 1277960 | tf_op jit(solution)/shard_map/ppermute | solution.py:243
  64.4 10.8 %collective-permute-start.36 = (bf16[208,1024]{1,0:T(8,128)(2,1)S(1)}, bf16[208,1024]{1,0:T(8,128)(2,1)S(1)}, u32[]{:S(2)}, u32[]{:S(2)}) collective-permute-start(bf16[208,1024]{1,0:T(8,128)(2,1)S(1)} %collective-permute-done.35.refs_2_), channel_id=1, source_target_pairs={{0,8},{1,9},{2,10},{3,11},{4,12},{5,13},{6,14},{7,15},{8,0},{9,1},... | collective-permute-start | bytes 1277960 | tf_op jit(solution)/shard_map/ppermute | solution.py:243
  64.9 10.3 %collective-permute-start.38 = (bf16[208,1024]{1,0:T(8,128)(2,1)S(1)}, bf16[208,1024]{1,0:T(8,128)(2,1)S(1)}, u32[]{:S(2)}, u32[]{:S(2)}) collective-permute-start(bf16[208,1024]{1,0:T(8,128)(2,1)S(1)} %collective-permute-done.37.refs_4_), channel_id=1, source_target_pairs={{0,8},{1,9},{2,10},{3,11},{4,12},{5,13},{6,14},{7,15},{8,0},{9,1},... | collective-permute-start | bytes 1277960 | tf_op jit(solution)/shard_map/ppermute | solution.py:243
  69.3 13.5 %collective-permute-start.28 = (bf16[208,1024]{1,0:T(8,128)(2,1)S(1)}, bf16[208,1024]{1,0:T(8,128)(2,1)S(1)}, u32[]{:S(2)}, u32[]{:S(2)}) collective-permute-start(bf16[208,1024]{1,0:T(8,128)(2,1)S(1)} %collective-permute-done.27.refs_0_), channel_id=1, source_target_pairs={{0,8},{1,9},{2,10},{3,11},{4,12},{5,13},{6,14},{7,15},{8,0},{9,1},... | collective-permute-start | bytes 1277960 | tf_op jit(solution)/shard_map/ppermute | solution.py:243
  69.3 13.5 %collective-permute-start.30 = (bf16[208,1024]{1,0:T(8,128)(2,1)S(1)}, bf16[208,1024]{1,0:T(8,128)(2,1)S(1)}, u32[]{:S(2)}, u32[]{:S(2)}) collective-permute-start(bf16[208,1024]{1,0:T(8,128)(2,1)S(1)} %collective-permute-done.29.refs_2_), channel_id=1, source_target_pairs={{0,8},{1,9},{2,10},{3,11},{4,12},{5,13},{6,14},{7,15},{8,0},{9,1},... | collective-permute-start | bytes 1277960 | tf_op jit(solution)/shard_map/ppermute | solution.py:243
  69.8 13.0 %collective-permute-start.32 = (bf16[208,1024]{1,0:T(8,128)(2,1)S(1)}, bf16[208,1024]{1,0:T(8,128)(2,1)S(1)}, u32[]{:S(2)}, u32[]{:S(2)}) collective-permute-start(bf16[208,1024]{1,0:T(8,128)(2,1)S(1)} %collective-permute-done.31.refs_4_), channel_id=1, source_target_pairs={{0,8},{1,9},{2,10},{3,11},{4,12},{5,13},{6,14},{7,15},{8,0},{9,1},... | collective-permute-start | bytes 1277960 | tf_op jit(solution)/shard_map/ppermute | solution.py:243
  96.5 11.8 %collective-permute-start.51 = (f32[8,1152]{1,0:T(8,128)S(1)}, f32[8,1152]{1,0:T(8,128)S(1)}, u32[]{:S(2)}, u32[]{:S(2)}) collective-permute-start(f32[8,1152]{1,0:T(8,128)S(1)} %max.6.refs_0_), channel_id=1, source_target_pairs={{0,2},{1,3},{2,0},{3,1},{4,6},{5,7},{6,4},{7,5},{8,10},{9,11},{10,... | collective-permute-start | bytes 110600 | tf_op jit(solution)/shard_map/ppermute | solution.py:243
  105.2 5.8 %collective-permute-start.53 = (f32[8,1152]{1,0:T(8,128)S(1)}, f32[8,1152]{1,0:T(8,128)S(1)}, u32[]{:S(2)}, u32[]{:S(2)}) collective-permute-start(f32[8,1152]{1,0:T(8,128)S(1)} %max.6.refs_0_), channel_id=1, source_target_pairs={{0,6},{1,7},{2,4},{3,5},{4,2},{5,3},{6,0},{7,1},{8,14},{9,15},{10,... | collective-permute-start | bytes 110600 | tf_op jit(solution)/shard_map/ppermute | solution.py:243
  (11 other events, 123.8 us)

commit v3 on v2

--- a/solution.py
+++ b/solution.py
@@ -24,6 +24,26 @@
     )
 
 
+def steps(pieces):
+    return [p ^ (p >> 1) for p in range(pieces)]
+
+
+def after(blocks, earlier):
+    if not earlier:
+        return blocks
+    held = [pltpu.with_memory_space_constraint(x, pltpu.VMEM) for x in blocks]
+    return list(pl.pallas_call(
+        lambda *refs: None,
+        out_shape=[pltpu.VMEM(x.shape, x.dtype) for x in blocks],
+        in_specs=[pl.BlockSpec(memory_space=pltpu.VMEM)] * len(blocks)
+        + [pl.BlockSpec(memory_space=pl.ANY)] * len(earlier),
+        out_specs=[pl.BlockSpec(memory_space=pltpu.VMEM)] * len(blocks),
+        input_output_aliases={i: i for i in range(len(blocks))},
+        compiler_params=pltpu.CompilerParams(vmem_limit_bytes=VMEM),
+        name="after",
+    )(*held, *earlier))
+
+
 def flat(ref):
     return jnp.concatenate([ref[b : b + 1, :] for b in range(ref.shape[0])], axis=1)
 
@@ -41,7 +61,10 @@
         scale = lax.rsqrt(jnp.sum(wide * wide, axis=1, keepdims=True) + 1e-06)
         unit[at, :] = (wide * scale).astype(jnp.bfloat16)
 
-    piece = flat(cid) ^ plane
+    step = flat(cid) ^ plane
+    piece = jnp.zeros(step.shape, jnp.int32)
+    for p, s in enumerate(steps(pieces)):
+        piece = jnp.where(step == s, p, piece)
     which = lax.broadcasted_iota(jnp.int32, (16, LANES), 0)
     upper = (
         lax.broadcasted_iota(jnp.int32, (LANES, LANES), 0)
@@ -106,15 +129,17 @@
     )(emb, cid.reshape(rows // LANES, LANES), rank.reshape(rows // LANES, LANES))
 
 
-def stage_kernel(p, pieces, groups, cap, flagged, chunk, *refs):
+def stage_kernel(p, pieces, groups, cap, flagged, *refs):
     blocks, refs = refs[:groups], refs[groups:]
     if p:
-        refs = refs[4:]
-    store, keys, limits, best, refs = *refs[:4], refs[4:]
+        refs = refs[5:]
+    store, keys, limits, best, cols, token, refs = *refs[:6], refs[6:]
     sem = refs[-1]
     lanes_per = ceil_to(cap, LANES)
     per = groups * cap
     base = p * per
+    shared = per - 2 * cap
+    token[...] = jnp.zeros(token.shape, jnp.float32)
 
     copies = []
     for g in range(groups):
@@ -130,6 +155,9 @@
     if p == 0:
         limits[...] = jnp.zeros(limits.shape, jnp.float32)
         best[...] = jnp.full(best.shape, -1.0, jnp.float32)
+        cols[...] = jnp.full(cols.shape, -1.0, jnp.float32)
+        if lanes_per > cap:
+            store[pieces * per :, :] = jnp.zeros((lanes_per - cap, store.shape[1]), jnp.bfloat16)
     for g in range(groups):
         copies[g].wait()
         end = base + (g + 1) * cap
@@ -138,8 +166,8 @@
         ranks = jnp.where(lane < cap - 1, ranks, EMPTY * RADIX)
         if flagged:
             flag = jnp.maximum(flag, note[:, 2 * lanes_per : 2 * lanes_per + LANES])
-        if g in (0, 2):
-            at = (2 * p + g // 2) * lanes_per
+        if g in (0, groups - 1):
+            at = (2 * p + g // (groups - 1)) * lanes_per
             limits[:, at : at + lanes_per] = jnp.broadcast_to(ranks, (8, lanes_per))
         column = jnp.sum(jnp.where(square, ranks, 0.0), axis=1, keepdims=True)
         keys[end - cap : end, :] = jnp.broadcast_to(column, (cap, LANES))
@@ -152,24 +180,46 @@
         old = t > p
         first = jnp.where(old, t - p - 1, p)
         second = jnp.where(old, p, t)
-        for group, start, total in ((0, 0, per), (2, 4 * cap, per - 4 * cap)):
+        for side, group in enumerate((0, groups - 1)):
             query = store[pl.ds(pl.multiple_of(first * per + group * cap, 16), lanes_per), :]
-            at = pl.ds(pl.multiple_of((first * 2 + group // 2) * lanes_per, LANES), lanes_per)
+            at = pl.ds(pl.multiple_of((first * 2 + side) * lanes_per, LANES), lanes_per)
             limit = limits[0:1, at]
             top = best[:, at]
-            for offset in range(start, start + total, chunk):
+            if side == 0:
+                chunks = [(0, 2 * cap)]
+                chunks += [(g * cap, 2 * cap) for g in range(2, groups - 1, 2)]
+                if groups % 2:
+                    chunks.append(((groups - 1) * cap, cap))
+            else:
+                chunks = [(g * cap, cap) for g in range(2, groups - 1)]
+            for offset, chunk in chunks:
                 rows = pl.ds(pl.multiple_of(second * per + offset, 16), chunk)
                 sims = nt_dot(store[rows, :], query)
                 kr = jnp.concatenate([keys[rows, :]] * (lanes_per // LANES), axis=1)
-                sims = jnp.where(kr < limit, sims, -1.0)
-                top = jnp.maximum(top, jnp.max(sims.reshape(chunk // 8, 8, lanes_per), axis=0))
+                earlier = kr < limit
+                ahead = jnp.where(earlier, sims, -1.0)
+                top = jnp.maximum(top, jnp.max(ahead.reshape(chunk // 8, 8, lanes_per), axis=0))
+                if offset >= 2 * cap:
+                    spot = pl.ds(pl.multiple_of(second * shared + offset - 2 * cap, 16), chunk)
+                    behind = jnp.where(earlier, -1.0, sims)
+                    fold = cols[spot, :]
+                    for k in range(0, lanes_per, LANES):
+                        fold = jnp.maximum(fold, behind[:, k : k + LANES])
+                    cols[spot, :] = fold
             best[:, at] = top
 
     if p == pieces - 1:
-        for group, out in enumerate(refs[:2]):
+        for i, out in enumerate(refs[: groups - 1]):
             for s in range(pieces):
-                at = (2 * s + group) * lanes_per
-                row = jnp.max(best[:, at : at + lanes_per], axis=0, keepdims=True)
+                row = jnp.full((1, lanes_per), -1.0, jnp.float32)
+                if i in (0, groups - 2):
+                    at = (2 * s + i // (groups - 2)) * lanes_per
+                    row = jnp.max(best[:, at : at + lanes_per], axis=0, keepdims=True)
+                if i:
+                    at = s * shared + (i - 1) * cap
+                    column = jnp.max(cols[at : at + cap, :], axis=1, keepdims=True)
+                    turned = jnp.max(jnp.where(square, column, -1.0), axis=0, keepdims=True)
+                    row = jnp.maximum(row, turned)
                 out[:, s * lanes_per : (s + 1) * lanes_per] = jnp.broadcast_to(row, (8, lanes_per))
             out[:, pieces * lanes_per :] = best[:, 2 * pieces * lanes_per :]
 
@@ -180,22 +230,24 @@
     lanes_per = ceil_to(cap, LANES)
     per = groups * cap
     f32 = jnp.float32
-    chunk = 2 * cap
     kept = [
-        pltpu.VMEM((pieces * per, width), jnp.bfloat16),
+        pltpu.VMEM((pieces * per + lanes_per - cap, width), jnp.bfloat16),
         pltpu.VMEM((pieces * per, LANES), f32),
         pltpu.VMEM((8, 2 * pieces * lanes_per), f32),
         pltpu.VMEM((8, 2 * pieces * lanes_per + LANES), f32),
+        pltpu.VMEM((pieces * (groups - 2) * cap, LANES), f32),
+        jax.ShapeDtypeStruct((8, LANES), f32),
     ]
-    ends = [jax.ShapeDtypeStruct((8, pieces * lanes_per + LANES), f32)] * 2
-    last = p == pieces - 1
-    pairs = (2 * p + 1) * (2 * per - 4 * cap) * cap
+    ends = [jax.ShapeDtypeStruct((8, pieces * lanes_per + LANES), f32)] * (groups - 1)
+    if p < pieces - 1:
+        ends = []
+    pairs = (2 * p + 1) * (2 * groups - 3) * cap * cap
     got = pl.pallas_call(
-        functools.partial(stage_kernel, p, pieces, groups, cap, flagged, chunk),
-        out_shape=kept + (ends if last else []),
+        functools.partial(stage_kernel, p, pieces, groups, cap, flagged),
+        out_shape=kept + ends,
         in_specs=[pl.BlockSpec(memory_space=pl.ANY)] * groups
         + [pl.BlockSpec(memory_space=pltpu.VMEM)] * len(carried),
-        out_specs=[pl.BlockSpec(memory_space=pltpu.VMEM)] * (4 + 2 * last),
+        out_specs=[pl.BlockSpec(memory_space=pltpu.VMEM)] * (6 + len(ends)),
         scratch_shapes=[pltpu.SemaphoreType.DMA((groups,))],
         input_output_aliases={groups + i: i for i in range(len(carried))},
         cost_estimate=pl.CostEstimate(
@@ -204,7 +256,7 @@
         compiler_params=pltpu.CompilerParams(vmem_limit_bytes=VMEM),
         name="stage" + str(p),
     )(*blocks, *[pltpu.with_memory_space_constraint(x, pltpu.VMEM) for x in carried])
-    return got[:4], got[4:]
+    return got[:5], got[5], got[6:]
 
 
 def collect_kernel(pieces, per, place, *refs):
@@ -248,25 +300,41 @@
     def to_twin(block):
         return send(block, lambda x, c, z, y: (x, 1 - c, z, y))
 
+    def bit(x, j):
+        return (x // (j & -j)) % 2
+
     def to_near(block):
-        return send(block, lambda x, c, z, y: (x, c, z, 1 - y))
+        return send(block, lambda x, c, z, y: (x, c ^ (1 - y), z, 1 - y))
+
+    def from_near(block):
+        return send(block, lambda x, c, z, y: (x, c ^ y, z, 1 - y))
 
     def to_cross(block, j):
-        return send(block, lambda x, c, z, y: (x ^ j, c, z, y))
+        return send(block, lambda x, c, z, y: (x ^ j, c ^ y ^ bit(x ^ j, j), z, y))
+
+    def from_cross(block, j):
+        return send(block, lambda x, c, z, y: (x ^ j, c ^ y ^ bit(x, j), z, y))
 
     def attempt(cap, flagged, embeddings, cluster_id, cluster_rank):
         rows = embeddings.shape[0]
         *own, place = dispatch(pieces, low, cap, flagged, embeddings, cluster_id, cluster_rank)
-        own = [own[0]] + [to_plane(own[s], s) for s in range(1, pieces)]
-        carried = []
+        step = steps(pieces)
+        moved = [own[0]] + [None] * (pieces - 1)
+        carried, token, ends = [], None, None
+        for p in range(1, pieces):
+            moved[p] = to_plane(own[p], step[p])
+        earlier = []
         for p in range(pieces):
-            near = to_near(own[p])
-            cross = [to_cross(own[p], j) for j in range(1, chips)]
-            blocks = [own[p], to_twin(own[p]), near, to_twin(near)]
-            blocks += cross + [to_twin(block) for block in cross]
-            carried, ends = stage(p, pieces, cap, flagged, blocks, carried)
-        a = jnp.maximum(ends[0], to_near(ends[1]))
-        back = [a] + [to_plane(a, s) for s in range(1, pieces)]
+            (mine,) = after([moved[p]], earlier)
+            cross = [to_cross(mine, j) for j in range(1, chips)]
+            near = to_near(mine)
+            earlier = cross + [near]
+            blocks = [mine, to_twin(mine)] + cross + [near]
+            carried, token, ends = stage(p, pieces, cap, flagged, blocks, carried)
+        a = jnp.maximum(ends[0], from_near(ends[-1]))
+        for j in range(1, chips):
+            a = jnp.maximum(a, from_cross(ends[j], j))
+        back = [a] + [to_plane(a, s) for s in step[1:]]
         where = jnp.pad(place.reshape(rows // LANES, LANES), ((0, 8 - rows // LANES), (0, 0)))
         result = collect(pieces, cap, where, back)
         return result[: rows // LANES].reshape(rows), a[0, -1]

time: 114 us -> 90.9 us (0.80)
  waiting for transfers between devices: 50.6 us -> 38.5 us
  Pallas kernels: 31.4 us -> 24.5 us
  starting transfers between devices: 27.9 us -> 24.4 us
    ppermute x27 -> x20, waiting for transfers between devices: 50.6 us -> 38.5 us  [send(): return lax.ppermute(block, AXES, route)]
    pallas_call x4, Pallas kernels: 25.6 us -> 18.6 us  [stage(): pl.pallas_call(functools.partial(stage_kernel, p, pieces, groups, cap, fl...]
    ppermute x27 -> x20, starting transfers between devices: 27.9 us -> 24.4 us  [send(): return lax.ppermute(block, AXES, route)]
  transfers between devices with their start and end apart: 27 -> 20, of which waited for: 10 -> 12; matrix products, arithmetic and copies ran while one was open for 1% -> 1% of each run, Pallas kernels for 14% -> 12%
where the time goes in v3:
time: 90.9 us; the launch traced here: 90.7 us
  waiting for transfers between devices  38.5 us (42%)
  Pallas kernels  24.5 us (27%)
  starting transfers between devices  24.4 us (27%)
  local copies, waits for them, and re-layouts  2.39 us (3%)
    ppermute x20, waiting for transfers between devices, send(): return lax.ppermute(block, AXES, route)  38.5 us
    ppermute x20, starting transfers between devices, send(): return lax.ppermute(block, AXES, route)  24.4 us
    pallas_call x4, Pallas kernels, stage(): pl.pallas_call(functools.partial(stage_kernel, p, pieces, groups, cap, fl...  18.6 us
    pallas_call x1, Pallas kernels, dispatch(): pl.pallas_call(functools.partial(dispatch_kernel, pieces, low, cap, flagg...  4.91 us
  transfers between devices with their start and end apart: 20, of which 12 were waited for; matrix products, arithmetic and copies ran while one was open for 1% of the time, Pallas kernels for 12%

profile of v3, /device:TPU:0, one launch (start us, length us, event | category | flops | bytes accessed | tf_op | source)
XLA Modules:
  0.0 90.7 jit_solution(16379677227300421739)
XLA Ops:
  0.0 4.9 %dispatch.3 = (bf16[208,1024]{1,0:T(8,128)(2,1)S(1)}, bf16[208,1024]{1,0:T(8,128)(2,1)S(1)}, bf16[208,1024]{1,0:T(8,128)(2,1)S(1)}, bf16[208,1024]{1,0:T(8,128)(2,1)S(1)}, s32[1,768]{1,0:T(1,128)S(1)}) custom-call(bf16[768,1024]{1,0:T(8,128)(2,1)} %emb.1, s32[6,128]{1,0:T(8,128)} %bitcast.11, s32[6,128]{1,0:T(8,128)} %bitcast.13), custom_call_target="tpu_custom_call" | custom-call | tf_op jit(solution)/shard_map/dispatch/pallas_call | solution.py:119
  4.9 2.4 %collective-permute-start.23 = (bf16[208,1024]{1,0:T(8,128)(2,1)S(1)}, bf16[208,1024]{1,0:T(8,128)(2,1)S(1)}, u32[]{:S(2)}, u32[]{:S(2)}) collective-permute-start(bf16[208,1024]{1,0:T(8,128)(2,1)S(1)} %get-tuple-element.70.refs_0_), channel_id=1, source_target_pairs={{0,24},{1,17},{2,26},{3,19},{4,28},{5,21},{6,30},{7,23},{8,16},{9,... | collective-permute-start | bytes 1277960 | tf_op jit(solution)/shard_map/ppermute | solution.py:295
  7.4 1.2 %collective-permute-start.24 = (bf16[208,1024]{1,0:T(8,128)(2,1)S(1)}, bf16[208,1024]{1,0:T(8,128)(2,1)S(1)}, u32[]{:S(2)}, u32[]{:S(2)}) collective-permute-start(bf16[208,1024]{1,0:T(8,128)(2,1)S(1)} %get-tuple-element.70.refs_0_), channel_id=1, source_target_pairs={{0,9},{1,0},{2,11},{3,2},{4,13},{5,4},{6,15},{7,6},{8,1},{9,8},{10... | collective-permute-start | bytes 1277960 | tf_op jit(solution)/shard_map/ppermute | solution.py:295
  8.6 1.6 %collective-permute-start.22 = (bf16[208,1024]{1,0:T(8,128)(2,1)S(1)}, bf16[208,1024]{1,0:T(8,128)(2,1)S(1)}, u32[]{:S(2)}, u32[]{:S(2)}) collective-permute-start(bf16[208,1024]{1,0:T(8,128)(2,1)S(1)} %get-tuple-element.69), channel_id=1, source_target_pairs={{0,2},{1,3},{2,0},{3,1},{4,6},{5,7},{6,4},{7,5},{8,10},{9,11},{10,... | collective-permute-start | bytes 1277960 | tf_op jit(solution)/shard_map/ppermute | solution.py:295
  10.2 2.5 %collective-permute-start.21 = (bf16[208,1024]{1,0:T(8,128)(2,1)S(1)}, bf16[208,1024]{1,0:T(8,128)(2,1)S(1)}, u32[]{:S(2)}, u32[]{:S(2)}) collective-permute-start(bf16[208,1024]{1,0:T(8,128)(2,1)S(1)} %get-tuple-element.68), channel_id=1, source_target_pairs={{0,6},{1,7},{2,4},{3,5},{4,2},{5,3},{6,0},{7,1},{8,14},{9,15},{10,... | collective-permute-start | bytes 1277960 | tf_op jit(solution)/shard_map/ppermute | solution.py:295
  12.6 5.1 %collective-permute-done.23.refs_1_.refs_2_ = bf16[208,1024]{1,0:T(8,128)(2,1)S(1)} collective-permute-done((bf16[208,1024]{1,0:T(8,128)(2,1)S(1)}, bf16[208,1024]{1,0:T(8,128)(2,1)S(1)}, u32[]{:S(2)}, u32[]{:S(2)}) %collective-permute-start.23) | collective-permute-done | bytes 426016 | tf_op jit(solution)/shard_map/ppermute | solution.py:295
  17.7 2.0 %collective-permute-done.24.refs_2_.refs_3_ = bf16[208,1024]{1,0:T(8,128)(2,1)S(1)} collective-permute-done((bf16[208,1024]{1,0:T(8,128)(2,1)S(1)}, bf16[208,1024]{1,0:T(8,128)(2,1)S(1)}, u32[]{:S(2)}, u32[]{:S(2)}) %collective-permute-start.24) | collective-permute-done | bytes 426016 | tf_op jit(solution)/shard_map/ppermute | solution.py:295
  19.7 1.5 %collective-permute-done.22.refs_0_ = bf16[208,1024]{1,0:T(8,128)(2,1)S(1)} collective-permute-done((bf16[208,1024]{1,0:T(8,128)(2,1)S(1)}, bf16[208,1024]{1,0:T(8,128)(2,1)S(1)}, u32[]{:S(2)}, u32[]{:S(2)}) %collective-permute-start.22) | collective-permute-done | bytes 426016 | tf_op jit(solution)/shard_map/ppermute | solution.py:295
  21.3 2.7 %collective-permute-start.20 = (bf16[208,1024]{1,0:T(8,128)(2,1)S(1)}, bf16[208,1024]{1,0:T(8,128)(2,1)S(1)}, u32[]{:S(2)}, u32[]{:S(2)}) collective-permute-start(bf16[208,1024]{1,0:T(8,128)(2,1)S(1)} %get-tuple-element.67), channel_id=1, source_target_pairs={{0,4},{1,5},{2,6},{3,7},{4,0},{5,1},{6,2},{7,3},{8,12},{9,13},{10,... | collective-permute-start | bytes 1277960 | tf_op jit(solution)/shard_map/ppermute | solution.py:295
  23.9 8.6 %collective-permute-done.21.refs_0_ = bf16[208,1024]{1,0:T(8,128)(2,1)S(1)} collective-permute-done((bf16[208,1024]{1,0:T(8,128)(2,1)S(1)}, bf16[208,1024]{1,0:T(8,128)(2,1)S(1)}, u32[]{:S(2)}, u32[]{:S(2)}) %collective-permute-start.21) | collective-permute-done | bytes 426016 | tf_op jit(solution)/shard_map/ppermute | solution.py:295
  33.4 1.2 %collective-permute-start.28 = (bf16[208,1024]{1,0:T(8,128)(2,1)S(1)}, bf16[208,1024]{1,0:T(8,128)(2,1)S(1)}, u32[]{:S(2)}, u32[]{:S(2)}) collective-permute-start(bf16[208,1024]{1,0:T(8,128)(2,1)S(1)} %after.10.refs_0_), channel_id=1, source_target_pairs={{0,9},{1,0},{2,11},{3,2},{4,13},{5,4},{6,15},{7,6},{8,1},{9,8},{10... | collective-permute-start | bytes 1277960 | tf_op jit(solution)/shard_map/ppermute | solution.py:295
  35.1 15.7 %collective-permute-done.20.refs_0_ = bf16[208,1024]{1,0:T(8,128)(2,1)S(1)} collective-permute-done((bf16[208,1024]{1,0:T(8,128)(2,1)S(1)}, bf16[208,1024]{1,0:T(8,128)(2,1)S(1)}, u32[]{:S(2)}, u32[]{:S(2)}) %collective-permute-start.20) | collective-permute-done | bytes 426016 | tf_op jit(solution)/shard_map/ppermute | solution.py:295
  51.3 2.1 %stage0.3 = (bf16[3376,1024]{1,0:T(8,128)(2,1)S(1)}, f32[3328,128]{1,0:T(8,128)S(1)}, f32[8,2048]{1,0:T(8,128)S(1)}, f32[8,2176]{1,0:T(8,128)S(1)}, f32[1664,128]{1,0:T(8,128)S(1)}, /*index=5*/f32[8,128]{1,0:T(8,128)}) custom-call(bf16[208,1024]{1,0:T(8,128)(2,1)S(1)} %get-tuple-element.70.refs_0_, bf16[208,1024]{1,0:T(8,128)(2,1)S(1)} %collective-permute-done.34.refs_1_, ...), custom_call_target="tpu_custom_call" | custom-call | flops 443023360 | bytes 1703936 | tf_op jit(solution)/shard_map/stage0/pallas_call | solution.py:245
  53.4 3.8 %stage1.3 = (bf16[3376,1024]{1,0:T(8,128)(2,1)S(1)}, f32[3328,128]{1,0:T(8,128)S(1)}, f32[8,2048]{1,0:T(8,128)S(1)}, f32[8,2176]{1,0:T(8,128)S(1)}, f32[1664,128]{1,0:T(8,128)S(1)}, /*index=5*/f32[8,128]{1,0:T(8,128)}) custom-call(bf16[208,1024]{1,0:T(8,128)(2,1)S(1)} %after.9.refs_0_, ...), custom_call_target="tpu_custom_call", output_to_operand_aliasing={{0}: (4, {}), {1}: (5, {}), {2}: (6, {}), {3}: (7, {}), {4}... | custom-call | flops 1329070080 | bytes 1703936 | tf_op jit(solution)/shard_map/stage1/pallas_call | solution.py:245
  57.2 5.3 %stage2.3 = (bf16[3376,1024]{1,0:T(8,128)(2,1)S(1)}, f32[3328,128]{1,0:T(8,128)S(1)}, f32[8,2048]{1,0:T(8,128)S(1)}, f32[8,2176]{1,0:T(8,128)S(1)}, f32[1664,128]{1,0:T(8,128)S(1)}, /*index=5*/f32[8,128]{1,0:T(8,128)}) custom-call(bf16[208,1024]{1,0:T(8,128)(2,1)S(1)} %after.10.refs_0_,, ...), custom_call_target="tpu_custom_call", output_to_operand_aliasing={{0}: (4, {}), {1}: (5, {}), {2}: (6, {}), {3}: (7, {}), {4}... | custom-call | flops 2215116800 | bytes 1703936 | tf_op jit(solution)/shard_map/stage2/pallas_call | solution.py:245
  63.2 7.4 %stage3.3 = (bf16[3376,1024]{1,0:T(8,128)(2,1)S(1)}, f32[3328,128]{1,0:T(8,128)S(1)}, f32[8,2048]{1,0:T(8,128)S(1)}, f32[8,2176]{1,0:T(8,128)S(1)}, f32[1664,128...) custom-call(bf16[208,1024]{1,0:T(8,128)(2,1)S(1)} %after.11.refs_0_,, ...), custom_call_target="tpu_custom_call", output_to_operand_aliasing={{0}: (4, {}), {1}: (5, {}), {2}: (6, {}), {3}: (7, {}), {4}... | custom-call | flops 3101163520 | bytes 1703936 | tf_op jit(solution)/shard_map/stage3/pallas_call | solution.py:245
  70.6 1.5 %collective-permute-start.35 = (f32[8,1152]{1,0:T(8,128)S(1)}, f32[8,1152]{1,0:T(8,128)S(1)}, u32[]{:S(2)}, u32[]{:S(2)}) collective-permute-start(f32[8,1152]{1,0:T(8,128)S(1)} %get-tuple-element.87), channel_id=1, source_target_pairs={{0,1},{1,8},{2,3},{3,10},{4,5},{5,12},{6,7},{7,14},{8,9},{9,0},{10... | collective-permute-start | bytes 110600 | tf_op jit(solution)/shard_map/ppermute | solution.py:295
  72.1 2.0 %collective-permute-start.36 = (f32[8,1152]{1,0:T(8,128)S(1)}, f32[8,1152]{1,0:T(8,128)S(1)}, u32[]{:S(2)}, u32[]{:S(2)}) collective-permute-start(f32[8,1152]{1,0:T(8,128)S(1)} %get-tuple-element.88), channel_id=1, source_target_pairs={{0,16},{1,25},{2,18},{3,27},{4,20},{5,29},{6,22},{7,31},{8,24},{9,... | collective-permute-start | bytes 110600 | tf_op jit(solution)/shard_map/ppermute | solution.py:295
  74.2 1.6 %collective-permute-done.36 = f32[8,1152]{1,0:T(8,128)S(1)} collective-permute-done((f32[8,1152]{1,0:T(8,128)S(1)}, f32[8,1152]{1,0:T(8,128)S(1)}, u32[]{:S(2)}, u32[]{:S(2)}) %collective-permute-start.36) | collective-permute-done | bytes 36896 | tf_op jit(solution)/shard_map/ppermute | solution.py:295
  75.8 3.5 %collective-permute-start.37 = (f32[8,1152]{1,0:T(8,128)S(1)}, f32[8,1152]{1,0:T(8,128)S(1)}, u32[]{:S(2)}, u32[]{:S(2)}) collective-permute-start(f32[8,1152]{1,0:T(8,128)S(1)} %maximum_maximum_fusion.1.refs_0_), channel_id=1, source_target_pairs={{0,2},{1,3},{2,0},{3,1},{4,6},{5,7},{6,4},{7,5},{8,10},{9,11},{10,... | collective-permute-start | bytes 110600 | tf_op jit(solution)/shard_map/ppermute | solution.py:295
  79.3 4.1 %collective-permute-start.38 = (f32[8,1152]{1,0:T(8,128)S(1)}, f32[8,1152]{1,0:T(8,128)S(1)}, u32[]{:S(2)}, u32[]{:S(2)}) collective-permute-start(f32[8,1152]{1,0:T(8,128)S(1)} %maximum_maximum_fusion.1.refs_0_), channel_id=1, source_target_pairs={{0,6},{1,7},{2,4},{3,5},{4,2},{5,3},{6,0},{7,1},{8,14},{9,15},{10,... | collective-permute-start | bytes 110600 | tf_op jit(solution)/shard_map/ppermute | solution.py:295
  86.0 2.3 %collective-permute-done.39.refs_3_ = f32[8,1152]{1,0:T(8,128)S(1)} collective-permute-done((f32[8,1152]{1,0:T(8,128)S(1)}, f32[8,1152]{1,0:T(8,128)S(1)}, u32[]{:S(2)}, u32[]{:S(2)}) %collective-permute-start.39) | collective-permute-done | bytes 36896 | tf_op jit(solution)/shard_map/ppermute | solution.py:295
  88.3 0.6 copy-done.8
  88.9 0.9 %collect.3 = f32[8,128]{1,0:T(8,128)S(1)} custom-call(s32[8,128]{1,0:T(8,128)} %pad.7.place, f32[8,1152]{1,0:T(8,128)} %copy-done.2, f32[8,1152]{1,0:T(8,128)} %copy-done.6, f32[8,1152]{1,0:T(8,128)} %copy-done.7, f32[8,1152]{1,0:T(8,128)} %copy-done.8), custom_call_target="tpu_custom_call" | custom-call | tf_op jit(solution)/shard_map/collect/pallas_call | solution.py:276
  (47 shorter events, 5.4 us)
Async XLA Ops:
  4.9 12.8 %collective-permute-start.23 = (bf16[208,1024]{1,0:T(8,128)(2,1)S(1)}, bf16[208,1024]{1,0:T(8,128)(2,1)S(1)}, u32[]{:S(2)}, u32[]{:S(2)}) collective-permute-start(bf16[208,1024]{1,0:T(8,128)(2,1)S(1)} %get-tuple-element.70.refs_0_), channel_id=1, source_target_pairs={{0,24},{1,17},{2,26},{3,19},{4,28},{5,21},{6,30},{7,23},{8,16},{9,... | collective-permute-start | bytes 1277960 | tf_op jit(solution)/shard_map/ppermute | solution.py:295
  7.4 12.4 %collective-permute-start.24 = (bf16[208,1024]{1,0:T(8,128)(2,1)S(1)}, bf16[208,1024]{1,0:T(8,128)(2,1)S(1)}, u32[]{:S(2)}, u32[]{:S(2)}) collective-permute-start(bf16[208,1024]{1,0:T(8,128)(2,1)S(1)} %get-tuple-element.70.refs_0_), channel_id=1, source_target_pairs={{0,9},{1,0},{2,11},{3,2},{4,13},{5,4},{6,15},{7,6},{8,1},{9,8},{10... | collective-permute-start | bytes 1277960 | tf_op jit(solution)/shard_map/ppermute | solution.py:295
  8.6 12.7 %collective-permute-start.22 = (bf16[208,1024]{1,0:T(8,128)(2,1)S(1)}, bf16[208,1024]{1,0:T(8,128)(2,1)S(1)}, u32[]{:S(2)}, u32[]{:S(2)}) collective-permute-start(bf16[208,1024]{1,0:T(8,128)(2,1)S(1)} %get-tuple-element.69), channel_id=1, source_target_pairs={{0,2},{1,3},{2,0},{3,1},{4,6},{5,7},{6,4},{7,5},{8,10},{9,11},{10,... | collective-permute-start | bytes 1277960 | tf_op jit(solution)/shard_map/ppermute | solution.py:295
  10.2 22.4 %collective-permute-start.21 = (bf16[208,1024]{1,0:T(8,128)(2,1)S(1)}, bf16[208,1024]{1,0:T(8,128)(2,1)S(1)}, u32[]{:S(2)}, u32[]{:S(2)}) collective-permute-start(bf16[208,1024]{1,0:T(8,128)(2,1)S(1)} %get-tuple-element.68), channel_id=1, source_target_pairs={{0,6},{1,7},{2,4},{3,5},{4,2},{5,3},{6,0},{7,1},{8,14},{9,15},{10,... | collective-permute-start | bytes 1277960 | tf_op jit(solution)/shard_map/ppermute | solution.py:295
  21.3 11.8 %collective-permute-start.25 = (bf16[208,1024]{1,0:T(8,128)(2,1)S(1)}, bf16[208,1024]{1,0:T(8,128)(2,1)S(1)}, u32[]{:S(2)}, u32[]{:S(2)}) collective-permute-start(bf16[208,1024]{1,0:T(8,128)(2,1)S(1)} %after.9.refs_0_), channel_id=1, source_target_pairs={{0,24},{1,17},{2,26},{3,19},{4,28},{5,21},{6,30},{7,23},{8,16},{9,... | collective-permute-start | bytes 1277960 | tf_op jit(solution)/shard_map/ppermute | solution.py:295
  21.3 12.0 %collective-permute-start.26 = (bf16[208,1024]{1,0:T(8,128)(2,1)S(1)}, bf16[208,1024]{1,0:T(8,128)(2,1)S(1)}, u32[]{:S(2)}, u32[]{:S(2)}) collective-permute-start(bf16[208,1024]{1,0:T(8,128)(2,1)S(1)} %after.9.refs_0_), channel_id=1, source_target_pairs={{0,9},{1,0},{2,11},{3,2},{4,13},{5,4},{6,15},{7,6},{8,1},{9,8},{10... | collective-permute-start | bytes 1277960 | tf_op jit(solution)/shard_map/ppermute | solution.py:295
  21.3 29.5 %collective-permute-start.20 = (bf16[208,1024]{1,0:T(8,128)(2,1)S(1)}, bf16[208,1024]{1,0:T(8,128)(2,1)S(1)}, u32[]{:S(2)}, u32[]{:S(2)}) collective-permute-start(bf16[208,1024]{1,0:T(8,128)(2,1)S(1)} %get-tuple-element.67), channel_id=1, source_target_pairs={{0,4},{1,5},{2,6},{3,7},{4,0},{5,1},{6,2},{7,3},{8,12},{9,13},{10,... | collective-permute-start | bytes 1277960 | tf_op jit(solution)/shard_map/ppermute | solution.py:295
  33.3 17.5 %collective-permute-start.27 = (bf16[208,1024]{1,0:T(8,128)(2,1)S(1)}, bf16[208,1024]{1,0:T(8,128)(2,1)S(1)}, u32[]{:S(2)}, u32[]{:S(2)}) collective-permute-start(bf16[208,1024]{1,0:T(8,128)(2,1)S(1)} %after.10.refs_0_), channel_id=1, source_target_pairs={{0,24},{1,17},{2,26},{3,19},{4,28},{5,21},{6,30},{7,23},{8,16},{9,... | collective-permute-start | bytes 1277960 | tf_op jit(solution)/shard_map/ppermute | solution.py:295
  33.4 17.5 %collective-permute-start.28 = (bf16[208,1024]{1,0:T(8,128)(2,1)S(1)}, bf16[208,1024]{1,0:T(8,128)(2,1)S(1)}, u32[]{:S(2)}, u32[]{:S(2)}) collective-permute-start(bf16[208,1024]{1,0:T(8,128)(2,1)S(1)} %after.10.refs_0_), channel_id=1, source_target_pairs={{0,9},{1,0},{2,11},{3,2},{4,13},{5,4},{6,15},{7,6},{8,1},{9,8},{10... | collective-permute-start | bytes 1277960 | tf_op jit(solution)/shard_map/ppermute | solution.py:295
  34.6 16.7 %collective-permute-start.34 = (bf16[208,1024]{1,0:T(8,128)(2,1)S(1)}, bf16[208,1024]{1,0:T(8,128)(2,1)S(1)}, u32[]{:S(2)}, u32[]{:S(2)}) collective-permute-start(bf16[208,1024]{1,0:T(8,128)(2,1)S(1)} %get-tuple-element.70.refs_0_), channel_id=1, source_target_pairs={{0,8},{1,9},{2,10},{3,11},{4,12},{5,13},{6,14},{7,15},{8,0},{9,1},... | collective-permute-start | bytes 1277960 | tf_op jit(solution)/shard_map/ppermute | solution.py:295
  35.0 18.5 %collective-permute-start.33 = (bf16[208,1024]{1,0:T(8,128)(2,1)S(1)}, bf16[208,1024]{1,0:T(8,128)(2,1)S(1)}, u32[]{:S(2)}, u32[]{:S(2)}) collective-permute-start(bf16[208,1024]{1,0:T(8,128)(2,1)S(1)} %after.9.refs_0_), channel_id=1, source_target_pairs={{0,8},{1,9},{2,10},{3,11},{4,12},{5,13},{6,14},{7,15},{8,0},{9,1},... | collective-permute-start | bytes 1277960 | tf_op jit(solution)/shard_map/ppermute | solution.py:295
  50.7 6.5 %collective-permute-start.32 = (bf16[208,1024]{1,0:T(8,128)(2,1)S(1)}, bf16[208,1024]{1,0:T(8,128)(2,1)S(1)}, u32[]{:S(2)}, u32[]{:S(2)}) collective-permute-start(bf16[208,1024]{1,0:T(8,128)(2,1)S(1)} %after.10.refs_0_), channel_id=1, source_target_pairs={{0,8},{1,9},{2,10},{3,11},{4,12},{5,13},{6,14},{7,15},{8,0},{9,1},... | collective-permute-start | bytes 1277960 | tf_op jit(solution)/shard_map/ppermute | solution.py:295
  50.9 11.7 %collective-permute-start.29 = (bf16[208,1024]{1,0:T(8,128)(2,1)S(1)}, bf16[208,1024]{1,0:T(8,128)(2,1)S(1)}, u32[]{:S(2)}, u32[]{:S(2)}) collective-permute-start(bf16[208,1024]{1,0:T(8,128)(2,1)S(1)} %after.11.refs_0_), channel_id=1, source_target_pairs={{0,8},{1,9},{2,10},{3,11},{4,12},{5,13},{6,14},{7,15},{8,0},{9,1},... | collective-permute-start | bytes 1277960 | tf_op jit(solution)/shard_map/ppermute | solution.py:295
  51.3 11.9 %collective-permute-start.30 = (bf16[208,1024]{1,0:T(8,128)(2,1)S(1)}, bf16[208,1024]{1,0:T(8,128)(2,1)S(1)}, u32[]{:S(2)}, u32[]{:S(2)}) collective-permute-start(bf16[208,1024]{1,0:T(8,128)(2,1)S(1)} %after.11.refs_0_), channel_id=1, source_target_pairs={{0,24},{1,17},{2,26},{3,19},{4,28},{5,21},{6,30},{7,23},{8,16},{9,... | collective-permute-start | bytes 1277960 | tf_op jit(solution)/shard_map/ppermute | solution.py:295
  51.3 11.9 %collective-permute-start.31 = (bf16[208,1024]{1,0:T(8,128)(2,1)S(1)}, bf16[208,1024]{1,0:T(8,128)(2,1)S(1)}, u32[]{:S(2)}, u32[]{:S(2)}) collective-permute-start(bf16[208,1024]{1,0:T(8,128)(2,1)S(1)} %after.11.refs_0_), channel_id=1, source_target_pairs={{0,9},{1,0},{2,11},{3,2},{4,13},{5,4},{6,15},{7,6},{8,1},{9,8},{10... | collective-permute-start | bytes 1277960 | tf_op jit(solution)/shard_map/ppermute | solution.py:295
  63.2 26.7 %copy-start = (bf16[768,1024]{1,0:T(8,128)(2,1)S(1)}, bf16[768,1024]{1,0:T(8,128)(2,1)}, u32[]{:S(2)}) copy-start(bf16[768,1024]{1,0:T(8,128)(2,1)} %emb.1) | copy-start | bytes 4718596
  63.2 26.7 %copy-start.9 = (s32[768]{0:T(1024)S(1)}, s32[768]{0:T(1024)}, u32[]{:S(2)}) copy-start(s32[768]{0:T(1024)} %param.6) | copy-start | bytes 9220
  63.2 26.7 %copy-start.10 = (s32[768]{0:T(1024)S(1)}, s32[768]{0:T(1024)}, u32[]{:S(2)}) copy-start(s32[768]{0:T(1024)} %param.7) | copy-start | bytes 9220
  70.6 3.6 %collective-permute-start.35 = (f32[8,1152]{1,0:T(8,128)S(1)}, f32[8,1152]{1,0:T(8,128)S(1)}, u32[]{:S(2)}, u32[]{:S(2)}) collective-permute-start(f32[8,1152]{1,0:T(8,128)S(1)} %get-tuple-element.87), channel_id=1, source_target_pairs={{0,1},{1,8},{2,3},{3,10},{4,5},{5,12},{6,7},{7,14},{8,9},{9,0},{10... | collective-permute-start | bytes 110600 | tf_op jit(solution)/shard_map/ppermute | solution.py:295
  72.1 3.7 %collective-permute-start.36 = (f32[8,1152]{1,0:T(8,128)S(1)}, f32[8,1152]{1,0:T(8,128)S(1)}, u32[]{:S(2)}, u32[]{:S(2)}) collective-permute-start(f32[8,1152]{1,0:T(8,128)S(1)} %get-tuple-element.88), channel_id=1, source_target_pairs={{0,16},{1,25},{2,18},{3,27},{4,20},{5,29},{6,22},{7,31},{8,24},{9,... | collective-permute-start | bytes 110600 | tf_op jit(solution)/shard_map/ppermute | solution.py:295
  75.8 12.5 %copy-start.2 = (f32[8,1152]{1,0:T(8,128)}, f32[8,1152]{1,0:T(8,128)S(1)}, u32[]{:S(2)}) copy-start(f32[8,1152]{1,0:T(8,128)S(1)} %maximum_maximum_fusion.1.refs_0_) | copy-start | bytes 110596
  75.8 9.9 %collective-permute-start.37 = (f32[8,1152]{1,0:T(8,128)S(1)}, f32[8,1152]{1,0:T(8,128)S(1)}, u32[]{:S(2)}, u32[]{:S(2)}) collective-permute-start(f32[8,1152]{1,0:T(8,128)S(1)} %maximum_maximum_fusion.1.refs_0_), channel_id=1, source_target_pairs={{0,2},{1,3},{2,0},{3,1},{4,6},{5,7},{6,4},{7,5},{8,10},{9,11},{10,... | collective-permute-start | bytes 110600 | tf_op jit(solution)/shard_map/ppermute | solution.py:295
  79.3 6.7 %collective-permute-start.38 = (f32[8,1152]{1,0:T(8,128)S(1)}, f32[8,1152]{1,0:T(8,128)S(1)}, u32[]{:S(2)}, u32[]{:S(2)}) collective-permute-start(f32[8,1152]{1,0:T(8,128)S(1)} %maximum_maximum_fusion.1.refs_0_), channel_id=1, source_target_pairs={{0,6},{1,7},{2,4},{3,5},{4,2},{5,3},{6,0},{7,1},{8,14},{9,15},{10,... | collective-permute-start | bytes 110600 | tf_op jit(solution)/shard_map/ppermute | solution.py:295
  83.4 4.9 %collective-permute-start.39 = (f32[8,1152]{1,0:T(8,128)S(1)}, f32[8,1152]{1,0:T(8,128)S(1)}, u32[]{:S(2)}, u32[]{:S(2)}) collective-permute-start(f32[8,1152]{1,0:T(8,128)S(1)} %maximum_maximum_fusion.1.refs_0_), channel_id=1, source_target_pairs={{0,4},{1,5},{2,6},{3,7},{4,0},{5,1},{6,2},{7,3},{8,12},{9,13},{10,... | collective-permute-start | bytes 110600 | tf_op jit(solution)/shard_map/ppermute | solution.py:295
  (4 other events, 6.2 us)

commit v4 on v3

v4 whole, which is shorter than its diff:
```python
import functools

import jax
import jax.numpy as jnp
from jax import lax
from jax.experimental import pallas as pl
from jax.experimental.pallas import tpu as pltpu
from jax.sharding import PartitionSpec as P

AXES = ("grp", "sub")
LANES = 128
RADIX = 128
EMPTY = 255.0
VMEM = 16 * 1024 * 1024


def ceil_to(value, unit):
    return -(-value // unit) * unit


def nt_dot(left, right):
    return lax.dot_general(
        left, right, (((1,), (1,)), ((), ())), preferred_element_type=jnp.float32
    )


def steps(pieces):
    return sorted(range(pieces), key=lambda s: (min(s, pieces - s), s))


def in_place(array):
    return pltpu.with_memory_space_constraint(array, pltpu.VMEM)


def after(blocks, earlier):
    if not earlier:
        return blocks
    held = [in_place(x) for x in blocks]
    return list(pl.pallas_call(
        lambda *refs: None,
        out_shape=[pltpu.VMEM(x.shape, x.dtype) for x in blocks],
        in_specs=[pl.BlockSpec(memory_space=pltpu.VMEM)] * len(blocks)
        + [pl.BlockSpec(memory_space=pl.ANY)] * len(earlier),
        out_specs=[pl.BlockSpec(memory_space=pltpu.VMEM)] * len(blocks),
        input_output_aliases={i: i for i in range(len(blocks))},
        compiler_params=pltpu.CompilerParams(vmem_limit_bytes=VMEM),
        name="after",
    )(*held, *earlier))


def sizes(pieces, cap):
    return [cap] * pieces


def starts_of(counts):
    return [sum(counts[:i]) for i in range(len(counts))]


def flat(ref):
    return jnp.concatenate([ref[b : b + 1, :] for b in range(ref.shape[0])], axis=1)


def fill(first, caps, flagged, outs, unit, sorting, pick):
    rows, width = unit.shape
    target = sorting[0:1, :].astype(jnp.int32)
    digits = jnp.concatenate([sorting[...], jnp.zeros((8, rows), jnp.float32)], axis=0)
    digits = digits.astype(jnp.bfloat16)
    notes = []
    starts = starts_of(caps)
    for i, cap in enumerate(caps):
        lanes_per = ceil_to(cap, LANES)
        slots = lax.broadcasted_iota(jnp.int32, (lanes_per, rows), 0) + (first + i) * 1024
        found = jnp.where(slots == target, 1.0, 0.0).astype(jnp.bfloat16)
        pick[starts[i] : starts[i] + cap, :] = found[:cap]
        ranks = nt_dot(digits, found)
        parts = [jnp.where(ranks[3:4, :] > 0.5, ranks[1:2, :], EMPTY), ranks[2:3, :]]
        if flagged:
            parts.append(jnp.broadcast_to(sorting[4:5, :LANES], (1, LANES)))
        used = 2 * lanes_per + (LANES if flagged else 0)
        if used < width:
            parts.append(jnp.zeros((1, width - used), jnp.float32))
        notes.append(jnp.concatenate(parts, axis=1))
    last = lax.broadcasted_iota(jnp.int32, (16, 1), 0) == 15
    for at in range(0, width, 256):
        lanes = slice(at, at + 256)
        moved = jnp.dot(pick[...], unit[:, lanes], preferred_element_type=jnp.float32)
        for i, (cap, out) in enumerate(zip(caps, outs)):
            part = moved[starts[i] : starts[i] + cap]
            out[: cap - 16, lanes] = part[: cap - 16].astype(jnp.bfloat16)
            end = jnp.where(last, notes[i][:, lanes], part[cap - 16 :])
            out[cap - 16 :, lanes] = end.astype(jnp.bfloat16)


def sort_kernel(pieces, low, caps, flagged, emb, cid, rank, *refs):
    out, unit, sorting, place, held, pick, slot_ref, sem = refs
    rows, width = unit.shape
    parts = 4
    share = rows // parts
    copies = []
    for i in range(parts):
        at = pl.ds(i * share, share)
        copy = pltpu.make_async_copy(emb.at[at, :], held.at[at, :], sem.at[i])
        copy.start()
        copies.append(copy)

    plane = lax.axis_index("sub") // low
    step = flat(cid) - plane
    step = jnp.where(step < 0, step + pieces, step)
    piece = jnp.zeros(step.shape, jnp.int32)
    for p, s in enumerate(steps(pieces)):
        piece = jnp.where(step == s, p, piece)
    which = lax.broadcasted_iota(jnp.int32, (16, LANES), 0)
    upper = (
        lax.broadcasted_iota(jnp.int32, (LANES, LANES), 0)
        < lax.broadcasted_iota(jnp.int32, (LANES, LANES), 1)
    ).astype(jnp.bfloat16)
    before = jnp.zeros((16, 1), jnp.float32)
    for b in range(rows // LANES):
        lanes = slice(b * LANES, (b + 1) * LANES)
        member = piece[:, lanes] == which
        ones = member.astype(jnp.float32)
        prefix = jnp.dot(ones.astype(jnp.bfloat16), upper, preferred_element_type=jnp.float32)
        slot = jnp.sum(jnp.where(member, prefix + before, 0.0), axis=0, keepdims=True)
        slot_ref[:, lanes] = slot.astype(jnp.int32)
        before = before + jnp.sum(ones, axis=1, keepdims=True)
    slot = slot_ref[...]
    lane_starts = starts_of([ceil_to(c, LANES) for c in caps])
    spot = slot
    for p in range(1, len(caps)):
        spot = spot + jnp.where(piece == p, lane_starts[p], 0)
    place[...] = jnp.zeros(place.shape, jnp.int32)
    for b in range(rows // LANES):
        place[b : b + 1, :] = spot[:, b * LANES : (b + 1) * LANES]
    full = (jnp.max(before, axis=0, keepdims=True) > caps[0] - 1).astype(jnp.float32)
    r = flat(rank)
    sorting[0:1, :] = (piece * 1024 + slot).astype(jnp.float32)
    sorting[1:2, :] = (r // RADIX).astype(jnp.float32)
    sorting[2:3, :] = (r % RADIX).astype(jnp.float32)
    sorting[3:4, :] = jnp.ones((1, rows), jnp.float32)
    sorting[4:5, :] = jnp.broadcast_to(full, (1, rows))
    sorting[5:8, :] = jnp.zeros((3, rows), jnp.float32)

    for i in range(parts):
        copies[i].wait()

        @pl.loop(i * share // 64, (i + 1) * share // 64)
        def _(j):
            at = pl.ds(pl.multiple_of(j * 64, 64), 64)
            wide = held[at, :].astype(jnp.float32)
            scale = lax.rsqrt(jnp.sum(wide * wide, axis=1, keepdims=True) + 1e-06)
            unit[at, :] = (wide * scale).astype(jnp.bfloat16)

    fill(1, caps[1:2], flagged, [out], unit, sorting, pick)


def fill_kernel(first, caps, flagged, unit, sorting, *refs):
    fill(first, caps, flagged, refs[:-1], unit, sorting, refs[-1])


def dispatch(pieces, low, caps, flagged, emb, cid, rank):
    rows, width = emb.shape
    bf16 = jnp.bfloat16
    in_vmem = pl.BlockSpec(memory_space=pltpu.VMEM)
    one, unit, sorting, place = pl.pallas_call(
        functools.partial(sort_kernel, pieces, low, caps, flagged),
        out_shape=[
            pltpu.VMEM((caps[1], width), bf16),
            pltpu.VMEM((rows, width), bf16),
            pltpu.VMEM((8, rows), jnp.float32),
            pltpu.VMEM((8, LANES), jnp.int32),
        ],
        in_specs=[pl.BlockSpec(memory_space=pl.ANY), in_vmem, in_vmem],
        out_specs=[in_vmem] * 4,
        scratch_shapes=[
            pltpu.VMEM((rows, width), bf16),
            pltpu.VMEM((caps[1], rows), bf16),
            pltpu.VMEM((1, rows), jnp.int32),
            pltpu.SemaphoreType.DMA((4,)),
        ],
        compiler_params=pltpu.CompilerParams(vmem_limit_bytes=VMEM),
        name="sort",
    )(emb, cid.reshape(rows // LANES, LANES), rank.reshape(rows // LANES, LANES))

    def more(first, stop):
        return list(
            pl.pallas_call(
                functools.partial(fill_kernel, first, caps[first:stop], flagged),
                out_shape=[pltpu.VMEM((cap, width), bf16) for cap in caps[first:stop]],
                in_specs=[in_vmem, in_vmem],
                out_specs=[in_vmem] * (stop - first),
                scratch_shapes=[pltpu.VMEM((sum(caps[first:stop]), rows), bf16)],
                compiler_params=pltpu.CompilerParams(vmem_limit_bytes=VMEM),
                name="fill" + str(first),
            )(in_place(unit), in_place(sorting))
        )

    return more(0, 1) + [one] + more(2, len(caps)), place


def stage_kernel(p, part, caps, groups, flagged, *refs):
    new = {"all": range(groups), "home": range(2), "away": range(2, groups)}[part]
    blocks, refs = refs[: len(new)], refs[len(new) :]
    if p or part == "away":
        refs = refs[3:]
    store, limits, best, token, refs = *refs[:4], refs[4:]
    *ends, keys, cols, sem = refs
    token[...] = jnp.zeros(token.shape, jnp.float32)
    cap = caps[p]
    mine, near = 1, groups - 1
    lanes = [ceil_to(c, LANES) for c in caps]
    base = groups * starts_of(caps)[p]
    lane_base = [groups * s for s in starts_of(lanes)]
    wide = lanes[p]

    copies = []
    for g, block in zip(new, blocks):
        copy = pltpu.make_async_copy(block, store.at[pl.ds(base + g * cap, cap), :], sem.at[g])
        copy.start()
        copies.append(copy)

    lane = lax.broadcasted_iota(jnp.int32, (1, wide), 1)
    square = lax.broadcasted_iota(jnp.int32, (cap, wide), 0) == lax.broadcasted_iota(
        jnp.int32, (cap, wide), 1
    )
    flag = jnp.zeros((1, LANES), jnp.float32)
    if p == 0:
        best[...] = jnp.full(best.shape, -1.0, jnp.float32)
    cols[...] = jnp.full(cols.shape, -1.0, jnp.float32)
    for g, block in zip(new, blocks):
        note = block[cap - 16 :, :].astype(jnp.float32)[15:16, :]
        ranks = note[:, :wide] * RADIX + note[:, wide : 2 * wide]
        ranks = jnp.where(lane < cap - 1, ranks, EMPTY * RADIX)
        if flagged:
            flag = jnp.maximum(flag, note[:, 2 * wide : 2 * wide + LANES])
        at = lane_base[p] + g * wide
        limits[:, at : at + wide] = jnp.broadcast_to(ranks, (8, wide))
        column = jnp.sum(jnp.where(square, ranks, 0.0), axis=1, keepdims=True)
        keys[g * cap : (g + 1) * cap, :] = jnp.broadcast_to(column, (cap, LANES))
    if flagged:
        at = best.shape[1] - LANES
        best[:, at:] = jnp.maximum(best[:, at:], jnp.broadcast_to(flag, (8, LANES)))
    for copy in copies:
        copy.wait()

    def product(first, at, count, g, runs):
        if not runs:
            return
        query = store[pl.ds(first, count), :]
        limit = limits[0:1, pl.ds(at, count)]
        top = best[:, pl.ds(at, count)]
        for start, size, low, high in runs:
            start, size, low, high = start * cap, size * cap, low * cap, high * cap
            sims = nt_dot(store[base + start : base + start + size, :], query)
            kr = jnp.concatenate([keys[start : start + size, :]] * (count // LANES), axis=1)
            earlier = kr < limit
            if g:
                ahead = jnp.where(earlier, sims, -1.0)
                top = jnp.maximum(top, jnp.max(ahead.reshape(size // 8, 8, count), axis=0))
            if low < high:
                behind = jnp.where(earlier, -1.0, sims)[low - start : high - start]
                fold = cols[low:high, :]
                for k in range(0, count, LANES):
                    fold = jnp.maximum(fold, behind[:, k : k + LANES])
                cols[low:high, :] = fold
        if g:
            best[:, pl.ds(at, count)] = top

    def partners(g, alone):
        just_mine = [] if alone else [(mine, 1, mine, 2)]
        if part == "home":
            if g == mine:
                return [(0, 2, 1, 1 if alone else 2)]
            return just_mine
        if part == "away":
            if g == mine:
                return [(2, groups - 2, 2, groups)]
            if g == near:
                return [(2, near - 2, 2, near)]
            return [] if alone or g == 0 else [(near, 1, near, groups)]
        if g == mine:
            return [(0, near, 2, near)] if alone else [(0, groups, 1, groups)]
        if g == near:
            return [(mine, near - 1, mine, near)]
        if alone or g == 0:
            return just_mine
        return [(mine, 1, mine, 2), (near, 1, near, groups)]

    if p:

        @pl.loop(0, p)
        def _(i):
            for g in range(groups):
                at = (i * groups + g) * wide
                first = (i * groups + g) * cap
                product(
                    pl.multiple_of(first, 16), pl.multiple_of(at, LANES), wide, g, partners(g, False)
                )

    for g in range(groups):
        product(base + g * cap, lane_base[p] + g * wide, wide, g, partners(g, True))

    for g in new:
        if g:
            at = lane_base[p] + g * wide
            column = jnp.max(cols[g * cap : (g + 1) * cap, :], axis=1, keepdims=True)
            turned = jnp.max(jnp.where(square, column, -1.0), axis=0, keepdims=True)
            best[:, at : at + wide] = jnp.maximum(best[:, at : at + wide], turned)

    for g, out in enumerate(ends, start=1):
        for q, start in enumerate(starts_of(lanes)):
            at = lane_base[q] + g * lanes[q]
            row = jnp.max(best[:, at : at + lanes[q]], axis=0, keepdims=True)
            out[:, start : start + lanes[q]] = row
        out[:, sum(lanes) :] = best[0:1, best.shape[1] - LANES :]


def stage(p, part, caps, groups, flagged, blocks, carried):
    width = blocks[0].shape[1]
    lanes = sum(ceil_to(c, LANES) for c in caps)
    f32 = jnp.float32
    in_vmem = pl.BlockSpec(memory_space=pltpu.VMEM)
    kept = [
        pltpu.VMEM((groups * sum(caps) + LANES, width), jnp.bfloat16),
        pltpu.VMEM((8, groups * lanes), f32),
        pltpu.VMEM((8, groups * lanes + LANES), f32),
        jax.ShapeDtypeStruct((8, LANES), f32),
    ]
    ends = [jax.ShapeDtypeStruct((1, lanes + LANES), f32)] * (groups - 1)
    if p < len(caps) - 1 or part == "home":
        ends = []
    got = pl.pallas_call(
        functools.partial(stage_kernel, p, part, caps, groups, flagged),
        out_shape=kept + ends,
        in_specs=[in_vmem] * (len(blocks) + len(carried)),
        out_specs=[in_vmem] * (4 + len(ends)),
        scratch_shapes=[
            pltpu.VMEM((groups * caps[p], LANES), f32),
            pltpu.VMEM((groups * caps[p], LANES), f32),
            pltpu.SemaphoreType.DMA((groups,)),
        ],
        input_output_aliases={len(blocks) + i: i for i in range(len(carried))},
        cost_estimate=pl.CostEstimate(flops=0, bytes_accessed=0, transcendentals=0),
        compiler_params=pltpu.CompilerParams(vmem_limit_bytes=VMEM),
        name="stage" + str(p) + part,
    )(*[in_place(x) for x in blocks], *[in_place(x) for x in carried])
    return got[:3], got[3], got[4:]


def collect_kernel(lanes, shifts, low, place, *refs):
    rows, out = refs[:-1], refs[-1]
    plane = lax.axis_index("sub") // low
    count = len(rows)
    where = place[...]
    result = jnp.zeros((8, LANES), jnp.float32)
    for q, start in enumerate(starts_of(lanes)):
        apart = plane ^ ((plane + shifts[q]) % count)
        for first in range(start, start + lanes[q], LANES):
            back = rows[0][:, first : first + LANES]
            for s in range(1, count):
                back = jnp.where(apart == s, rows[s][:, first : first + LANES], back)
            back = jnp.broadcast_to(back, (8, LANES))
            inside = where - first
            hit = (inside >= 0) & (inside < LANES)
            taken = jnp.take_along_axis(back, jnp.where(hit, inside, 0), axis=1)
            result = jnp.where(hit, taken, result)
    out[...] = result


def collect(caps, shifts, low, place, rows):
    lanes = [ceil_to(c, LANES) for c in caps]
    return pl.pallas_call(
        functools.partial(collect_kernel, lanes, shifts, low),
        out_shape=jax.ShapeDtypeStruct((8, LANES), jnp.float32),
        in_specs=[pl.BlockSpec(memory_space=pltpu.VMEM)] * (1 + len(rows)),
        name="collect",
    )(*[in_place(x) for x in [place] + rows])


def solution(mesh):
    ngrp, nsub = mesh.shape["grp"], mesh.shape["sub"]
    low = nsub // ngrp
    pieces = ngrp
    chips = ngrp // 2

    def send(block, target):
        route = []
        for g in range(ngrp):
            for s in range(nsub):
                chip, core, plane, small = target(g // 2, g % 2, s // low, s % low)
                route.append((g * nsub + s, (chip * 2 + core) * nsub + plane * low + small))
        return lax.ppermute(block, AXES, route)

    def to_plane(block, s):
        return send(block, lambda x, c, z, y: (x, c, (z + s) % pieces, y))

    def across(block, s):
        return send(block, lambda x, c, z, y: (x, c, z ^ s, y))

    def to_twin(block):
        return send(block, lambda x, c, z, y: (x, 1 - c, z, y))

    def bit(x, j):
        return (x // (j & -j)) % 2

    def to_near(block):
        return send(block, lambda x, c, z, y: (x, c ^ (1 - y), z, 1 - y))

    def from_near(block):
        return send(block, lambda x, c, z, y: (x, c ^ y, z, 1 - y))

    def to_cross(block, j):
        return send(block, lambda x, c, z, y: (x ^ j, c ^ y ^ bit(x ^ j, j), z, y))

    def from_cross(block, j):
        return send(block, lambda x, c, z, y: (x ^ j, c ^ y ^ bit(x, j), z, y))

    def attempt(cap, flagged, embeddings, cluster_id, cluster_rank):
        rows = embeddings.shape[0]
        caps = sizes(pieces, cap)
        count = len(caps)
        step = steps(pieces)
        own, place = dispatch(pieces, low, caps, flagged, embeddings, cluster_id, cluster_rank)
        moved = [own[0]] + [None] * (count - 1)

        def leave(q, earlier):
            moved[q] = to_plane(after([own[q]], earlier)[0], step[q])

        leave(1, [])
        links, carried, tokens = [], [], []
        for p in range(count):
            earlier = links[p - 1] if p else []
            if p > 1:
                earlier = earlier + [tokens[p - 1 - 1]]
            (mine,) = after([moved[p]], earlier)
            twin = to_twin(mine)
            if p == 0:
                (mine,) = after([mine], [twin])
            cross = [to_cross(mine, j) for j in range(1, chips)]
            near = to_near(mine)
            links.append(cross + [near, twin])
            if p == 0:
                for q in range(2, pieces):
                    leave(q, [twin] if q == 2 else [])
            groups = 3 + len(cross)
            home, away = [twin, mine], cross + [near]
            if p < count - 1:
                carried, token, ends = stage(p, "all", caps, groups, flagged, home + away, carried)
            else:
                carried, token, ends = stage(p, "home", caps, groups, flagged, home, carried)
                carried, token, ends = stage(p, "away", caps, groups, flagged, away, carried)
            tokens.append(token)
        a = jnp.maximum(ends[0], from_near(ends[-1]))
        for j in range(1, chips):
            a = jnp.maximum(a, from_cross(ends[j], j))
        back = [a] + [across(a, s) for s in range(1, pieces)]
        result = collect(caps, step, low, place, back)
        return result[: rows // LANES].reshape(rows), a[0, -1]

    def body(embeddings, cluster_id, cluster_rank):
        share = embeddings.shape[0] // ngrp
        usual = ceil_to(share + 1, 16)
        most = ceil_to(2 * share + 1, 16)
        result, over = attempt(usual, True, embeddings, cluster_id, cluster_rank)

        def again():
            return attempt(most, False, embeddings, cluster_id, cluster_rank)[0]

        return lax.cond(over > 0.5, again, lambda: result)

    placed = (P(AXES, None), P(AXES), P(AXES))
    return jax.shard_map(body, mesh=mesh, in_specs=placed, out_specs=P(AXES), check_vma=False)
```

time: 90.9 us -> 83 us (0.913)
  waiting for transfers between devices: 38.5 us -> 27.5 us
  starting transfers between devices: 24.4 us -> 30.6 us
  Pallas kernels: 24.5 us -> 22.3 us
  local copies, waits for them, and re-layouts: 2.39 us -> 1.19 us
    ppermute x20, waiting for transfers between devices: 38.5 us -> 27.5 us  [send(): return lax.ppermute(block, AXES, route)]
    ppermute x20, starting transfers between devices: 24.4 us -> 30.6 us  [send(): return lax.ppermute(block, AXES, route)]
    pallas_call x6 -> x9, Pallas kernels: 24.5 us -> 22.3 us  [the longest x5 16.8 us: stage(): pl.pallas_call(functools.partial(stage_kernel, p, part, caps, groups, fla...]
  transfers between devices with their start and end apart: 20 -> 20, of which waited for: 12 -> 7; matrix products, arithmetic and copies ran while one was open for 1% -> 1% of each run, Pallas kernels for 12% -> 18%
where the time goes in v4:
time: 83 us; the launch traced here: 82.7 us
  starting transfers between devices  30.6 us (37%)
  waiting for transfers between devices  27.5 us (33%)
  Pallas kernels  22.3 us (27%)
  local copies, waits for them, and re-layouts  1.19 us (1%)
  between operations  0.87 us (1%)
    ppermute x20, starting transfers between devices, send(): return lax.ppermute(block, AXES, route)  30.6 us
    ppermute x20, waiting for transfers between devices, send(): return lax.ppermute(block, AXES, route)  27.5 us
    pallas_call x5, Pallas kernels, stage(): pl.pallas_call(functools.partial(stage_kernel, p, part, caps, groups, fla...  16.8 us
    pallas_call x1, Pallas kernels, dispatch(): pl.pallas_call(functools.partial(sort_kernel, pieces, low, caps, flagged)...  3.72 us
  transfers between devices with their start and end apart: 20, of which 7 were waited for; matrix products, arithmetic and copies ran while one was open for 1% of the time, Pallas kernels for 18%

profile of v4, /device:TPU:0, one launch (start us, length us, event | category | flops | bytes accessed | tf_op | source)
XLA Modules:
  0.0 82.7 jit_solution(6967032550551628743)
XLA Ops:
  0.0 3.7 %sort.3 = (bf16[208,1024]{1,0:T(8,128)(2,1)S(1)}, bf16[768,1024]{1,0:T(8,128)(2,1)S(1)}, f32[8,768]{1,0:T(8,128)S(1)}, s32[8,128]{1,0:T(8,128)S(1)}) custom-call(bf16[768,1024]{1,0:T(8,128)(2,1)} %emb.1, s32[6,128]{1,0:T(8,128)} %bitcast.9, s32[6,128]{1,0:T(8,128)} %bitcast.11), custom_call_target="tpu_custom_call" | custom-call | tf_op jit(solution)/shard_map/sort/pallas_call | solution.py:164
  4.8 2.6 %collective-permute-start.23 = (bf16[208,1024]{1,0:T(8,128)(2,1)S(1)}, bf16[208,1024]{1,0:T(8,128)(2,1)S(1)}, u32[]{:S(2)}, u32[]{:S(2)}) collective-permute-start(bf16[208,1024]{1,0:T(8,128)(2,1)S(1)} %get-tuple-element.71), channel_id=1, source_target_pairs={{0,2},{1,3},{2,4},{3,5},{4,6},{5,7},{6,0},{7,1},{8,10},{9,11},{10,... | collective-permute-start | bytes 1277960 | tf_op jit(solution)/shard_map/ppermute | solution.py:391
  7.5 1.4 %collective-permute-start.25 = (bf16[208,1024]{1,0:T(8,128)(2,1)S(1)}, bf16[208,1024]{1,0:T(8,128)(2,1)S(1)}, u32[]{:S(2)}, u32[]{:S(2)}) collective-permute-start(bf16[208,1024]{1,0:T(8,128)(2,1)S(1)} %after.16.refs_1_), channel_id=1, source_target_pairs={{0,9},{1,0},{2,11},{3,2},{4,13},{5,4},{6,15},{7,6},{8,1},{9,8},{10... | collective-permute-start | bytes 1277960 | tf_op jit(solution)/shard_map/ppermute | solution.py:391
  8.9 1.5 %collective-permute-start.24 = (bf16[208,1024]{1,0:T(8,128)(2,1)S(1)}, bf16[208,1024]{1,0:T(8,128)(2,1)S(1)}, u32[]{:S(2)}, u32[]{:S(2)}) collective-permute-start(bf16[208,1024]{1,0:T(8,128)(2,1)S(1)} %after.16.refs_1_), channel_id=1, source_target_pairs={{0,24},{1,17},{2,26},{3,19},{4,28},{5,21},{6,30},{7,23},{8,16},{9,... | collective-permute-start | bytes 1277960 | tf_op jit(solution)/shard_map/ppermute | solution.py:391
  10.3 1.0 %fill2.3 = (bf16[208,1024]{1,0:T(8,128)(2,1)S(1)}, bf16[208,1024]{1,0:T(8,128)(2,1)S(1)}) custom-call(bf16[768,1024]{1,0:T(8,128)(2,1)S(1)} %get-tuple-element.67.unit, f32[8,768]{1,0:T(8,128)S(1)} %get-tuple-element.68.sorting), custom_call_target="tpu_custom_call" | custom-call | tf_op jit(solution)/shard_map/fill2/pallas_call | solution.py:186
  11.4 3.7 %collective-permute-start.22 = (bf16[208,1024]{1,0:T(8,128)(2,1)S(1)}, bf16[208,1024]{1,0:T(8,128)(2,1)S(1)}, u32[]{:S(2)}, u32[]{:S(2)}) collective-permute-start(bf16[208,1024]{1,0:T(8,128)(2,1)S(1)} %after.15), channel_id=1, source_target_pairs={{0,6},{1,7},{2,0},{3,1},{4,2},{5,3},{6,4},{7,5},{8,14},{9,15},{10,... | collective-permute-start | bytes 1277960 | tf_op jit(solution)/shard_map/ppermute | solution.py:391
  15.0 5.2 %collective-permute-done.23.refs_0_ = bf16[208,1024]{1,0:T(8,128)(2,1)S(1)} collective-permute-done((bf16[208,1024]{1,0:T(8,128)(2,1)S(1)}, bf16[208,1024]{1,0:T(8,128)(2,1)S(1)}, u32[]{:S(2)}, u32[]{:S(2)}) %collective-permute-start.23) | collective-permute-done | bytes 426016 | tf_op jit(solution)/shard_map/ppermute | solution.py:391
  20.2 0.7 collective-permute-done.24.refs_1_.refs_2_
  21.0 1.1 %collective-permute-start.27 = (bf16[208,1024]{1,0:T(8,128)(2,1)S(1)}, bf16[208,1024]{1,0:T(8,128)(2,1)S(1)}, u32[]{:S(2)}, u32[]{:S(2)}) collective-permute-start(bf16[208,1024]{1,0:T(8,128)(2,1)S(1)} %after.17.refs_1_), channel_id=1, source_target_pairs={{0,9},{1,0},{2,11},{3,2},{4,13},{5,4},{6,15},{7,6},{8,1},{9,8},{10... | collective-permute-start | bytes 1277960 | tf_op jit(solution)/shard_map/ppermute | solution.py:391
  22.1 1.2 %collective-permute-start.26 = (bf16[208,1024]{1,0:T(8,128)(2,1)S(1)}, bf16[208,1024]{1,0:T(8,128)(2,1)S(1)}, u32[]{:S(2)}, u32[]{:S(2)}) collective-permute-start(bf16[208,1024]{1,0:T(8,128)(2,1)S(1)} %after.17.refs_1_), channel_id=1, source_target_pairs={{0,24},{1,17},{2,26},{3,19},{4,28},{5,21},{6,30},{7,23},{8,16},{9,... | collective-permute-start | bytes 1277960 | tf_op jit(solution)/shard_map/ppermute | solution.py:391
  23.2 9.4 %collective-permute-start.20 = (bf16[208,1024]{1,0:T(8,128)(2,1)S(1)}, bf16[208,1024]{1,0:T(8,128)(2,1)S(1)}, u32[]{:S(2)}, u32[]{:S(2)}) collective-permute-start(bf16[208,1024]{1,0:T(8,128)(2,1)S(1)} %get-tuple-element.69), channel_id=1, source_target_pairs={{0,4},{1,5},{2,6},{3,7},{4,0},{5,1},{6,2},{7,3},{8,12},{9,13},{10,... | collective-permute-start | bytes 1277960 | tf_op jit(solution)/shard_map/ppermute | solution.py:391
  32.7 2.0 %stage0all.3 = (bf16[3456,1024]{1,0:T(8,128)(2,1)S(1)}, f32[8,4096]{1,0:T(8,128)S(1)}, f32[8,4224]{1,0:T(8,128)S(1)}, f32[8,128]{1,0:T(8,128)S(1)}) custom-call(bf16[208,1024]{1,0:T(8,128)(2,1)S(1)} %collective-permute-done.21.refs_1_.refs_3_.refs_0_, bf16[208,1024]{1,0:T(8,128)(2,1)S(1)} %after.16.refs_1_, ...), custom_call_target="tpu_custom_call" | custom-call | tf_op jit(solution)/shard_map/stage0all/pallas_call | solution.py:331
  34.9 0.7 collective-permute-start.30
  35.8 3.1 %stage1all.3 = (bf16[3456,1024]{1,0:T(8,128)(2,1)S(1)}, f32[8,4096]{1,0:T(8,128)S(1)}, f32[8,4224]{1,0:T(8,128)S(1)}, f32[8,128]{1,0:T(8,128)S(1)}) custom-call(bf16[208,1024]{1,0:T(8,128)(2,1)S(1)} %collective-permute-done.28.refs_3_.refs_0_, bf16[208,1024]{1,0:T(8,128)(2,1)S(1)} %after.17.refs_1_, ...), custom_call_target="tpu_custom_call", output_to_operand_aliasing={{0}: (4, {}), {1}: (5, {}), {2}: (6, {})} | custom-call | tf_op jit(solution)/shard_map/stage1all/pallas_call | solution.py:331
  38.9 13.3 %collective-permute-done.20.refs_0_ = bf16[208,1024]{1,0:T(8,128)(2,1)S(1)} collective-permute-done((bf16[208,1024]{1,0:T(8,128)(2,1)S(1)}, bf16[208,1024]{1,0:T(8,128)(2,1)S(1)}, u32[]{:S(2)}, u32[]{:S(2)}) %collective-permute-start.20) | collective-permute-done | bytes 426016 | tf_op jit(solution)/shard_map/ppermute | solution.py:391
  53.1 4.7 %stage2all.3 = (bf16[3456,1024]{1,0:T(8,128)(2,1)S(1)}, f32[8,4096]{1,0:T(8,128)S(1)}, f32[8,4224]{1,0:T(8,128)S(1)}, f32[8,128]{1,0:T(8,128)}) custom-call(bf16[208,1024]{1,0:T(8,128)(2,1)S(1)} %collective-permute-done.31.refs_3_.refs_0_, bf16[208,1024]{1,0:T(8,128)(2,1)S(1)} %after.18.refs_1_, ...), custom_call_target="tpu_custom_call", output_to_operand_aliasing={{0}: (4, {}), {1}: (5, {}), {2}: (6, {})} | custom-call | tf_op jit(solution)/shard_map/stage2all/pallas_call | solution.py:331
  57.8 3.6 %stage3home.3 = (bf16[3456,1024]{1,0:T(8,128)(2,1)S(1)}, f32[8,4096]{1,0:T(8,128)S(1)}, f32[8,4224]{1,0:T(8,128)S(1)}, f32[8,128]{1,0:T(8,128)}) custom-call(bf16[208,1024]{1,0:T(8,128)(2,1)S(1)} %collective-permute-done.34.refs_0_, bf16[208,1024]{1,0:T(8,128)(2,1)S(1)} %after.19.refs_1_, ...), custom_call_target="tpu_custom_call", output_to_operand_aliasing={{0}: (2, {}), {1}: (3, {}), {2}: (4, {})} | custom-call | tf_op jit(solution)/shard_map/stage3home/pallas_call | solution.py:331
  61.5 3.1 %collective-permute-done.33.refs_1_ = bf16[208,1024]{1,0:T(8,128)(2,1)S(1)} collective-permute-done((bf16[208,1024]{1,0:T(8,128)(2,1)S(1)}, bf16[208,1024]{1,0:T(8,128)(2,1)S(1)}, u32[]{:S(2)}, u32[]{:S(2)}) %collective-permute-start.33) | collective-permute-done | bytes 426016 | tf_op jit(solution)/shard_map/ppermute | solution.py:391
  64.5 3.4 %stage3away.3 = (bf16[3456,1024]{1,0:T(8,128)(2,1)S(1)}, f32[8,4096]{1,0:T(8,128)S(1)}, f32[8,4224]{1,0:T(8,128)S(1)}, f32[8,128]{1,0:T(8,128)}, f32[1,1152]{1,0...) custom-call(bf16[208,1024]{1,0:T(8,128)(2,1)S(1)} %collective-permut, ...), custom_call_target="tpu_custom_call", output_to_operand_aliasing={{0}: (2, {}), {1}: (3, {}), {2}: (4, {})} | custom-call | tf_op jit(solution)/shard_map/stage3away/pallas_call | solution.py:331
  67.9 1.7 %collective-permute-start.35 = (f32[1,1152]{1,0:T(1,128)S(1)}, f32[1,1152]{1,0:T(1,128)S(1)}, u32[]{:S(2)}, u32[]{:S(2)}) collective-permute-start(f32[1,1152]{1,0:T(1,128)S(1)} %get-tuple-element.87), channel_id=1, source_target_pairs={{0,1},{1,8},{2,3},{3,10},{4,5},{5,12},{6,7},{7,14},{8,9},{9,0},{10... | collective-permute-start | bytes 13832 | tf_op jit(solution)/shard_map/ppermute | solution.py:391
  70.0 1.0 %collective-permute-done.35 = f32[1,1152]{1,0:T(1,128)S(1)} collective-permute-done((f32[1,1152]{1,0:T(1,128)S(1)}, f32[1,1152]{1,0:T(1,128)S(1)}, u32[]{:S(2)}, u32[]{:S(2)}) %collective-permute-start.35) | collective-permute-done | bytes 4640 | tf_op jit(solution)/shard_map/ppermute | solution.py:391
  71.0 1.6 %collective-permute-done.36 = f32[1,1152]{1,0:T(1,128)S(1)} collective-permute-done((f32[1,1152]{1,0:T(1,128)S(1)}, f32[1,1152]{1,0:T(1,128)S(1)}, u32[]{:S(2)}, u32[]{:S(2)}) %collective-permute-start.36) | collective-permute-done | bytes 4640 | tf_op jit(solution)/shard_map/ppermute | solution.py:391
  72.7 4.6 %collective-permute-start.39 = (f32[1,1152]{1,0:T(1,128)S(1)}, f32[1,1152]{1,0:T(1,128)S(1)}, u32[]{:S(2)}, u32[]{:S(2)}) collective-permute-start(f32[1,1152]{1,0:T(1,128)S(1)} %maximum_maximum_fusion.1.refs_0_), channel_id=1, source_target_pairs={{0,6},{1,7},{2,4},{3,5},{4,2},{5,3},{6,0},{7,1},{8,14},{9,15},{10,... | collective-permute-start | bytes 13832 | tf_op jit(solution)/shard_map/ppermute | solution.py:391
  79.1 2.6 %collective-permute-done.38.refs_2_ = f32[1,1152]{1,0:T(1,128)S(1)} collective-permute-done((f32[1,1152]{1,0:T(1,128)S(1)}, f32[1,1152]{1,0:T(1,128)S(1)}, u32[]{:S(2)}, u32[]{:S(2)}) %collective-permute-start.38) | collective-permute-done | bytes 4640 | tf_op jit(solution)/shard_map/ppermute | solution.py:391
  (42 shorter events, 4.9 us)
Async XLA Ops:
  4.3 3.2 %collective-permute-start.21 = (bf16[208,1024]{1,0:T(8,128)(2,1)S(1)}, bf16[208,1024]{1,0:T(8,128)(2,1)S(1)}, u32[]{:S(2)}, u32[]{:S(2)}) collective-permute-start(bf16[208,1024]{1,0:T(8,128)(2,1)S(1)} %fill0.3.refs_0_), channel_id=1, source_target_pairs={{0,8},{1,9},{2,10},{3,11},{4,12},{5,13},{6,14},{7,15},{8,0},{9,1},... | collective-permute-start | bytes 1277960 | tf_op jit(solution)/shard_map/ppermute | solution.py:391
  4.8 15.4 %collective-permute-start.23 = (bf16[208,1024]{1,0:T(8,128)(2,1)S(1)}, bf16[208,1024]{1,0:T(8,128)(2,1)S(1)}, u32[]{:S(2)}, u32[]{:S(2)}) collective-permute-start(bf16[208,1024]{1,0:T(8,128)(2,1)S(1)} %get-tuple-element.71), channel_id=1, source_target_pairs={{0,2},{1,3},{2,4},{3,5},{4,6},{5,7},{6,0},{7,1},{8,10},{9,11},{10,... | collective-permute-start | bytes 1277960 | tf_op jit(solution)/shard_map/ppermute | solution.py:391
  7.5 12.7 %collective-permute-start.25 = (bf16[208,1024]{1,0:T(8,128)(2,1)S(1)}, bf16[208,1024]{1,0:T(8,128)(2,1)S(1)}, u32[]{:S(2)}, u32[]{:S(2)}) collective-permute-start(bf16[208,1024]{1,0:T(8,128)(2,1)S(1)} %after.16.refs_1_), channel_id=1, source_target_pairs={{0,9},{1,0},{2,11},{3,2},{4,13},{5,4},{6,15},{7,6},{8,1},{9,8},{10... | collective-permute-start | bytes 1277960 | tf_op jit(solution)/shard_map/ppermute | solution.py:391
  8.9 12.1 %collective-permute-start.24 = (bf16[208,1024]{1,0:T(8,128)(2,1)S(1)}, bf16[208,1024]{1,0:T(8,128)(2,1)S(1)}, u32[]{:S(2)}, u32[]{:S(2)}) collective-permute-start(bf16[208,1024]{1,0:T(8,128)(2,1)S(1)} %after.16.refs_1_), channel_id=1, source_target_pairs={{0,24},{1,17},{2,26},{3,19},{4,28},{5,21},{6,30},{7,23},{8,16},{9,... | collective-permute-start | bytes 1277960 | tf_op jit(solution)/shard_map/ppermute | solution.py:391
  11.4 23.3 %collective-permute-start.22 = (bf16[208,1024]{1,0:T(8,128)(2,1)S(1)}, bf16[208,1024]{1,0:T(8,128)(2,1)S(1)}, u32[]{:S(2)}, u32[]{:S(2)}) collective-permute-start(bf16[208,1024]{1,0:T(8,128)(2,1)S(1)} %after.15), channel_id=1, source_target_pairs={{0,6},{1,7},{2,0},{3,1},{4,2},{5,3},{6,4},{7,5},{8,14},{9,15},{10,... | collective-permute-start | bytes 1277960 | tf_op jit(solution)/shard_map/ppermute | solution.py:391
  21.0 13.7 %collective-permute-start.28 = (bf16[208,1024]{1,0:T(8,128)(2,1)S(1)}, bf16[208,1024]{1,0:T(8,128)(2,1)S(1)}, u32[]{:S(2)}, u32[]{:S(2)}) collective-permute-start(bf16[208,1024]{1,0:T(8,128)(2,1)S(1)} %after.17.refs_1_), channel_id=1, source_target_pairs={{0,8},{1,9},{2,10},{3,11},{4,12},{5,13},{6,14},{7,15},{8,0},{9,1},... | collective-permute-start | bytes 1277960 | tf_op jit(solution)/shard_map/ppermute | solution.py:391
  21.0 13.7 %collective-permute-start.27 = (bf16[208,1024]{1,0:T(8,128)(2,1)S(1)}, bf16[208,1024]{1,0:T(8,128)(2,1)S(1)}, u32[]{:S(2)}, u32[]{:S(2)}) collective-permute-start(bf16[208,1024]{1,0:T(8,128)(2,1)S(1)} %after.17.refs_1_), channel_id=1, source_target_pairs={{0,9},{1,0},{2,11},{3,2},{4,13},{5,4},{6,15},{7,6},{8,1},{9,8},{10... | collective-permute-start | bytes 1277960 | tf_op jit(solution)/shard_map/ppermute | solution.py:391
  22.1 12.6 %collective-permute-start.26 = (bf16[208,1024]{1,0:T(8,128)(2,1)S(1)}, bf16[208,1024]{1,0:T(8,128)(2,1)S(1)}, u32[]{:S(2)}, u32[]{:S(2)}) collective-permute-start(bf16[208,1024]{1,0:T(8,128)(2,1)S(1)} %after.17.refs_1_), channel_id=1, source_target_pairs={{0,24},{1,17},{2,26},{3,19},{4,28},{5,21},{6,30},{7,23},{8,16},{9,... | collective-permute-start | bytes 1277960 | tf_op jit(solution)/shard_map/ppermute | solution.py:391
  23.2 29.0 %collective-permute-start.20 = (bf16[208,1024]{1,0:T(8,128)(2,1)S(1)}, bf16[208,1024]{1,0:T(8,128)(2,1)S(1)}, u32[]{:S(2)}, u32[]{:S(2)}) collective-permute-start(bf16[208,1024]{1,0:T(8,128)(2,1)S(1)} %get-tuple-element.69), channel_id=1, source_target_pairs={{0,4},{1,5},{2,6},{3,7},{4,0},{5,1},{6,2},{7,3},{8,12},{9,13},{10,... | collective-permute-start | bytes 1277960 | tf_op jit(solution)/shard_map/ppermute | solution.py:391
  34.7 17.5 %collective-permute-start.31 = (bf16[208,1024]{1,0:T(8,128)(2,1)S(1)}, bf16[208,1024]{1,0:T(8,128)(2,1)S(1)}, u32[]{:S(2)}, u32[]{:S(2)}) collective-permute-start(bf16[208,1024]{1,0:T(8,128)(2,1)S(1)} %after.18.refs_1_), channel_id=1, source_target_pairs={{0,8},{1,9},{2,10},{3,11},{4,12},{5,13},{6,14},{7,15},{8,0},{9,1},... | collective-permute-start | bytes 1277960 | tf_op jit(solution)/shard_map/ppermute | solution.py:391
  34.9 17.3 %collective-permute-start.30 = (bf16[208,1024]{1,0:T(8,128)(2,1)S(1)}, bf16[208,1024]{1,0:T(8,128)(2,1)S(1)}, u32[]{:S(2)}, u32[]{:S(2)}) collective-permute-start(bf16[208,1024]{1,0:T(8,128)(2,1)S(1)} %after.18.refs_1_), channel_id=1, source_target_pairs={{0,9},{1,0},{2,11},{3,2},{4,13},{5,4},{6,15},{7,6},{8,1},{9,8},{10... | collective-permute-start | bytes 1277960 | tf_op jit(solution)/shard_map/ppermute | solution.py:391
  35.7 16.5 %collective-permute-start.29 = (bf16[208,1024]{1,0:T(8,128)(2,1)S(1)}, bf16[208,1024]{1,0:T(8,128)(2,1)S(1)}, u32[]{:S(2)}, u32[]{:S(2)}) collective-permute-start(bf16[208,1024]{1,0:T(8,128)(2,1)S(1)} %after.18.refs_1_), channel_id=1, source_target_pairs={{0,24},{1,17},{2,26},{3,19},{4,28},{5,21},{6,30},{7,23},{8,16},{9,... | collective-permute-start | bytes 1277960 | tf_op jit(solution)/shard_map/ppermute | solution.py:391
  52.2 5.6 %collective-permute-start.34 = (bf16[208,1024]{1,0:T(8,128)(2,1)S(1)}, bf16[208,1024]{1,0:T(8,128)(2,1)S(1)}, u32[]{:S(2)}, u32[]{:S(2)}) collective-permute-start(bf16[208,1024]{1,0:T(8,128)(2,1)S(1)} %after.19.refs_1_), channel_id=1, source_target_pairs={{0,8},{1,9},{2,10},{3,11},{4,12},{5,13},{6,14},{7,15},{8,0},{9,1},... | collective-permute-start | bytes 1277960 | tf_op jit(solution)/shard_map/ppermute | solution.py:391
  52.3 12.2 %collective-permute-start.33 = (bf16[208,1024]{1,0:T(8,128)(2,1)S(1)}, bf16[208,1024]{1,0:T(8,128)(2,1)S(1)}, u32[]{:S(2)}, u32[]{:S(2)}) collective-permute-start(bf16[208,1024]{1,0:T(8,128)(2,1)S(1)} %after.19.refs_1_), channel_id=1, source_target_pairs={{0,9},{1,0},{2,11},{3,2},{4,13},{5,4},{6,15},{7,6},{8,1},{9,8},{10... | collective-permute-start | bytes 1277960 | tf_op jit(solution)/shard_map/ppermute | solution.py:391
  52.6 11.9 %collective-permute-start.32 = (bf16[208,1024]{1,0:T(8,128)(2,1)S(1)}, bf16[208,1024]{1,0:T(8,128)(2,1)S(1)}, u32[]{:S(2)}, u32[]{:S(2)}) collective-permute-start(bf16[208,1024]{1,0:T(8,128)(2,1)S(1)} %after.19.refs_1_), channel_id=1, source_target_pairs={{0,24},{1,17},{2,26},{3,19},{4,28},{5,21},{6,30},{7,23},{8,16},{9,... | collective-permute-start | bytes 1277960 | tf_op jit(solution)/shard_map/ppermute | solution.py:391
  57.8 24.1 %copy-start = (bf16[768,1024]{1,0:T(8,128)(2,1)S(1)}, bf16[768,1024]{1,0:T(8,128)(2,1)}, u32[]{:S(2)}) copy-start(bf16[768,1024]{1,0:T(8,128)(2,1)} %emb.1) | copy-start | bytes 4718596
  57.8 24.1 %copy-start.1 = (s32[768]{0:T(1024)S(1)}, s32[768]{0:T(1024)}, u32[]{:S(2)}) copy-start(s32[768]{0:T(1024)} %param.6) | copy-start | bytes 9220
  57.8 24.1 %copy-start.2 = (s32[768]{0:T(1024)S(1)}, s32[768]{0:T(1024)}, u32[]{:S(2)}) copy-start(s32[768]{0:T(1024)} %param.7) | copy-start | bytes 9220
  67.9 3.1 %collective-permute-start.35 = (f32[1,1152]{1,0:T(1,128)S(1)}, f32[1,1152]{1,0:T(1,128)S(1)}, u32[]{:S(2)}, u32[]{:S(2)}) collective-permute-start(f32[1,1152]{1,0:T(1,128)S(1)} %get-tuple-element.87), channel_id=1, source_target_pairs={{0,1},{1,8},{2,3},{3,10},{4,5},{5,12},{6,7},{7,14},{8,9},{9,0},{10... | collective-permute-start | bytes 13832 | tf_op jit(solution)/shard_map/ppermute | solution.py:391
  69.6 3.0 %collective-permute-start.36 = (f32[1,1152]{1,0:T(1,128)S(1)}, f32[1,1152]{1,0:T(1,128)S(1)}, u32[]{:S(2)}, u32[]{:S(2)}) collective-permute-start(f32[1,1152]{1,0:T(1,128)S(1)} %get-tuple-element.88), channel_id=1, source_target_pairs={{0,16},{1,25},{2,18},{3,27},{4,20},{5,29},{6,22},{7,31},{8,24},{9,... | collective-permute-start | bytes 13832 | tf_op jit(solution)/shard_map/ppermute | solution.py:391
  72.7 6.5 %collective-permute-start.39 = (f32[1,1152]{1,0:T(1,128)S(1)}, f32[1,1152]{1,0:T(1,128)S(1)}, u32[]{:S(2)}, u32[]{:S(2)}) collective-permute-start(f32[1,1152]{1,0:T(1,128)S(1)} %maximum_maximum_fusion.1.refs_0_), channel_id=1, source_target_pairs={{0,6},{1,7},{2,4},{3,5},{4,2},{5,3},{6,0},{7,1},{8,14},{9,15},{10,... | collective-permute-start | bytes 13832 | tf_op jit(solution)/shard_map/ppermute | solution.py:391
  77.2 4.5 %collective-permute-start.38 = (f32[1,1152]{1,0:T(1,128)S(1)}, f32[1,1152]{1,0:T(1,128)S(1)}, u32[]{:S(2)}, u32[]{:S(2)}) collective-permute-start(f32[1,1152]{1,0:T(1,128)S(1)} %maximum_maximum_fusion.1.refs_0_), channel_id=1, source_target_pairs={{0,4},{1,5},{2,6},{3,7},{4,0},{5,1},{6,2},{7,3},{8,12},{9,13},{10,... | collective-permute-start | bytes 13832 | tf_op jit(solution)/shard_map/ppermute | solution.py:391
  77.3 4.5 %collective-permute-start.37 = (f32[1,1152]{1,0:T(1,128)S(1)}, f32[1,1152]{1,0:T(1,128)S(1)}, u32[]{:S(2)}, u32[]{:S(2)}) collective-permute-start(f32[1,1152]{1,0:T(1,128)S(1)} %maximum_maximum_fusion.1.refs_0_), channel_id=1, source_target_pairs={{0,2},{1,3},{2,0},{3,1},{4,6},{5,7},{6,4},{7,5},{8,10},{9,11},{10,... | collective-permute-start | bytes 13832 | tf_op jit(solution)/shard_map/ppermute | solution.py:391
  82.1 0.6 copy-start.3

commit v5 on v4

--- a/solution.py
+++ b/solution.py
@@ -60,8 +60,8 @@
     return jnp.concatenate([ref[b : b + 1, :] for b in range(ref.shape[0])], axis=1)
 
 
-def fill(first, caps, flagged, outs, unit, sorting, pick):
-    rows, width = unit.shape
+def fill(first, caps, flagged, outs, emb, sorting, pick, raw):
+    rows, width = emb.shape
     target = sorting[0:1, :].astype(jnp.int32)
     digits = jnp.concatenate([sorting[...], jnp.zeros((8, rows), jnp.float32)], axis=0)
     digits = digits.astype(jnp.bfloat16)
@@ -80,20 +80,21 @@
         if used < width:
             parts.append(jnp.zeros((1, width - used), jnp.float32))
         notes.append(jnp.concatenate(parts, axis=1))
-    last = lax.broadcasted_iota(jnp.int32, (16, 1), 0) == 15
     for at in range(0, width, 256):
         lanes = slice(at, at + 256)
-        moved = jnp.dot(pick[...], unit[:, lanes], preferred_element_type=jnp.float32)
-        for i, (cap, out) in enumerate(zip(caps, outs)):
-            part = moved[starts[i] : starts[i] + cap]
-            out[: cap - 16, lanes] = part[: cap - 16].astype(jnp.bfloat16)
-            end = jnp.where(last, notes[i][:, lanes], part[cap - 16 :])
-            out[cap - 16 :, lanes] = end.astype(jnp.bfloat16)
+        raw[:, lanes] = jnp.dot(pick[...], emb[:, lanes], preferred_element_type=jnp.float32)
+    last = lax.broadcasted_iota(jnp.int32, (16, 1), 0) == 15
+    for i, (cap, out) in enumerate(zip(caps, outs)):
+        wide = raw[starts[i] : starts[i] + cap, :]
+        scale = lax.rsqrt(jnp.sum(wide * wide, axis=1, keepdims=True) + 1e-06)
+        unit = wide * scale
+        out[: cap - 16, :] = unit[: cap - 16].astype(jnp.bfloat16)
+        out[cap - 16 :, :] = jnp.where(last, notes[i], unit[cap - 16 :]).astype(jnp.bfloat16)
 
 
 def sort_kernel(pieces, low, caps, flagged, emb, cid, rank, *refs):
-    out, unit, sorting, place, held, pick, slot_ref, sem = refs
-    rows, width = unit.shape
+    out, held, sorting, place, pick, raw, slot_ref, sem = refs
+    rows, width = held.shape
     parts = 4
     share = rows // parts
     copies = []
@@ -140,28 +141,20 @@
     sorting[4:5, :] = jnp.broadcast_to(full, (1, rows))
     sorting[5:8, :] = jnp.zeros((3, rows), jnp.float32)
 
-    for i in range(parts):
-        copies[i].wait()
-
-        @pl.loop(i * share // 64, (i + 1) * share // 64)
-        def _(j):
-            at = pl.ds(pl.multiple_of(j * 64, 64), 64)
-            wide = held[at, :].astype(jnp.float32)
-            scale = lax.rsqrt(jnp.sum(wide * wide, axis=1, keepdims=True) + 1e-06)
-            unit[at, :] = (wide * scale).astype(jnp.bfloat16)
-
-    fill(1, caps[1:2], flagged, [out], unit, sorting, pick)
-
-
-def fill_kernel(first, caps, flagged, unit, sorting, *refs):
-    fill(first, caps, flagged, refs[:-1], unit, sorting, refs[-1])
+    for copy in copies:
+        copy.wait()
+    fill(1, caps[1:2], flagged, [out], held, sorting, pick, raw)
+
+
+def fill_kernel(first, caps, flagged, emb, sorting, *refs):
+    fill(first, caps, flagged, refs[:-2], emb, sorting, refs[-2], refs[-1])
 
 
 def dispatch(pieces, low, caps, flagged, emb, cid, rank):
     rows, width = emb.shape
     bf16 = jnp.bfloat16
     in_vmem = pl.BlockSpec(memory_space=pltpu.VMEM)
-    one, unit, sorting, place = pl.pallas_call(
+    one, held, sorting, place = pl.pallas_call(
         functools.partial(sort_kernel, pieces, low, caps, flagged),
         out_shape=[
             pltpu.VMEM((caps[1], width), bf16),
@@ -172,8 +165,8 @@
         in_specs=[pl.BlockSpec(memory_space=pl.ANY), in_vmem, in_vmem],
         out_specs=[in_vmem] * 4,
         scratch_shapes=[
-            pltpu.VMEM((rows, width), bf16),
             pltpu.VMEM((caps[1], rows), bf16),
+            pltpu.VMEM((caps[1], width), jnp.float32),
             pltpu.VMEM((1, rows), jnp.int32),
             pltpu.SemaphoreType.DMA((4,)),
         ],
@@ -188,10 +181,13 @@
                 out_shape=[pltpu.VMEM((cap, width), bf16) for cap in caps[first:stop]],
                 in_specs=[in_vmem, in_vmem],
                 out_specs=[in_vmem] * (stop - first),
-                scratch_shapes=[pltpu.VMEM((sum(caps[first:stop]), rows), bf16)],
+                scratch_shapes=[
+                    pltpu.VMEM((sum(caps[first:stop]), rows), bf16),
+                    pltpu.VMEM((sum(caps[first:stop]), width), jnp.float32),
+                ],
                 compiler_params=pltpu.CompilerParams(vmem_limit_bytes=VMEM),
                 name="fill" + str(first),
-            )(in_place(unit), in_place(sorting))
+            )(in_place(held), in_place(sorting))
         )
 
     return more(0, 1) + [one] + more(2, len(caps)), place
@@ -223,7 +219,7 @@
         jnp.int32, (cap, wide), 1
     )
     flag = jnp.zeros((1, LANES), jnp.float32)
-    if p == 0:
+    if p == 0 and part != "away":
         best[...] = jnp.full(best.shape, -1.0, jnp.float32)
     cols[...] = jnp.full(cols.shape, -1.0, jnp.float32)
     for g, block in zip(new, blocks):
@@ -285,16 +281,19 @@
             return just_mine
         return [(mine, 1, mine, 2), (near, 1, near, groups)]
 
-    if p:
-
-        @pl.loop(0, p)
-        def _(i):
-            for g in range(groups):
-                at = (i * groups + g) * wide
-                first = (i * groups + g) * cap
-                product(
-                    pl.multiple_of(first, 16), pl.multiple_of(at, LANES), wide, g, partners(g, False)
-                )
+    def old(i):
+        for g in range(groups):
+            at = (i * groups + g) * wide
+            first = (i * groups + g) * cap
+            if part != "away":
+                first, at = pl.multiple_of(first, 16), pl.multiple_of(at, LANES)
+            product(first, at, wide, g, partners(g, False))
+
+    if part == "away":
+        for i in range(p):
+            old(i)
+    elif p:
+        pl.loop(0, p)(old)
 
     for g in range(groups):
         product(base + g * cap, lane_base[p] + g * wide, wide, g, partners(g, True))
@@ -428,7 +427,7 @@
         leave(1, [])
         links, carried, tokens = [], [], []
         for p in range(count):
-            earlier = links[p - 1] if p else []
+            earlier = links[p - 2] if p >= 2 else []
             if p > 1:
                 earlier = earlier + [tokens[p - 1 - 1]]
             (mine,) = after([moved[p]], earlier)
@@ -438,16 +437,19 @@
             cross = [to_cross(mine, j) for j in range(1, chips)]
             near = to_near(mine)
             links.append(cross + [near, twin])
-            if p == 0:
-                for q in range(2, pieces):
-                    leave(q, [twin] if q == 2 else [])
             groups = 3 + len(cross)
             home, away = [twin, mine], cross + [near]
-            if p < count - 1:
+            if p in (count - 1,):
+                carried, token, ends = stage(p, "home", caps, groups, flagged, home, carried)
+                if p == 0:
+                    for q in range(2, pieces):
+                        leave(q, [token] if q == 2 else [])
+                carried, token, ends = stage(p, "away", caps, groups, flagged, away, carried)
+            else:
+                if p == 0:
+                    for q in range(2, pieces):
+                        leave(q, [twin] if q == 2 else [])
                 carried, token, ends = stage(p, "all", caps, groups, flagged, home + away, carried)
-            else:
-                carried, token, ends = stage(p, "home", caps, groups, flagged, home, carried)
-                carried, token, ends = stage(p, "away", caps, groups, flagged, away, carried)
             tokens.append(token)
         a = jnp.maximum(ends[0], from_near(ends[-1]))
         for j in range(1, chips):

time: 83 us -> 80.5 us (0.970)
  Pallas kernels: 22.3 us -> 21 us
  waiting for transfers between devices: 27.5 us -> 26.6 us
    pallas_call x1, Pallas kernels: 3.72 us -> 2.79 us  [dispatch(): pl.pallas_call(functools.partial(sort_kernel, pieces, low, caps, flagged)...]
    ppermute x20, waiting for transfers between devices: 27.5 us -> 26.6 us  [send(): return lax.ppermute(block, AXES, route)]
  transfers between devices with their start and end apart: 20 -> 20, of which waited for: 7 -> 6; matrix products, arithmetic and copies ran while one was open for 1% -> 1% of each run, Pallas kernels for 18% -> 18%
where the time goes in v5:
time: 80.5 us; the launch traced here: 80.3 us
  starting transfers between devices  30.3 us (38%)
  waiting for transfers between devices  26.6 us (33%)
  Pallas kernels  21 us (26%)
  local copies, waits for them, and re-layouts  1.19 us (1%)
  between operations  0.84 us (1%)
    ppermute x20, starting transfers between devices, send(): return lax.ppermute(block, AXES, route)  30.3 us
    ppermute x20, waiting for transfers between devices, send(): return lax.ppermute(block, AXES, route)  26.6 us
    pallas_call x5, Pallas kernels, stage(): pl.pallas_call(functools.partial(stage_kernel, p, part, caps, groups, fla...  16.3 us
    pallas_call x1, Pallas kernels, dispatch(): pl.pallas_call(functools.partial(sort_kernel, pieces, low, caps, flagged)...  2.79 us
    pallas_call x2, Pallas kernels, more(): pl.pallas_call(functools.partial(fill_kernel, first, caps[first:stop], fl...  1.84 us
  transfers between devices with their start and end apart: 20, of which 6 were waited for; matrix products, arithmetic and copies ran while one was open for 1% of the time, Pallas kernels for 18%

profile of v5, /device:TPU:0, one launch (start us, length us, event | category | flops | bytes accessed | tf_op | source)
XLA Modules:
  0.0 80.3 jit_solution(721489060238856347)
XLA Ops:
  0.0 2.8 %sort.3 = (bf16[208,1024]{1,0:T(8,128)(2,1)S(1)}, bf16[768,1024]{1,0:T(8,128)(2,1)S(1)}, f32[8,768]{1,0:T(8,128)S(1)}, s32[8,128]{1,0:T(8,128)S(1)}) custom-call(bf16[768,1024]{1,0:T(8,128)(2,1)} %emb.1, s32[6,128]{1,0:T(8,128)} %bitcast.9, s32[6,128]{1,0:T(8,128)} %bitcast.11), custom_call_target="tpu_custom_call" | custom-call | tf_op jit(solution)/shard_map/sort/pallas_call | solution.py:157
  4.0 2.6 %collective-permute-start.21 = (bf16[208,1024]{1,0:T(8,128)(2,1)S(1)}, bf16[208,1024]{1,0:T(8,128)(2,1)S(1)}, u32[]{:S(2)}, u32[]{:S(2)}) collective-permute-start(bf16[208,1024]{1,0:T(8,128)(2,1)S(1)} %get-tuple-element.70), channel_id=1, source_target_pairs={{0,2},{1,3},{2,4},{3,5},{4,6},{5,7},{6,0},{7,1},{8,10},{9,11},{10,... | collective-permute-start | bytes 1277960 | tf_op jit(solution)/shard_map/ppermute | solution.py:390
  6.7 1.4 %collective-permute-start.27 = (bf16[208,1024]{1,0:T(8,128)(2,1)S(1)}, bf16[208,1024]{1,0:T(8,128)(2,1)S(1)}, u32[]{:S(2)}, u32[]{:S(2)}) collective-permute-start(bf16[208,1024]{1,0:T(8,128)(2,1)S(1)} %after.12.refs_1_), channel_id=1, source_target_pairs={{0,9},{1,0},{2,11},{3,2},{4,13},{5,4},{6,15},{7,6},{8,1},{9,8},{10... | collective-permute-start | bytes 1277960 | tf_op jit(solution)/shard_map/ppermute | solution.py:390
  8.0 1.5 %collective-permute-start.26 = (bf16[208,1024]{1,0:T(8,128)(2,1)S(1)}, bf16[208,1024]{1,0:T(8,128)(2,1)S(1)}, u32[]{:S(2)}, u32[]{:S(2)}) collective-permute-start(bf16[208,1024]{1,0:T(8,128)(2,1)S(1)} %after.12.refs_1_), channel_id=1, source_target_pairs={{0,24},{1,17},{2,26},{3,19},{4,28},{5,21},{6,30},{7,23},{8,16},{9,... | collective-permute-start | bytes 1277960 | tf_op jit(solution)/shard_map/ppermute | solution.py:390
  9.5 1.1 %fill2.3 = (bf16[208,1024]{1,0:T(8,128)(2,1)S(1)}, bf16[208,1024]{1,0:T(8,128)(2,1)S(1)}) custom-call(bf16[768,1024]{1,0:T(8,128)(2,1)S(1)} %get-tuple-element.67.emb, f32[8,768]{1,0:T(8,128)S(1)} %get-tuple-element.68.sorting), custom_call_target="tpu_custom_call" | custom-call | tf_op jit(solution)/shard_map/fill2/pallas_call | solution.py:179
  10.7 3.7 %collective-permute-start.31 = (bf16[208,1024]{1,0:T(8,128)(2,1)S(1)}, bf16[208,1024]{1,0:T(8,128)(2,1)S(1)}, u32[]{:S(2)}, u32[]{:S(2)}) collective-permute-start(bf16[208,1024]{1,0:T(8,128)(2,1)S(1)} %after.14), channel_id=1, source_target_pairs={{0,6},{1,7},{2,0},{3,1},{4,2},{5,3},{6,4},{7,5},{8,14},{9,15},{10,... | collective-permute-start | bytes 1277960 | tf_op jit(solution)/shard_map/ppermute | solution.py:390
  14.3 5.1 %collective-permute-done.21.refs_1_ = bf16[208,1024]{1,0:T(8,128)(2,1)S(1)} collective-permute-done((bf16[208,1024]{1,0:T(8,128)(2,1)S(1)}, bf16[208,1024]{1,0:T(8,128)(2,1)S(1)}, u32[]{:S(2)}, u32[]{:S(2)}) %collective-permute-start.21) | collective-permute-done | bytes 426016 | tf_op jit(solution)/shard_map/ppermute | solution.py:390
  19.4 1.8 %collective-permute-start.23 = (bf16[208,1024]{1,0:T(8,128)(2,1)S(1)}, bf16[208,1024]{1,0:T(8,128)(2,1)S(1)}, u32[]{:S(2)}, u32[]{:S(2)}) collective-permute-start(bf16[208,1024]{1,0:T(8,128)(2,1)S(1)} %collective-permute-done.21.refs_1_), channel_id=1, source_target_pairs={{0,9},{1,0},{2,11},{3,2},{4,13},{5,4},{6,15},{7,6},{8,1},{9,8},{10... | collective-permute-start | bytes 1277960 | tf_op jit(solution)/shard_map/ppermute | solution.py:390
  21.2 1.1 %collective-permute-start.22 = (bf16[208,1024]{1,0:T(8,128)(2,1)S(1)}, bf16[208,1024]{1,0:T(8,128)(2,1)S(1)}, u32[]{:S(2)}, u32[]{:S(2)}) collective-permute-start(bf16[208,1024]{1,0:T(8,128)(2,1)S(1)} %collective-permute-done.21.refs_1_), channel_id=1, source_target_pairs={{0,24},{1,17},{2,26},{3,19},{4,28},{5,21},{6,30},{7,23},{8,16},{9,... | collective-permute-start | bytes 1277960 | tf_op jit(solution)/shard_map/ppermute | solution.py:390
  22.3 9.4 %collective-permute-start.20 = (bf16[208,1024]{1,0:T(8,128)(2,1)S(1)}, bf16[208,1024]{1,0:T(8,128)(2,1)S(1)}, u32[]{:S(2)}, u32[]{:S(2)}) collective-permute-start(bf16[208,1024]{1,0:T(8,128)(2,1)S(1)} %get-tuple-element.69), channel_id=1, source_target_pairs={{0,4},{1,5},{2,6},{3,7},{4,0},{5,1},{6,2},{7,3},{8,12},{9,13},{10,... | collective-permute-start | bytes 1277960 | tf_op jit(solution)/shard_map/ppermute | solution.py:390
  31.7 2.0 %stage0all.3 = (bf16[3456,1024]{1,0:T(8,128)(2,1)S(1)}, f32[8,4096]{1,0:T(8,128)S(1)}, f32[8,4224]{1,0:T(8,128)S(1)}, f32[8,128]{1,0:T(8,128)S(1)}) custom-call(bf16[208,1024]{1,0:T(8,128)(2,1)S(1)} %collective-permute-done.25.refs_1_.refs_0_.refs_3_, bf16[208,1024]{1,0:T(8,128)(2,1)S(1)} %after.12.refs_1_, ...), custom_call_target="tpu_custom_call" | custom-call | tf_op jit(solution)/shard_map/stage0all/pallas_call | solution.py:330
  33.8 0.8 %collective-permute-start.33 = (bf16[208,1024]{1,0:T(8,128)(2,1)S(1)}, bf16[208,1024]{1,0:T(8,128)(2,1)S(1)}, u32[]{:S(2)}, u32[]{:S(2)}) collective-permute-start(bf16[208,1024]{1,0:T(8,128)(2,1)S(1)} %after.15.refs_1_), channel_id=1, source_target_pairs={{0,24},{1,17},{2,26},{3,19},{4,28},{5,21},{6,30},{7,23},{8,16},{9,... | collective-permute-start | bytes 1277960 | tf_op jit(solution)/shard_map/ppermute | solution.py:390
  34.9 3.1 %stage1all.3 = (bf16[3456,1024]{1,0:T(8,128)(2,1)S(1)}, f32[8,4096]{1,0:T(8,128)S(1)}, f32[8,4224]{1,0:T(8,128)S(1)}, f32[8,128]{1,0:T(8,128)S(1)}) custom-call(bf16[208,1024]{1,0:T(8,128)(2,1)S(1)} %collective-permute-done.24.refs_0_.refs_3_, ...), custom_call_target="tpu_custom_call", output_to_operand_aliasing={{0}: (4, {}), {1}: (5, {}), {2}: (6, {})} | custom-call | tf_op jit(solution)/shard_map/stage1all/pallas_call | solution.py:330
  38.0 13.3 %collective-permute-done.20.refs_0_ = bf16[208,1024]{1,0:T(8,128)(2,1)S(1)} collective-permute-done((bf16[208,1024]{1,0:T(8,128)(2,1)S(1)}, bf16[208,1024]{1,0:T(8,128)(2,1)S(1)}, u32[]{:S(2)}, u32[]{:S(2)}) %collective-permute-start.20) | collective-permute-done | bytes 426016 | tf_op jit(solution)/shard_map/ppermute | solution.py:390
  52.0 4.7 %stage2all.3 = (bf16[3456,1024]{1,0:T(8,128)(2,1)S(1)}, f32[8,4096]{1,0:T(8,128)S(1)}, f32[8,4224]{1,0:T(8,128)S(1)}, f32[8,128]{1,0:T(8,128)}) custom-call(bf16[208,1024]{1,0:T(8,128)(2,1)S(1)} %collective-permute-done.32.refs_0_, bf16[208,1024]{1,0:T(8,128)(2,1)S(1)} %after.15.refs_1_, ...), custom_call_target="tpu_custom_call", output_to_operand_aliasing={{0}: (4, {}), {1}: (5, {}), {2}: (6, {})} | custom-call | tf_op jit(solution)/shard_map/stage2all/pallas_call | solution.py:330
  56.7 3.6 %stage3home.3 = (bf16[3456,1024]{1,0:T(8,128)(2,1)S(1)}, f32[8,4096]{1,0:T(8,128)S(1)}, f32[8,4224]{1,0:T(8,128)S(1)}, f32[8,128]{1,0:T(8,128)}) custom-call(bf16[208,1024]{1,0:T(8,128)(2,1)S(1)} %collective-permute-done.30.refs_0_, bf16[208,1024]{1,0:T(8,128)(2,1)S(1)} %after.13.refs_1_, ...), custom_call_target="tpu_custom_call", output_to_operand_aliasing={{0}: (2, {}), {1}: (3, {}), {2}: (4, {})} | custom-call | tf_op jit(solution)/shard_map/stage3home/pallas_call | solution.py:330
  60.4 3.2 %collective-permute-done.29.refs_1_ = bf16[208,1024]{1,0:T(8,128)(2,1)S(1)} collective-permute-done((bf16[208,1024]{1,0:T(8,128)(2,1)S(1)}, bf16[208,1024]{1,0:T(8,128)(2,1)S(1)}, u32[]{:S(2)}, u32[]{:S(2)}) %collective-permute-start.29) | collective-permute-done | bytes 426016 | tf_op jit(solution)/shard_map/ppermute | solution.py:390
  63.6 2.8 %stage3away.3 = (bf16[3456,1024]{1,0:T(8,128)(2,1)S(1)}, f32[8,4096]{1,0:T(8,128)S(1)}, f32[8,4224]{1,0:T(8,128)S(1)}, f32[8,128]{1,0:T(8,128)}, f32[1,1152]{1,0...) custom-call(bf16[208,1024]{1,0:T(8,128)(2,1)S(1)} %collective-permut, ...), custom_call_target="tpu_custom_call", output_to_operand_aliasing={{0}: (2, {}), {1}: (3, {}), {2}: (4, {})} | custom-call | tf_op jit(solution)/shard_map/stage3away/pallas_call | solution.py:330
  66.4 1.6 %collective-permute-start.35 = (f32[1,1152]{1,0:T(1,128)S(1)}, f32[1,1152]{1,0:T(1,128)S(1)}, u32[]{:S(2)}, u32[]{:S(2)}) collective-permute-start(f32[1,1152]{1,0:T(1,128)S(1)} %get-tuple-element.87), channel_id=1, source_target_pairs={{0,1},{1,8},{2,3},{3,10},{4,5},{5,12},{6,7},{7,14},{8,9},{9,0},{10... | collective-permute-start | bytes 13832 | tf_op jit(solution)/shard_map/ppermute | solution.py:390
  68.5 1.0 %collective-permute-done.35 = f32[1,1152]{1,0:T(1,128)S(1)} collective-permute-done((f32[1,1152]{1,0:T(1,128)S(1)}, f32[1,1152]{1,0:T(1,128)S(1)}, u32[]{:S(2)}, u32[]{:S(2)}) %collective-permute-start.35) | collective-permute-done | bytes 4640 | tf_op jit(solution)/shard_map/ppermute | solution.py:390
  69.5 1.6 %collective-permute-done.36 = f32[1,1152]{1,0:T(1,128)S(1)} collective-permute-done((f32[1,1152]{1,0:T(1,128)S(1)}, f32[1,1152]{1,0:T(1,128)S(1)}, u32[]{:S(2)}, u32[]{:S(2)}) %collective-permute-start.36) | collective-permute-done | bytes 4640 | tf_op jit(solution)/shard_map/ppermute | solution.py:390
  71.1 3.6 %collective-permute-start.39 = (f32[1,1152]{1,0:T(1,128)S(1)}, f32[1,1152]{1,0:T(1,128)S(1)}, u32[]{:S(2)}, u32[]{:S(2)}) collective-permute-start(f32[1,1152]{1,0:T(1,128)S(1)} %maximum_maximum_fusion.1.refs_0_), channel_id=1, source_target_pairs={{0,6},{1,7},{2,4},{3,5},{4,2},{5,3},{6,0},{7,1},{8,14},{9,15},{10,... | collective-permute-start | bytes 13832 | tf_op jit(solution)/shard_map/ppermute | solution.py:390
  74.7 0.8 collective-permute-start.37
  76.8 2.5 %collective-permute-done.38.refs_2_ = f32[1,1152]{1,0:T(1,128)S(1)} collective-permute-done((f32[1,1152]{1,0:T(1,128)S(1)}, f32[1,1152]{1,0:T(1,128)S(1)}, u32[]{:S(2)}, u32[]{:S(2)}) %collective-permute-start.38) | collective-permute-done | bytes 4640 | tf_op jit(solution)/shard_map/ppermute | solution.py:390
  (41 shorter events, 4.3 us)
Async XLA Ops:
  3.5 3.2 %collective-permute-start.25 = (bf16[208,1024]{1,0:T(8,128)(2,1)S(1)}, bf16[208,1024]{1,0:T(8,128)(2,1)S(1)}, u32[]{:S(2)}, u32[]{:S(2)}) collective-permute-start(bf16[208,1024]{1,0:T(8,128)(2,1)S(1)} %fill0.3.refs_0_), channel_id=1, source_target_pairs={{0,8},{1,9},{2,10},{3,11},{4,12},{5,13},{6,14},{7,15},{8,0},{9,1},... | collective-permute-start | bytes 1277960 | tf_op jit(solution)/shard_map/ppermute | solution.py:390
  4.0 15.4 %collective-permute-start.21 = (bf16[208,1024]{1,0:T(8,128)(2,1)S(1)}, bf16[208,1024]{1,0:T(8,128)(2,1)S(1)}, u32[]{:S(2)}, u32[]{:S(2)}) collective-permute-start(bf16[208,1024]{1,0:T(8,128)(2,1)S(1)} %get-tuple-element.70), channel_id=1, source_target_pairs={{0,2},{1,3},{2,4},{3,5},{4,6},{5,7},{6,0},{7,1},{8,10},{9,11},{10,... | collective-permute-start | bytes 1277960 | tf_op jit(solution)/shard_map/ppermute | solution.py:390
  6.7 14.5 %collective-permute-start.27 = (bf16[208,1024]{1,0:T(8,128)(2,1)S(1)}, bf16[208,1024]{1,0:T(8,128)(2,1)S(1)}, u32[]{:S(2)}, u32[]{:S(2)}) collective-permute-start(bf16[208,1024]{1,0:T(8,128)(2,1)S(1)} %after.12.refs_1_), channel_id=1, source_target_pairs={{0,9},{1,0},{2,11},{3,2},{4,13},{5,4},{6,15},{7,6},{8,1},{9,8},{10... | collective-permute-start | bytes 1277960 | tf_op jit(solution)/shard_map/ppermute | solution.py:390
  8.0 14.2 %collective-permute-start.26 = (bf16[208,1024]{1,0:T(8,128)(2,1)S(1)}, bf16[208,1024]{1,0:T(8,128)(2,1)S(1)}, u32[]{:S(2)}, u32[]{:S(2)}) collective-permute-start(bf16[208,1024]{1,0:T(8,128)(2,1)S(1)} %after.12.refs_1_), channel_id=1, source_target_pairs={{0,24},{1,17},{2,26},{3,19},{4,28},{5,21},{6,30},{7,23},{8,16},{9,... | collective-permute-start | bytes 1277960 | tf_op jit(solution)/shard_map/ppermute | solution.py:390
  10.7 23.0 %collective-permute-start.31 = (bf16[208,1024]{1,0:T(8,128)(2,1)S(1)}, bf16[208,1024]{1,0:T(8,128)(2,1)S(1)}, u32[]{:S(2)}, u32[]{:S(2)}) collective-permute-start(bf16[208,1024]{1,0:T(8,128)(2,1)S(1)} %after.14), channel_id=1, source_target_pairs={{0,6},{1,7},{2,0},{3,1},{4,2},{5,3},{6,4},{7,5},{8,14},{9,15},{10,... | collective-permute-start | bytes 1277960 | tf_op jit(solution)/shard_map/ppermute | solution.py:390
  19.4 14.4 %collective-permute-start.24 = (bf16[208,1024]{1,0:T(8,128)(2,1)S(1)}, bf16[208,1024]{1,0:T(8,128)(2,1)S(1)}, u32[]{:S(2)}, u32[]{:S(2)}) collective-permute-start(bf16[208,1024]{1,0:T(8,128)(2,1)S(1)} %collective-permute-done.21.refs_1_), channel_id=1, source_target_pairs={{0,8},{1,9},{2,10},{3,11},{4,12},{5,13},{6,14},{7,15},{8,0},{9,1},... | collective-permute-start | bytes 1277960 | tf_op jit(solution)/shard_map/ppermute | solution.py:390
  19.4 15.3 %collective-permute-start.23 = (bf16[208,1024]{1,0:T(8,128)(2,1)S(1)}, bf16[208,1024]{1,0:T(8,128)(2,1)S(1)}, u32[]{:S(2)}, u32[]{:S(2)}) collective-permute-start(bf16[208,1024]{1,0:T(8,128)(2,1)S(1)} %collective-permute-done.21.refs_1_), channel_id=1, source_target_pairs={{0,9},{1,0},{2,11},{3,2},{4,13},{5,4},{6,15},{7,6},{8,1},{9,8},{10... | collective-permute-start | bytes 1277960 | tf_op jit(solution)/shard_map/ppermute | solution.py:390
  21.2 13.7 %collective-permute-start.22 = (bf16[208,1024]{1,0:T(8,128)(2,1)S(1)}, bf16[208,1024]{1,0:T(8,128)(2,1)S(1)}, u32[]{:S(2)}, u32[]{:S(2)}) collective-permute-start(bf16[208,1024]{1,0:T(8,128)(2,1)S(1)} %collective-permute-done.21.refs_1_), channel_id=1, source_target_pairs={{0,24},{1,17},{2,26},{3,19},{4,28},{5,21},{6,30},{7,23},{8,16},{9,... | collective-permute-start | bytes 1277960 | tf_op jit(solution)/shard_map/ppermute | solution.py:390
  22.3 29.0 %collective-permute-start.20 = (bf16[208,1024]{1,0:T(8,128)(2,1)S(1)}, bf16[208,1024]{1,0:T(8,128)(2,1)S(1)}, u32[]{:S(2)}, u32[]{:S(2)}) collective-permute-start(bf16[208,1024]{1,0:T(8,128)(2,1)S(1)} %get-tuple-element.69), channel_id=1, source_target_pairs={{0,4},{1,5},{2,6},{3,7},{4,0},{5,1},{6,2},{7,3},{8,12},{9,13},{10,... | collective-permute-start | bytes 1277960 | tf_op jit(solution)/shard_map/ppermute | solution.py:390
  33.7 17.9 %collective-permute-start.34 = (bf16[208,1024]{1,0:T(8,128)(2,1)S(1)}, bf16[208,1024]{1,0:T(8,128)(2,1)S(1)}, u32[]{:S(2)}, u32[]{:S(2)}) collective-permute-start(bf16[208,1024]{1,0:T(8,128)(2,1)S(1)} %after.15.refs_1_), channel_id=1, source_target_pairs={{0,9},{1,0},{2,11},{3,2},{4,13},{5,4},{6,15},{7,6},{8,1},{9,8},{10... | collective-permute-start | bytes 1277960 | tf_op jit(solution)/shard_map/ppermute | solution.py:390
  33.8 18.1 %collective-permute-start.33 = (bf16[208,1024]{1,0:T(8,128)(2,1)S(1)}, bf16[208,1024]{1,0:T(8,128)(2,1)S(1)}, u32[]{:S(2)}, u32[]{:S(2)}) collective-permute-start(bf16[208,1024]{1,0:T(8,128)(2,1)S(1)} %after.15.refs_1_), channel_id=1, source_target_pairs={{0,24},{1,17},{2,26},{3,19},{4,28},{5,21},{6,30},{7,23},{8,16},{9,... | collective-permute-start | bytes 1277960 | tf_op jit(solution)/shard_map/ppermute | solution.py:390
  34.7 17.3 %collective-permute-start.32 = (bf16[208,1024]{1,0:T(8,128)(2,1)S(1)}, bf16[208,1024]{1,0:T(8,128)(2,1)S(1)}, u32[]{:S(2)}, u32[]{:S(2)}) collective-permute-start(bf16[208,1024]{1,0:T(8,128)(2,1)S(1)} %after.15.refs_1_), channel_id=1, source_target_pairs={{0,8},{1,9},{2,10},{3,11},{4,12},{5,13},{6,14},{7,15},{8,0},{9,1},... | collective-permute-start | bytes 1277960 | tf_op jit(solution)/shard_map/ppermute | solution.py:390
  51.3 5.4 %collective-permute-start.30 = (bf16[208,1024]{1,0:T(8,128)(2,1)S(1)}, bf16[208,1024]{1,0:T(8,128)(2,1)S(1)}, u32[]{:S(2)}, u32[]{:S(2)}) collective-permute-start(bf16[208,1024]{1,0:T(8,128)(2,1)S(1)} %after.13.refs_1_), channel_id=1, source_target_pairs={{0,8},{1,9},{2,10},{3,11},{4,12},{5,13},{6,14},{7,15},{8,0},{9,1},... | collective-permute-start | bytes 1277960 | tf_op jit(solution)/shard_map/ppermute | solution.py:390
  51.3 12.2 %collective-permute-start.29 = (bf16[208,1024]{1,0:T(8,128)(2,1)S(1)}, bf16[208,1024]{1,0:T(8,128)(2,1)S(1)}, u32[]{:S(2)}, u32[]{:S(2)}) collective-permute-start(bf16[208,1024]{1,0:T(8,128)(2,1)S(1)} %after.13.refs_1_), channel_id=1, source_target_pairs={{0,9},{1,0},{2,11},{3,2},{4,13},{5,4},{6,15},{7,6},{8,1},{9,8},{10... | collective-permute-start | bytes 1277960 | tf_op jit(solution)/shard_map/ppermute | solution.py:390
  51.7 11.9 %collective-permute-start.28 = (bf16[208,1024]{1,0:T(8,128)(2,1)S(1)}, bf16[208,1024]{1,0:T(8,128)(2,1)S(1)}, u32[]{:S(2)}, u32[]{:S(2)}) collective-permute-start(bf16[208,1024]{1,0:T(8,128)(2,1)S(1)} %after.13.refs_1_), channel_id=1, source_target_pairs={{0,24},{1,17},{2,26},{3,19},{4,28},{5,21},{6,30},{7,23},{8,16},{9,... | collective-permute-start | bytes 1277960 | tf_op jit(solution)/shard_map/ppermute | solution.py:390
  56.7 22.6 %copy-start = (bf16[768,1024]{1,0:T(8,128)(2,1)S(1)}, bf16[768,1024]{1,0:T(8,128)(2,1)}, u32[]{:S(2)}) copy-start(bf16[768,1024]{1,0:T(8,128)(2,1)} %emb.1) | copy-start | bytes 4718596
  56.7 22.6 %copy-start.1 = (s32[768]{0:T(1024)S(1)}, s32[768]{0:T(1024)}, u32[]{:S(2)}) copy-start(s32[768]{0:T(1024)} %param.6) | copy-start | bytes 9220
  56.7 22.6 %copy-start.2 = (s32[768]{0:T(1024)S(1)}, s32[768]{0:T(1024)}, u32[]{:S(2)}) copy-start(s32[768]{0:T(1024)} %param.7) | copy-start | bytes 9220
  66.4 3.1 %collective-permute-start.35 = (f32[1,1152]{1,0:T(1,128)S(1)}, f32[1,1152]{1,0:T(1,128)S(1)}, u32[]{:S(2)}, u32[]{:S(2)}) collective-permute-start(f32[1,1152]{1,0:T(1,128)S(1)} %get-tuple-element.87), channel_id=1, source_target_pairs={{0,1},{1,8},{2,3},{3,10},{4,5},{5,12},{6,7},{7,14},{8,9},{9,0},{10... | collective-permute-start | bytes 13832 | tf_op jit(solution)/shard_map/ppermute | solution.py:390
  68.0 3.0 %collective-permute-start.36 = (f32[1,1152]{1,0:T(1,128)S(1)}, f32[1,1152]{1,0:T(1,128)S(1)}, u32[]{:S(2)}, u32[]{:S(2)}) collective-permute-start(f32[1,1152]{1,0:T(1,128)S(1)} %get-tuple-element.88), channel_id=1, source_target_pairs={{0,16},{1,25},{2,18},{3,27},{4,20},{5,29},{6,22},{7,31},{8,24},{9,... | collective-permute-start | bytes 13832 | tf_op jit(solution)/shard_map/ppermute | solution.py:390
  71.1 5.7 %collective-permute-start.39 = (f32[1,1152]{1,0:T(1,128)S(1)}, f32[1,1152]{1,0:T(1,128)S(1)}, u32[]{:S(2)}, u32[]{:S(2)}) collective-permute-start(f32[1,1152]{1,0:T(1,128)S(1)} %maximum_maximum_fusion.1.refs_0_), channel_id=1, source_target_pairs={{0,6},{1,7},{2,4},{3,5},{4,2},{5,3},{6,0},{7,1},{8,14},{9,15},{10,... | collective-permute-start | bytes 13832 | tf_op jit(solution)/shard_map/ppermute | solution.py:390
  74.7 4.5 %collective-permute-start.38 = (f32[1,1152]{1,0:T(1,128)S(1)}, f32[1,1152]{1,0:T(1,128)S(1)}, u32[]{:S(2)}, u32[]{:S(2)}) collective-permute-start(f32[1,1152]{1,0:T(1,128)S(1)} %maximum_maximum_fusion.1.refs_0_), channel_id=1, source_target_pairs={{0,4},{1,5},{2,6},{3,7},{4,0},{5,1},{6,2},{7,3},{8,12},{9,13},{10,... | collective-permute-start | bytes 13832 | tf_op jit(solution)/shard_map/ppermute | solution.py:390
  74.7 4.5 %collective-permute-start.37 = (f32[1,1152]{1,0:T(1,128)S(1)}, f32[1,1152]{1,0:T(1,128)S(1)}, u32[]{:S(2)}, u32[]{:S(2)}) collective-permute-start(f32[1,1152]{1,0:T(1,128)S(1)} %maximum_maximum_fusion.1.refs_0_), channel_id=1, source_target_pairs={{0,2},{1,3},{2,0},{3,1},{4,6},{5,7},{6,4},{7,5},{8,10},{9,11},{10,... | collective-permute-start | bytes 13832 | tf_op jit(solution)/shard_map/ppermute | solution.py:390
  79.7 0.6 copy-start.3

commit v6 on v5

--- a/solution.py
+++ b/solution.py
@@ -25,7 +25,8 @@
 
 
 def steps(pieces):
-    return sorted(range(pieces), key=lambda s: (min(s, pieces - s), s))
+    bits = (pieces - 1).bit_length()
+    return [sum((p >> i & 1) << (bits - 1 - i) for i in range(bits)) for p in range(pieces)]
 
 
 def in_place(array):
@@ -105,8 +106,7 @@
         copies.append(copy)
 
     plane = lax.axis_index("sub") // low
-    step = flat(cid) - plane
-    step = jnp.where(step < 0, step + pieces, step)
+    step = flat(cid) ^ plane
     piece = jnp.zeros(step.shape, jnp.int32)
     for p, s in enumerate(steps(pieces)):
         piece = jnp.where(step == s, p, piece)
@@ -345,19 +345,13 @@
     return got[:3], got[3], got[4:]
 
 
-def collect_kernel(lanes, shifts, low, place, *refs):
+def collect_kernel(lanes, step, place, *refs):
     rows, out = refs[:-1], refs[-1]
-    plane = lax.axis_index("sub") // low
-    count = len(rows)
     where = place[...]
     result = jnp.zeros((8, LANES), jnp.float32)
     for q, start in enumerate(starts_of(lanes)):
-        apart = plane ^ ((plane + shifts[q]) % count)
         for first in range(start, start + lanes[q], LANES):
-            back = rows[0][:, first : first + LANES]
-            for s in range(1, count):
-                back = jnp.where(apart == s, rows[s][:, first : first + LANES], back)
-            back = jnp.broadcast_to(back, (8, LANES))
+            back = jnp.broadcast_to(rows[step[q]][:, first : first + LANES], (8, LANES))
             inside = where - first
             hit = (inside >= 0) & (inside < LANES)
             taken = jnp.take_along_axis(back, jnp.where(hit, inside, 0), axis=1)
@@ -365,10 +359,10 @@
     out[...] = result
 
 
-def collect(caps, shifts, low, place, rows):
+def collect(caps, step, place, rows):
     lanes = [ceil_to(c, LANES) for c in caps]
     return pl.pallas_call(
-        functools.partial(collect_kernel, lanes, shifts, low),
+        functools.partial(collect_kernel, lanes, step),
         out_shape=jax.ShapeDtypeStruct((8, LANES), jnp.float32),
         in_specs=[pl.BlockSpec(memory_space=pltpu.VMEM)] * (1 + len(rows)),
         name="collect",
@@ -390,9 +384,6 @@
         return lax.ppermute(block, AXES, route)
 
     def to_plane(block, s):
-        return send(block, lambda x, c, z, y: (x, c, (z + s) % pieces, y))
-
-    def across(block, s):
         return send(block, lambda x, c, z, y: (x, c, z ^ s, y))
 
     def to_twin(block):
@@ -454,8 +445,8 @@
         a = jnp.maximum(ends[0], from_near(ends[-1]))
         for j in range(1, chips):
             a = jnp.maximum(a, from_cross(ends[j], j))
-        back = [a] + [across(a, s) for s in range(1, pieces)]
-        result = collect(caps, step, low, place, back)
+        back = [a] + [to_plane(a, s) for s in range(1, pieces)]
+        result = collect(caps, step, place, back)
         return result[: rows // LANES].reshape(rows), a[0, -1]
 
     def body(embeddings, cluster_id, cluster_rank):

time: 80.5 us -> 78.2 us (0.971)
  starting transfers between devices: 30.3 us -> 25.7 us
  waiting for transfers between devices: 26.6 us -> 29 us
    ppermute x20, starting transfers between devices: 30.3 us -> 25.7 us  [send(): return lax.ppermute(block, AXES, route)]
    ppermute x20, waiting for transfers between devices: 26.6 us -> 29 us  [send(): return lax.ppermute(block, AXES, route)]
  transfers between devices with their start and end apart: 20 -> 20, of which waited for: 6 -> 9; matrix products, arithmetic and copies ran while one was open for 1% -> 1% of each run, Pallas kernels for 18% -> 19%
where the time goes in v6:
time: 78.2 us; the launch traced here: 78 us
  waiting for transfers between devices  29 us (37%)
  starting transfers between devices  25.7 us (33%)
  Pallas kernels  21 us (27%)
  local copies, waits for them, and re-layouts  1.19 us (2%)
  between operations  0.87 us (1%)
    ppermute x20, waiting for transfers between devices, send(): return lax.ppermute(block, AXES, route)  29 us
    ppermute x20, starting transfers between devices, send(): return lax.ppermute(block, AXES, route)  25.7 us
    pallas_call x5, Pallas kernels, stage(): pl.pallas_call(functools.partial(stage_kernel, p, part, caps, groups, fla...  16.3 us
    pallas_call x1, Pallas kernels, dispatch(): pl.pallas_call(functools.partial(sort_kernel, pieces, low, caps, flagged)...  2.79 us
    pallas_call x2, Pallas kernels, more(): pl.pallas_call(functools.partial(fill_kernel, first, caps[first:stop], fl...  1.84 us
  transfers between devices with their start and end apart: 20, of which 9 were waited for; matrix products, arithmetic and copies ran while one was open for 1% of the time, Pallas kernels for 19%

profile of v6, /device:TPU:0, one launch (start us, length us, event | category | flops | bytes accessed | tf_op | source)
XLA Modules:
  0.0 78.0 jit_solution(10826061084845880275)
XLA Ops:
  0.0 2.8 %sort.3 = (bf16[208,1024]{1,0:T(8,128)(2,1)S(1)}, bf16[768,1024]{1,0:T(8,128)(2,1)S(1)}, f32[8,768]{1,0:T(8,128)S(1)}, s32[8,128]{1,0:T(8,128)S(1)}) custom-call(bf16[768,1024]{1,0:T(8,128)(2,1)} %emb.1, s32[6,128]{1,0:T(8,128)} %bitcast.9, s32[6,128]{1,0:T(8,128)} %bitcast.11), custom_call_target="tpu_custom_call" | custom-call | tf_op jit(solution)/shard_map/sort/pallas_call | solution.py:157
  4.0 3.7 %collective-permute-start.21 = (bf16[208,1024]{1,0:T(8,128)(2,1)S(1)}, bf16[208,1024]{1,0:T(8,128)(2,1)S(1)}, u32[]{:S(2)}, u32[]{:S(2)}) collective-permute-start(bf16[208,1024]{1,0:T(8,128)(2,1)S(1)} %get-tuple-element.70), channel_id=1, source_target_pairs={{0,4},{1,5},{2,6},{3,7},{4,0},{5,1},{6,2},{7,3},{8,12},{9,13},{10,... | collective-permute-start | bytes 1277960 | tf_op jit(solution)/shard_map/ppermute | solution.py:384
  7.7 1.3 %collective-permute-start.27 = (bf16[208,1024]{1,0:T(8,128)(2,1)S(1)}, bf16[208,1024]{1,0:T(8,128)(2,1)S(1)}, u32[]{:S(2)}, u32[]{:S(2)}) collective-permute-start(bf16[208,1024]{1,0:T(8,128)(2,1)S(1)} %after.12.refs_1_), channel_id=1, source_target_pairs={{0,9},{1,0},{2,11},{3,2},{4,13},{5,4},{6,15},{7,6},{8,1},{9,8},{10... | collective-permute-start | bytes 1277960 | tf_op jit(solution)/shard_map/ppermute | solution.py:384
  9.0 1.4 %collective-permute-start.26 = (bf16[208,1024]{1,0:T(8,128)(2,1)S(1)}, bf16[208,1024]{1,0:T(8,128)(2,1)S(1)}, u32[]{:S(2)}, u32[]{:S(2)}) collective-permute-start(bf16[208,1024]{1,0:T(8,128)(2,1)S(1)} %after.12.refs_1_), channel_id=1, source_target_pairs={{0,24},{1,17},{2,26},{3,19},{4,28},{5,21},{6,30},{7,23},{8,16},{9,... | collective-permute-start | bytes 1277960 | tf_op jit(solution)/shard_map/ppermute | solution.py:384
  10.4 1.1 %fill2.3 = (bf16[208,1024]{1,0:T(8,128)(2,1)S(1)}, bf16[208,1024]{1,0:T(8,128)(2,1)S(1)}) custom-call(bf16[768,1024]{1,0:T(8,128)(2,1)S(1)} %get-tuple-element.67.emb, f32[8,768]{1,0:T(8,128)S(1)} %get-tuple-element.68.sorting), custom_call_target="tpu_custom_call" | custom-call | tf_op jit(solution)/shard_map/fill2/pallas_call | solution.py:179
  11.6 1.6 %collective-permute-start.31 = (bf16[208,1024]{1,0:T(8,128)(2,1)S(1)}, bf16[208,1024]{1,0:T(8,128)(2,1)S(1)}, u32[]{:S(2)}, u32[]{:S(2)}) collective-permute-start(bf16[208,1024]{1,0:T(8,128)(2,1)S(1)} %after.14), channel_id=1, source_target_pairs={{0,2},{1,3},{2,0},{3,1},{4,6},{5,7},{6,4},{7,5},{8,10},{9,11},{10,... | collective-permute-start | bytes 1277960 | tf_op jit(solution)/shard_map/ppermute | solution.py:384
  13.2 14.1 %collective-permute-done.21.refs_1_ = bf16[208,1024]{1,0:T(8,128)(2,1)S(1)} collective-permute-done((bf16[208,1024]{1,0:T(8,128)(2,1)S(1)}, bf16[208,1024]{1,0:T(8,128)(2,1)S(1)}, u32[]{:S(2)}, u32[]{:S(2)}) %collective-permute-start.21) | collective-permute-done | bytes 426016 | tf_op jit(solution)/shard_map/ppermute | solution.py:384
  27.3 1.7 %collective-permute-start.23 = (bf16[208,1024]{1,0:T(8,128)(2,1)S(1)}, bf16[208,1024]{1,0:T(8,128)(2,1)S(1)}, u32[]{:S(2)}, u32[]{:S(2)}) collective-permute-start(bf16[208,1024]{1,0:T(8,128)(2,1)S(1)} %collective-permute-done.21.refs_1_), channel_id=1, source_target_pairs={{0,9},{1,0},{2,11},{3,2},{4,13},{5,4},{6,15},{7,6},{8,1},{9,8},{10... | collective-permute-start | bytes 1277960 | tf_op jit(solution)/shard_map/ppermute | solution.py:384
  30.1 3.5 %collective-permute-start.20 = (bf16[208,1024]{1,0:T(8,128)(2,1)S(1)}, bf16[208,1024]{1,0:T(8,128)(2,1)S(1)}, u32[]{:S(2)}, u32[]{:S(2)}) collective-permute-start(bf16[208,1024]{1,0:T(8,128)(2,1)S(1)} %get-tuple-element.69), channel_id=1, source_target_pairs={{0,6},{1,7},{2,4},{3,5},{4,2},{5,3},{6,0},{7,1},{8,14},{9,15},{10,... | collective-permute-start | bytes 1277960 | tf_op jit(solution)/shard_map/ppermute | solution.py:384
  33.6 2.0 %stage0all.3 = (bf16[3456,1024]{1,0:T(8,128)(2,1)S(1)}, f32[8,4096]{1,0:T(8,128)S(1)}, f32[8,4224]{1,0:T(8,128)S(1)}, f32[8,128]{1,0:T(8,128)S(1)}) custom-call(bf16[208,1024]{1,0:T(8,128)(2,1)S(1)} %collective-permute-done.25.refs_1_.refs_0_.refs_3_, bf16[208,1024]{1,0:T(8,128)(2,1)S(1)} %after.12.refs_1_, ...), custom_call_target="tpu_custom_call" | custom-call | tf_op jit(solution)/shard_map/stage0all/pallas_call | solution.py:330
  36.6 3.4 %collective-permute-done.23.refs_3_.refs_2_ = bf16[208,1024]{1,0:T(8,128)(2,1)S(1)} collective-permute-done((bf16[208,1024]{1,0:T(8,128)(2,1)S(1)}, bf16[208,1024]{1,0:T(8,128)(2,1)S(1)}, u32[]{:S(2)}, u32[]{:S(2)}) %collective-permute-start.23) | collective-permute-done | bytes 426016 | tf_op jit(solution)/shard_map/ppermute | solution.py:384
  39.9 1.8 %collective-permute-done.22.refs_2_.refs_1_ = bf16[208,1024]{1,0:T(8,128)(2,1)S(1)} collective-permute-done((bf16[208,1024]{1,0:T(8,128)(2,1)S(1)}, bf16[208,1024]{1,0:T(8,128)(2,1)S(1)}, u32[]{:S(2)}, u32[]{:S(2)}) %collective-permute-start.22) | collective-permute-done | bytes 426016 | tf_op jit(solution)/shard_map/ppermute | solution.py:384
  41.7 3.1 %stage1all.3 = (bf16[3456,1024]{1,0:T(8,128)(2,1)S(1)}, f32[8,4096]{1,0:T(8,128)S(1)}, f32[8,4224]{1,0:T(8,128)S(1)}, f32[8,128]{1,0:T(8,128)S(1)}) custom-call(bf16[208,1024]{1,0:T(8,128)(2,1)S(1)} %collective-permute-done.24.refs_0_.refs_3_, ...), custom_call_target="tpu_custom_call", output_to_operand_aliasing={{0}: (4, {}), {1}: (5, {}), {2}: (6, {})} | custom-call | tf_op jit(solution)/shard_map/stage1all/pallas_call | solution.py:330
  45.2 3.9 %collective-permute-done.34.refs_3_ = bf16[208,1024]{1,0:T(8,128)(2,1)S(1)} collective-permute-done((bf16[208,1024]{1,0:T(8,128)(2,1)S(1)}, bf16[208,1024]{1,0:T(8,128)(2,1)S(1)}, u32[]{:S(2)}, u32[]{:S(2)}) %collective-permute-start.34) | collective-permute-done | bytes 426016 | tf_op jit(solution)/shard_map/ppermute | solution.py:384
  49.9 4.7 %stage2all.3 = (bf16[3456,1024]{1,0:T(8,128)(2,1)S(1)}, f32[8,4096]{1,0:T(8,128)S(1)}, f32[8,4224]{1,0:T(8,128)S(1)}, f32[8,128]{1,0:T(8,128)}) custom-call(bf16[208,1024]{1,0:T(8,128)(2,1)S(1)} %collective-permute-done.32.refs_0_, bf16[208,1024]{1,0:T(8,128)(2,1)S(1)} %after.15.refs_1_, ...), custom_call_target="tpu_custom_call", output_to_operand_aliasing={{0}: (4, {}), {1}: (5, {}), {2}: (6, {})} | custom-call | tf_op jit(solution)/shard_map/stage2all/pallas_call | solution.py:330
  54.7 3.6 %stage3home.3 = (bf16[3456,1024]{1,0:T(8,128)(2,1)S(1)}, f32[8,4096]{1,0:T(8,128)S(1)}, f32[8,4224]{1,0:T(8,128)S(1)}, f32[8,128]{1,0:T(8,128)}) custom-call(bf16[208,1024]{1,0:T(8,128)(2,1)S(1)} %collective-permute-done.30.refs_0_, bf16[208,1024]{1,0:T(8,128)(2,1)S(1)} %after.13.refs_1_, ...), custom_call_target="tpu_custom_call", output_to_operand_aliasing={{0}: (2, {}), {1}: (3, {}), {2}: (4, {})} | custom-call | tf_op jit(solution)/shard_map/stage3home/pallas_call | solution.py:330
  58.3 1.8 %collective-permute-done.28.refs_0_ = bf16[208,1024]{1,0:T(8,128)(2,1)S(1)} collective-permute-done((bf16[208,1024]{1,0:T(8,128)(2,1)S(1)}, bf16[208,1024]{1,0:T(8,128)(2,1)S(1)}, u32[]{:S(2)}, u32[]{:S(2)}) %collective-permute-start.28) | collective-permute-done | bytes 426016 | tf_op jit(solution)/shard_map/ppermute | solution.py:384
  60.1 2.8 %stage3away.3 = (bf16[3456,1024]{1,0:T(8,128)(2,1)S(1)}, f32[8,4096]{1,0:T(8,128)S(1)}, f32[8,4224]{1,0:T(8,128)S(1)}, f32[8,128]{1,0:T(8,128)}, f32[1,1152]{1,0...) custom-call(bf16[208,1024]{1,0:T(8,128)(2,1)S(1)} %collective-permut, ...), custom_call_target="tpu_custom_call", output_to_operand_aliasing={{0}: (2, {}), {1}: (3, {}), {2}: (4, {})} | custom-call | tf_op jit(solution)/shard_map/stage3away/pallas_call | solution.py:330
  63.0 1.5 %collective-permute-start.35 = (f32[1,1152]{1,0:T(1,128)S(1)}, f32[1,1152]{1,0:T(1,128)S(1)}, u32[]{:S(2)}, u32[]{:S(2)}) collective-permute-start(f32[1,1152]{1,0:T(1,128)S(1)} %get-tuple-element.87), channel_id=1, source_target_pairs={{0,1},{1,8},{2,3},{3,10},{4,5},{5,12},{6,7},{7,14},{8,9},{9,0},{10... | collective-permute-start | bytes 13832 | tf_op jit(solution)/shard_map/ppermute | solution.py:384
  64.5 1.8 %collective-permute-start.36 = (f32[1,1152]{1,0:T(1,128)S(1)}, f32[1,1152]{1,0:T(1,128)S(1)}, u32[]{:S(2)}, u32[]{:S(2)}) collective-permute-start(f32[1,1152]{1,0:T(1,128)S(1)} %get-tuple-element.88), channel_id=1, source_target_pairs={{0,16},{1,25},{2,18},{3,27},{4,20},{5,29},{6,22},{7,31},{8,24},{9,... | collective-permute-start | bytes 13832 | tf_op jit(solution)/shard_map/ppermute | solution.py:384
  66.2 1.3 %collective-permute-done.36 = f32[1,1152]{1,0:T(1,128)S(1)} collective-permute-done((f32[1,1152]{1,0:T(1,128)S(1)}, f32[1,1152]{1,0:T(1,128)S(1)}, u32[]{:S(2)}, u32[]{:S(2)}) %collective-permute-start.36) | collective-permute-done | bytes 4640 | tf_op jit(solution)/shard_map/ppermute | solution.py:384
  67.6 3.6 %collective-permute-start.39 = (f32[1,1152]{1,0:T(1,128)S(1)}, f32[1,1152]{1,0:T(1,128)S(1)}, u32[]{:S(2)}, u32[]{:S(2)}) collective-permute-start(f32[1,1152]{1,0:T(1,128)S(1)} %maximum_maximum_fusion.1.refs_0_), channel_id=1, source_target_pairs={{0,6},{1,7},{2,4},{3,5},{4,2},{5,3},{6,0},{7,1},{8,14},{9,15},{10,... | collective-permute-start | bytes 13832 | tf_op jit(solution)/shard_map/ppermute | solution.py:384
  71.1 2.3 %collective-permute-start.38 = (f32[1,1152]{1,0:T(1,128)S(1)}, f32[1,1152]{1,0:T(1,128)S(1)}, u32[]{:S(2)}, u32[]{:S(2)}) collective-permute-start(f32[1,1152]{1,0:T(1,128)S(1)} %maximum_maximum_fusion.1.refs_0_), channel_id=1, source_target_pairs={{0,4},{1,5},{2,6},{3,7},{4,0},{5,1},{6,2},{7,3},{8,12},{9,13},{10,... | collective-permute-start | bytes 13832 | tf_op jit(solution)/shard_map/ppermute | solution.py:384
  75.7 1.4 %collective-permute-done.37.refs_1_ = f32[1,1152]{1,0:T(1,128)S(1)} collective-permute-done((f32[1,1152]{1,0:T(1,128)S(1)}, f32[1,1152]{1,0:T(1,128)S(1)}, u32[]{:S(2)}, u32[]{:S(2)}) %collective-permute-start.37) | collective-permute-done | bytes 4640 | tf_op jit(solution)/shard_map/ppermute | solution.py:384
  (41 shorter events, 6.9 us)
Async XLA Ops:
  3.5 4.2 %collective-permute-start.25 = (bf16[208,1024]{1,0:T(8,128)(2,1)S(1)}, bf16[208,1024]{1,0:T(8,128)(2,1)S(1)}, u32[]{:S(2)}, u32[]{:S(2)}) collective-permute-start(bf16[208,1024]{1,0:T(8,128)(2,1)S(1)} %fill0.3.refs_0_), channel_id=1, source_target_pairs={{0,8},{1,9},{2,10},{3,11},{4,12},{5,13},{6,14},{7,15},{8,0},{9,1},... | collective-permute-start | bytes 1277960 | tf_op jit(solution)/shard_map/ppermute | solution.py:384
  4.0 23.3 %collective-permute-start.21 = (bf16[208,1024]{1,0:T(8,128)(2,1)S(1)}, bf16[208,1024]{1,0:T(8,128)(2,1)S(1)}, u32[]{:S(2)}, u32[]{:S(2)}) collective-permute-start(bf16[208,1024]{1,0:T(8,128)(2,1)S(1)} %get-tuple-element.70), channel_id=1, source_target_pairs={{0,4},{1,5},{2,6},{3,7},{4,0},{5,1},{6,2},{7,3},{8,12},{9,13},{10,... | collective-permute-start | bytes 1277960 | tf_op jit(solution)/shard_map/ppermute | solution.py:384
  7.7 21.4 %collective-permute-start.27 = (bf16[208,1024]{1,0:T(8,128)(2,1)S(1)}, bf16[208,1024]{1,0:T(8,128)(2,1)S(1)}, u32[]{:S(2)}, u32[]{:S(2)}) collective-permute-start(bf16[208,1024]{1,0:T(8,128)(2,1)S(1)} %after.12.refs_1_), channel_id=1, source_target_pairs={{0,9},{1,0},{2,11},{3,2},{4,13},{5,4},{6,15},{7,6},{8,1},{9,8},{10... | collective-permute-start | bytes 1277960 | tf_op jit(solution)/shard_map/ppermute | solution.py:384
  9.0 21.2 %collective-permute-start.26 = (bf16[208,1024]{1,0:T(8,128)(2,1)S(1)}, bf16[208,1024]{1,0:T(8,128)(2,1)S(1)}, u32[]{:S(2)}, u32[]{:S(2)}) collective-permute-start(bf16[208,1024]{1,0:T(8,128)(2,1)S(1)} %after.12.refs_1_), channel_id=1, source_target_pairs={{0,24},{1,17},{2,26},{3,19},{4,28},{5,21},{6,30},{7,23},{8,16},{9,... | collective-permute-start | bytes 1277960 | tf_op jit(solution)/shard_map/ppermute | solution.py:384
  11.6 24.1 %collective-permute-start.31 = (bf16[208,1024]{1,0:T(8,128)(2,1)S(1)}, bf16[208,1024]{1,0:T(8,128)(2,1)S(1)}, u32[]{:S(2)}, u32[]{:S(2)}) collective-permute-start(bf16[208,1024]{1,0:T(8,128)(2,1)S(1)} %after.14), channel_id=1, source_target_pairs={{0,2},{1,3},{2,0},{3,1},{4,6},{5,7},{6,4},{7,5},{8,10},{9,11},{10,... | collective-permute-start | bytes 1277960 | tf_op jit(solution)/shard_map/ppermute | solution.py:384
  27.3 8.4 %collective-permute-start.24 = (bf16[208,1024]{1,0:T(8,128)(2,1)S(1)}, bf16[208,1024]{1,0:T(8,128)(2,1)S(1)}, u32[]{:S(2)}, u32[]{:S(2)}) collective-permute-start(bf16[208,1024]{1,0:T(8,128)(2,1)S(1)} %collective-permute-done.21.refs_1_), channel_id=1, source_target_pairs={{0,8},{1,9},{2,10},{3,11},{4,12},{5,13},{6,14},{7,15},{8,0},{9,1},... | collective-permute-start | bytes 1277960 | tf_op jit(solution)/shard_map/ppermute | solution.py:384
  27.3 12.6 %collective-permute-start.23 = (bf16[208,1024]{1,0:T(8,128)(2,1)S(1)}, bf16[208,1024]{1,0:T(8,128)(2,1)S(1)}, u32[]{:S(2)}, u32[]{:S(2)}) collective-permute-start(bf16[208,1024]{1,0:T(8,128)(2,1)S(1)} %collective-permute-done.21.refs_1_), channel_id=1, source_target_pairs={{0,9},{1,0},{2,11},{3,2},{4,13},{5,4},{6,15},{7,6},{8,1},{9,8},{10... | collective-permute-start | bytes 1277960 | tf_op jit(solution)/shard_map/ppermute | solution.py:384
  29.0 12.7 %collective-permute-start.22 = (bf16[208,1024]{1,0:T(8,128)(2,1)S(1)}, bf16[208,1024]{1,0:T(8,128)(2,1)S(1)}, u32[]{:S(2)}, u32[]{:S(2)}) collective-permute-start(bf16[208,1024]{1,0:T(8,128)(2,1)S(1)} %collective-permute-done.21.refs_1_), channel_id=1, source_target_pairs={{0,24},{1,17},{2,26},{3,19},{4,28},{5,21},{6,30},{7,23},{8,16},{9,... | collective-permute-start | bytes 1277960 | tf_op jit(solution)/shard_map/ppermute | solution.py:384
  30.1 14.7 %collective-permute-start.20 = (bf16[208,1024]{1,0:T(8,128)(2,1)S(1)}, bf16[208,1024]{1,0:T(8,128)(2,1)S(1)}, u32[]{:S(2)}, u32[]{:S(2)}) collective-permute-start(bf16[208,1024]{1,0:T(8,128)(2,1)S(1)} %get-tuple-element.69), channel_id=1, source_target_pairs={{0,6},{1,7},{2,4},{3,5},{4,2},{5,3},{6,0},{7,1},{8,14},{9,15},{10,... | collective-permute-start | bytes 1277960 | tf_op jit(solution)/shard_map/ppermute | solution.py:384
  35.7 13.4 %collective-permute-start.34 = (bf16[208,1024]{1,0:T(8,128)(2,1)S(1)}, bf16[208,1024]{1,0:T(8,128)(2,1)S(1)}, u32[]{:S(2)}, u32[]{:S(2)}) collective-permute-start(bf16[208,1024]{1,0:T(8,128)(2,1)S(1)} %after.15.refs_1_), channel_id=1, source_target_pairs={{0,9},{1,0},{2,11},{3,2},{4,13},{5,4},{6,15},{7,6},{8,1},{9,8},{10... | collective-permute-start | bytes 1277960 | tf_op jit(solution)/shard_map/ppermute | solution.py:384
  35.8 14.1 %collective-permute-start.33 = (bf16[208,1024]{1,0:T(8,128)(2,1)S(1)}, bf16[208,1024]{1,0:T(8,128)(2,1)S(1)}, u32[]{:S(2)}, u32[]{:S(2)}) collective-permute-start(bf16[208,1024]{1,0:T(8,128)(2,1)S(1)} %after.15.refs_1_), channel_id=1, source_target_pairs={{0,24},{1,17},{2,26},{3,19},{4,28},{5,21},{6,30},{7,23},{8,16},{9,... | collective-permute-start | bytes 1277960 | tf_op jit(solution)/shard_map/ppermute | solution.py:384
  39.9 10.0 %collective-permute-start.32 = (bf16[208,1024]{1,0:T(8,128)(2,1)S(1)}, bf16[208,1024]{1,0:T(8,128)(2,1)S(1)}, u32[]{:S(2)}, u32[]{:S(2)}) collective-permute-start(bf16[208,1024]{1,0:T(8,128)(2,1)S(1)} %after.15.refs_1_), channel_id=1, source_target_pairs={{0,8},{1,9},{2,10},{3,11},{4,12},{5,13},{6,14},{7,15},{8,0},{9,1},... | collective-permute-start | bytes 1277960 | tf_op jit(solution)/shard_map/ppermute | solution.py:384
  44.9 9.7 %collective-permute-start.30 = (bf16[208,1024]{1,0:T(8,128)(2,1)S(1)}, bf16[208,1024]{1,0:T(8,128)(2,1)S(1)}, u32[]{:S(2)}, u32[]{:S(2)}) collective-permute-start(bf16[208,1024]{1,0:T(8,128)(2,1)S(1)} %after.13.refs_1_), channel_id=1, source_target_pairs={{0,8},{1,9},{2,10},{3,11},{4,12},{5,13},{6,14},{7,15},{8,0},{9,1},... | collective-permute-start | bytes 1277960 | tf_op jit(solution)/shard_map/ppermute | solution.py:384
  44.9 13.3 %collective-permute-start.29 = (bf16[208,1024]{1,0:T(8,128)(2,1)S(1)}, bf16[208,1024]{1,0:T(8,128)(2,1)S(1)}, u32[]{:S(2)}, u32[]{:S(2)}) collective-permute-start(bf16[208,1024]{1,0:T(8,128)(2,1)S(1)} %after.13.refs_1_), channel_id=1, source_target_pairs={{0,9},{1,0},{2,11},{3,2},{4,13},{5,4},{6,15},{7,6},{8,1},{9,8},{10... | collective-permute-start | bytes 1277960 | tf_op jit(solution)/shard_map/ppermute | solution.py:384
  49.1 11.1 %collective-permute-start.28 = (bf16[208,1024]{1,0:T(8,128)(2,1)S(1)}, bf16[208,1024]{1,0:T(8,128)(2,1)S(1)}, u32[]{:S(2)}, u32[]{:S(2)}) collective-permute-start(bf16[208,1024]{1,0:T(8,128)(2,1)S(1)} %after.13.refs_1_), channel_id=1, source_target_pairs={{0,24},{1,17},{2,26},{3,19},{4,28},{5,21},{6,30},{7,23},{8,16},{9,... | collective-permute-start | bytes 1277960 | tf_op jit(solution)/shard_map/ppermute | solution.py:384
  54.6 22.5 %copy-start = (bf16[768,1024]{1,0:T(8,128)(2,1)S(1)}, bf16[768,1024]{1,0:T(8,128)(2,1)}, u32[]{:S(2)}) copy-start(bf16[768,1024]{1,0:T(8,128)(2,1)} %emb.1) | copy-start | bytes 4718596
  54.6 22.5 %copy-start.1 = (s32[768]{0:T(1024)S(1)}, s32[768]{0:T(1024)}, u32[]{:S(2)}) copy-start(s32[768]{0:T(1024)} %param.6) | copy-start | bytes 9220
  54.6 22.5 %copy-start.2 = (s32[768]{0:T(1024)S(1)}, s32[768]{0:T(1024)}, u32[]{:S(2)}) copy-start(s32[768]{0:T(1024)} %param.7) | copy-start | bytes 9220
  63.0 3.3 %collective-permute-start.35 = (f32[1,1152]{1,0:T(1,128)S(1)}, f32[1,1152]{1,0:T(1,128)S(1)}, u32[]{:S(2)}, u32[]{:S(2)}) collective-permute-start(f32[1,1152]{1,0:T(1,128)S(1)} %get-tuple-element.87), channel_id=1, source_target_pairs={{0,1},{1,8},{2,3},{3,10},{4,5},{5,12},{6,7},{7,14},{8,9},{9,0},{10... | collective-permute-start | bytes 13832 | tf_op jit(solution)/shard_map/ppermute | solution.py:384
  64.5 3.1 %collective-permute-start.36 = (f32[1,1152]{1,0:T(1,128)S(1)}, f32[1,1152]{1,0:T(1,128)S(1)}, u32[]{:S(2)}, u32[]{:S(2)}) collective-permute-start(f32[1,1152]{1,0:T(1,128)S(1)} %get-tuple-element.88), channel_id=1, source_target_pairs={{0,16},{1,25},{2,18},{3,27},{4,20},{5,29},{6,22},{7,31},{8,24},{9,... | collective-permute-start | bytes 13832 | tf_op jit(solution)/shard_map/ppermute | solution.py:384
  67.6 7.1 %collective-permute-start.39 = (f32[1,1152]{1,0:T(1,128)S(1)}, f32[1,1152]{1,0:T(1,128)S(1)}, u32[]{:S(2)}, u32[]{:S(2)}) collective-permute-start(f32[1,1152]{1,0:T(1,128)S(1)} %maximum_maximum_fusion.1.refs_0_), channel_id=1, source_target_pairs={{0,6},{1,7},{2,4},{3,5},{4,2},{5,3},{6,0},{7,1},{8,14},{9,15},{10,... | collective-permute-start | bytes 13832 | tf_op jit(solution)/shard_map/ppermute | solution.py:384
  71.1 4.5 %collective-permute-start.38 = (f32[1,1152]{1,0:T(1,128)S(1)}, f32[1,1152]{1,0:T(1,128)S(1)}, u32[]{:S(2)}, u32[]{:S(2)}) collective-permute-start(f32[1,1152]{1,0:T(1,128)S(1)} %maximum_maximum_fusion.1.refs_0_), channel_id=1, source_target_pairs={{0,4},{1,5},{2,6},{3,7},{4,0},{5,1},{6,2},{7,3},{8,12},{9,13},{10,... | collective-permute-start | bytes 13832 | tf_op jit(solution)/shard_map/ppermute | solution.py:384
  73.4 3.6 %collective-permute-start.37 = (f32[1,1152]{1,0:T(1,128)S(1)}, f32[1,1152]{1,0:T(1,128)S(1)}, u32[]{:S(2)}, u32[]{:S(2)}) collective-permute-start(f32[1,1152]{1,0:T(1,128)S(1)} %maximum_maximum_fusion.1.refs_0_), channel_id=1, source_target_pairs={{0,2},{1,3},{2,0},{3,1},{4,6},{5,7},{6,4},{7,5},{8,10},{9,11},{10,... | collective-permute-start | bytes 13832 | tf_op jit(solution)/shard_map/ppermute | solution.py:384
  77.4 0.6 copy-start.3

commit v7 on v6

--- a/solution.py
+++ b/solution.py
@@ -61,7 +61,7 @@
     return jnp.concatenate([ref[b : b + 1, :] for b in range(ref.shape[0])], axis=1)
 
 
-def fill(first, caps, flagged, outs, emb, sorting, pick, raw):
+def fill(first, caps, flagged, outs, emb, sorting, pick, raw, copies=()):
     rows, width = emb.shape
     target = sorting[0:1, :].astype(jnp.int32)
     digits = jnp.concatenate([sorting[...], jnp.zeros((8, rows), jnp.float32)], axis=0)
@@ -81,6 +81,8 @@
         if used < width:
             parts.append(jnp.zeros((1, width - used), jnp.float32))
         notes.append(jnp.concatenate(parts, axis=1))
+    for copy in copies:
+        copy.wait()
     for at in range(0, width, 256):
         lanes = slice(at, at + 256)
         raw[:, lanes] = jnp.dot(pick[...], emb[:, lanes], preferred_element_type=jnp.float32)
@@ -141,9 +143,7 @@
     sorting[4:5, :] = jnp.broadcast_to(full, (1, rows))
     sorting[5:8, :] = jnp.zeros((3, rows), jnp.float32)
 
-    for copy in copies:
-        copy.wait()
-    fill(1, caps[1:2], flagged, [out], held, sorting, pick, raw)
+    fill(1, caps[1:2], flagged, [out], held, sorting, pick, raw, copies)
 
 
 def fill_kernel(first, caps, flagged, emb, sorting, *refs):

time: 78.2 us -> 78.5 us (level)
  no operation moved by 1% of the time
where the time goes in v7:
time: 78.5 us; the launch traced here: 78.3 us
  waiting for transfers between devices  29 us (37%)
  starting transfers between devices  25.7 us (33%)
  Pallas kernels  21.3 us (27%)
  local copies, waits for them, and re-layouts  1.19 us (2%)
  between operations  0.87 us (1%)
    ppermute x20, waiting for transfers between devices, send(): return lax.ppermute(block, AXES, route)  29 us
    ppermute x20, starting transfers between devices, send(): return lax.ppermute(block, AXES, route)  25.7 us
    pallas_call x5, Pallas kernels, stage(): pl.pallas_call(functools.partial(stage_kernel, p, part, caps, groups, fla...  16.3 us
    pallas_call x1, Pallas kernels, dispatch(): pl.pallas_call(functools.partial(sort_kernel, pieces, low, caps, flagged)...  3.08 us
    pallas_call x2, Pallas kernels, more(): pl.pallas_call(functools.partial(fill_kernel, first, caps[first:stop], fl...  1.83 us
  transfers between devices with their start and end apart: 20, of which 9 were waited for; matrix products, arithmetic and copies ran while one was open for 1% of the time, Pallas kernels for 19%

profile of v7, /device:TPU:0, one launch (start us, length us, event | category | flops | bytes accessed | tf_op | source)
XLA Modules:
  0.0 78.3 jit_solution(11186767497089596794)
XLA Ops:
  0.0 3.1 %sort.3 = (bf16[208,1024]{1,0:T(8,128)(2,1)S(1)}, bf16[768,1024]{1,0:T(8,128)(2,1)S(1)}, f32[8,768]{1,0:T(8,128)S(1)}, s32[8,128]{1,0:T(8,128)S(1)}) custom-call(bf16[768,1024]{1,0:T(8,128)(2,1)} %emb.1, s32[6,128]{1,0:T(8,128)} %bitcast.9, s32[6,128]{1,0:T(8,128)} %bitcast.11), custom_call_target="tpu_custom_call" | custom-call | tf_op jit(solution)/shard_map/sort/pallas_call | solution.py:157
  4.3 3.7 %collective-permute-start.21 = (bf16[208,1024]{1,0:T(8,128)(2,1)S(1)}, bf16[208,1024]{1,0:T(8,128)(2,1)S(1)}, u32[]{:S(2)}, u32[]{:S(2)}) collective-permute-start(bf16[208,1024]{1,0:T(8,128)(2,1)S(1)} %get-tuple-element.70), channel_id=1, source_target_pairs={{0,4},{1,5},{2,6},{3,7},{4,0},{5,1},{6,2},{7,3},{8,12},{9,13},{10,... | collective-permute-start | bytes 1277960 | tf_op jit(solution)/shard_map/ppermute | solution.py:384
  8.0 1.3 %collective-permute-start.27 = (bf16[208,1024]{1,0:T(8,128)(2,1)S(1)}, bf16[208,1024]{1,0:T(8,128)(2,1)S(1)}, u32[]{:S(2)}, u32[]{:S(2)}) collective-permute-start(bf16[208,1024]{1,0:T(8,128)(2,1)S(1)} %after.12.refs_1_), channel_id=1, source_target_pairs={{0,9},{1,0},{2,11},{3,2},{4,13},{5,4},{6,15},{7,6},{8,1},{9,8},{10... | collective-permute-start | bytes 1277960 | tf_op jit(solution)/shard_map/ppermute | solution.py:384
  9.3 1.4 %collective-permute-start.26 = (bf16[208,1024]{1,0:T(8,128)(2,1)S(1)}, bf16[208,1024]{1,0:T(8,128)(2,1)S(1)}, u32[]{:S(2)}, u32[]{:S(2)}) collective-permute-start(bf16[208,1024]{1,0:T(8,128)(2,1)S(1)} %after.12.refs_1_), channel_id=1, source_target_pairs={{0,24},{1,17},{2,26},{3,19},{4,28},{5,21},{6,30},{7,23},{8,16},{9,... | collective-permute-start | bytes 1277960 | tf_op jit(solution)/shard_map/ppermute | solution.py:384
  10.7 1.1 %fill2.3 = (bf16[208,1024]{1,0:T(8,128)(2,1)S(1)}, bf16[208,1024]{1,0:T(8,128)(2,1)S(1)}) custom-call(bf16[768,1024]{1,0:T(8,128)(2,1)S(1)} %get-tuple-element.67.emb, f32[8,768]{1,0:T(8,128)S(1)} %get-tuple-element.68.sorting), custom_call_target="tpu_custom_call" | custom-call | tf_op jit(solution)/shard_map/fill2/pallas_call | solution.py:179
  11.9 1.6 %collective-permute-start.31 = (bf16[208,1024]{1,0:T(8,128)(2,1)S(1)}, bf16[208,1024]{1,0:T(8,128)(2,1)S(1)}, u32[]{:S(2)}, u32[]{:S(2)}) collective-permute-start(bf16[208,1024]{1,0:T(8,128)(2,1)S(1)} %after.14), channel_id=1, source_target_pairs={{0,2},{1,3},{2,0},{3,1},{4,6},{5,7},{6,4},{7,5},{8,10},{9,11},{10,... | collective-permute-start | bytes 1277960 | tf_op jit(solution)/shard_map/ppermute | solution.py:384
  13.5 14.1 %collective-permute-done.21.refs_1_ = bf16[208,1024]{1,0:T(8,128)(2,1)S(1)} collective-permute-done((bf16[208,1024]{1,0:T(8,128)(2,1)S(1)}, bf16[208,1024]{1,0:T(8,128)(2,1)S(1)}, u32[]{:S(2)}, u32[]{:S(2)}) %collective-permute-start.21) | collective-permute-done | bytes 426016 | tf_op jit(solution)/shard_map/ppermute | solution.py:384
  27.6 1.7 %collective-permute-start.23 = (bf16[208,1024]{1,0:T(8,128)(2,1)S(1)}, bf16[208,1024]{1,0:T(8,128)(2,1)S(1)}, u32[]{:S(2)}, u32[]{:S(2)}) collective-permute-start(bf16[208,1024]{1,0:T(8,128)(2,1)S(1)} %collective-permute-done.21.refs_1_), channel_id=1, source_target_pairs={{0,9},{1,0},{2,11},{3,2},{4,13},{5,4},{6,15},{7,6},{8,1},{9,8},{10... | collective-permute-start | bytes 1277960 | tf_op jit(solution)/shard_map/ppermute | solution.py:384
  30.4 3.5 %collective-permute-start.20 = (bf16[208,1024]{1,0:T(8,128)(2,1)S(1)}, bf16[208,1024]{1,0:T(8,128)(2,1)S(1)}, u32[]{:S(2)}, u32[]{:S(2)}) collective-permute-start(bf16[208,1024]{1,0:T(8,128)(2,1)S(1)} %get-tuple-element.69), channel_id=1, source_target_pairs={{0,6},{1,7},{2,4},{3,5},{4,2},{5,3},{6,0},{7,1},{8,14},{9,15},{10,... | collective-permute-start | bytes 1277960 | tf_op jit(solution)/shard_map/ppermute | solution.py:384
  33.9 2.0 %stage0all.3 = (bf16[3456,1024]{1,0:T(8,128)(2,1)S(1)}, f32[8,4096]{1,0:T(8,128)S(1)}, f32[8,4224]{1,0:T(8,128)S(1)}, f32[8,128]{1,0:T(8,128)S(1)}) custom-call(bf16[208,1024]{1,0:T(8,128)(2,1)S(1)} %collective-permute-done.25.refs_1_.refs_0_.refs_3_, bf16[208,1024]{1,0:T(8,128)(2,1)S(1)} %after.12.refs_1_, ...), custom_call_target="tpu_custom_call" | custom-call | tf_op jit(solution)/shard_map/stage0all/pallas_call | solution.py:330
  36.9 3.4 %collective-permute-done.23.refs_3_.refs_2_ = bf16[208,1024]{1,0:T(8,128)(2,1)S(1)} collective-permute-done((bf16[208,1024]{1,0:T(8,128)(2,1)S(1)}, bf16[208,1024]{1,0:T(8,128)(2,1)S(1)}, u32[]{:S(2)}, u32[]{:S(2)}) %collective-permute-start.23) | collective-permute-done | bytes 426016 | tf_op jit(solution)/shard_map/ppermute | solution.py:384
  40.2 1.8 %collective-permute-done.22.refs_2_.refs_1_ = bf16[208,1024]{1,0:T(8,128)(2,1)S(1)} collective-permute-done((bf16[208,1024]{1,0:T(8,128)(2,1)S(1)}, bf16[208,1024]{1,0:T(8,128)(2,1)S(1)}, u32[]{:S(2)}, u32[]{:S(2)}) %collective-permute-start.22) | collective-permute-done | bytes 426016 | tf_op jit(solution)/shard_map/ppermute | solution.py:384
  42.0 3.1 %stage1all.3 = (bf16[3456,1024]{1,0:T(8,128)(2,1)S(1)}, f32[8,4096]{1,0:T(8,128)S(1)}, f32[8,4224]{1,0:T(8,128)S(1)}, f32[8,128]{1,0:T(8,128)S(1)}) custom-call(bf16[208,1024]{1,0:T(8,128)(2,1)S(1)} %collective-permute-done.24.refs_0_.refs_3_, ...), custom_call_target="tpu_custom_call", output_to_operand_aliasing={{0}: (4, {}), {1}: (5, {}), {2}: (6, {})} | custom-call | tf_op jit(solution)/shard_map/stage1all/pallas_call | solution.py:330
  45.4 3.9 %collective-permute-done.34.refs_3_ = bf16[208,1024]{1,0:T(8,128)(2,1)S(1)} collective-permute-done((bf16[208,1024]{1,0:T(8,128)(2,1)S(1)}, bf16[208,1024]{1,0:T(8,128)(2,1)S(1)}, u32[]{:S(2)}, u32[]{:S(2)}) %collective-permute-start.34) | collective-permute-done | bytes 426016 | tf_op jit(solution)/shard_map/ppermute | solution.py:384
  50.2 4.7 %stage2all.3 = (bf16[3456,1024]{1,0:T(8,128)(2,1)S(1)}, f32[8,4096]{1,0:T(8,128)S(1)}, f32[8,4224]{1,0:T(8,128)S(1)}, f32[8,128]{1,0:T(8,128)}) custom-call(bf16[208,1024]{1,0:T(8,128)(2,1)S(1)} %collective-permute-done.32.refs_0_, bf16[208,1024]{1,0:T(8,128)(2,1)S(1)} %after.15.refs_1_, ...), custom_call_target="tpu_custom_call", output_to_operand_aliasing={{0}: (4, {}), {1}: (5, {}), {2}: (6, {})} | custom-call | tf_op jit(solution)/shard_map/stage2all/pallas_call | solution.py:330
  55.0 3.6 %stage3home.3 = (bf16[3456,1024]{1,0:T(8,128)(2,1)S(1)}, f32[8,4096]{1,0:T(8,128)S(1)}, f32[8,4224]{1,0:T(8,128)S(1)}, f32[8,128]{1,0:T(8,128)}) custom-call(bf16[208,1024]{1,0:T(8,128)(2,1)S(1)} %collective-permute-done.30.refs_0_, bf16[208,1024]{1,0:T(8,128)(2,1)S(1)} %after.13.refs_1_, ...), custom_call_target="tpu_custom_call", output_to_operand_aliasing={{0}: (2, {}), {1}: (3, {}), {2}: (4, {})} | custom-call | tf_op jit(solution)/shard_map/stage3home/pallas_call | solution.py:330
  58.6 1.8 %collective-permute-done.28.refs_0_ = bf16[208,1024]{1,0:T(8,128)(2,1)S(1)} collective-permute-done((bf16[208,1024]{1,0:T(8,128)(2,1)S(1)}, bf16[208,1024]{1,0:T(8,128)(2,1)S(1)}, u32[]{:S(2)}, u32[]{:S(2)}) %collective-permute-start.28) | collective-permute-done | bytes 426016 | tf_op jit(solution)/shard_map/ppermute | solution.py:384
  60.4 2.8 %stage3away.3 = (bf16[3456,1024]{1,0:T(8,128)(2,1)S(1)}, f32[8,4096]{1,0:T(8,128)S(1)}, f32[8,4224]{1,0:T(8,128)S(1)}, f32[8,128]{1,0:T(8,128)}, f32[1,1152]{1,0...) custom-call(bf16[208,1024]{1,0:T(8,128)(2,1)S(1)} %collective-permut, ...), custom_call_target="tpu_custom_call", output_to_operand_aliasing={{0}: (2, {}), {1}: (3, {}), {2}: (4, {})} | custom-call | tf_op jit(solution)/shard_map/stage3away/pallas_call | solution.py:330
  63.3 1.5 %collective-permute-start.35 = (f32[1,1152]{1,0:T(1,128)S(1)}, f32[1,1152]{1,0:T(1,128)S(1)}, u32[]{:S(2)}, u32[]{:S(2)}) collective-permute-start(f32[1,1152]{1,0:T(1,128)S(1)} %get-tuple-element.87), channel_id=1, source_target_pairs={{0,1},{1,8},{2,3},{3,10},{4,5},{5,12},{6,7},{7,14},{8,9},{9,0},{10... | collective-permute-start | bytes 13832 | tf_op jit(solution)/shard_map/ppermute | solution.py:384
  64.8 1.8 %collective-permute-start.36 = (f32[1,1152]{1,0:T(1,128)S(1)}, f32[1,1152]{1,0:T(1,128)S(1)}, u32[]{:S(2)}, u32[]{:S(2)}) collective-permute-start(f32[1,1152]{1,0:T(1,128)S(1)} %get-tuple-element.88), channel_id=1, source_target_pairs={{0,16},{1,25},{2,18},{3,27},{4,20},{5,29},{6,22},{7,31},{8,24},{9,... | collective-permute-start | bytes 13832 | tf_op jit(solution)/shard_map/ppermute | solution.py:384
  66.5 1.3 %collective-permute-done.36 = f32[1,1152]{1,0:T(1,128)S(1)} collective-permute-done((f32[1,1152]{1,0:T(1,128)S(1)}, f32[1,1152]{1,0:T(1,128)S(1)}, u32[]{:S(2)}, u32[]{:S(2)}) %collective-permute-start.36) | collective-permute-done | bytes 4640 | tf_op jit(solution)/shard_map/ppermute | solution.py:384
  67.9 3.6 %collective-permute-start.39 = (f32[1,1152]{1,0:T(1,128)S(1)}, f32[1,1152]{1,0:T(1,128)S(1)}, u32[]{:S(2)}, u32[]{:S(2)}) collective-permute-start(f32[1,1152]{1,0:T(1,128)S(1)} %maximum_maximum_fusion.1.refs_0_), channel_id=1, source_target_pairs={{0,6},{1,7},{2,4},{3,5},{4,2},{5,3},{6,0},{7,1},{8,14},{9,15},{10,... | collective-permute-start | bytes 13832 | tf_op jit(solution)/shard_map/ppermute | solution.py:384
  71.4 2.3 %collective-permute-start.38 = (f32[1,1152]{1,0:T(1,128)S(1)}, f32[1,1152]{1,0:T(1,128)S(1)}, u32[]{:S(2)}, u32[]{:S(2)}) collective-permute-start(f32[1,1152]{1,0:T(1,128)S(1)} %maximum_maximum_fusion.1.refs_0_), channel_id=1, source_target_pairs={{0,4},{1,5},{2,6},{3,7},{4,0},{5,1},{6,2},{7,3},{8,12},{9,13},{10,... | collective-permute-start | bytes 13832 | tf_op jit(solution)/shard_map/ppermute | solution.py:384
  76.0 1.4 %collective-permute-done.37.refs_1_ = f32[1,1152]{1,0:T(1,128)S(1)} collective-permute-done((f32[1,1152]{1,0:T(1,128)S(1)}, f32[1,1152]{1,0:T(1,128)S(1)}, u32[]{:S(2)}, u32[]{:S(2)}) %collective-permute-start.37) | collective-permute-done | bytes 4640 | tf_op jit(solution)/shard_map/ppermute | solution.py:384
  (41 shorter events, 6.9 us)
Async XLA Ops:
  3.8 4.2 %collective-permute-start.25 = (bf16[208,1024]{1,0:T(8,128)(2,1)S(1)}, bf16[208,1024]{1,0:T(8,128)(2,1)S(1)}, u32[]{:S(2)}, u32[]{:S(2)}) collective-permute-start(bf16[208,1024]{1,0:T(8,128)(2,1)S(1)} %fill0.3.refs_0_), channel_id=1, source_target_pairs={{0,8},{1,9},{2,10},{3,11},{4,12},{5,13},{6,14},{7,15},{8,0},{9,1},... | collective-permute-start | bytes 1277960 | tf_op jit(solution)/shard_map/ppermute | solution.py:384
  4.3 23.3 %collective-permute-start.21 = (bf16[208,1024]{1,0:T(8,128)(2,1)S(1)}, bf16[208,1024]{1,0:T(8,128)(2,1)S(1)}, u32[]{:S(2)}, u32[]{:S(2)}) collective-permute-start(bf16[208,1024]{1,0:T(8,128)(2,1)S(1)} %get-tuple-element.70), channel_id=1, source_target_pairs={{0,4},{1,5},{2,6},{3,7},{4,0},{5,1},{6,2},{7,3},{8,12},{9,13},{10,... | collective-permute-start | bytes 1277960 | tf_op jit(solution)/shard_map/ppermute | solution.py:384
  8.0 21.4 %collective-permute-start.27 = (bf16[208,1024]{1,0:T(8,128)(2,1)S(1)}, bf16[208,1024]{1,0:T(8,128)(2,1)S(1)}, u32[]{:S(2)}, u32[]{:S(2)}) collective-permute-start(bf16[208,1024]{1,0:T(8,128)(2,1)S(1)} %after.12.refs_1_), channel_id=1, source_target_pairs={{0,9},{1,0},{2,11},{3,2},{4,13},{5,4},{6,15},{7,6},{8,1},{9,8},{10... | collective-permute-start | bytes 1277960 | tf_op jit(solution)/shard_map/ppermute | solution.py:384
  9.3 21.2 %collective-permute-start.26 = (bf16[208,1024]{1,0:T(8,128)(2,1)S(1)}, bf16[208,1024]{1,0:T(8,128)(2,1)S(1)}, u32[]{:S(2)}, u32[]{:S(2)}) collective-permute-start(bf16[208,1024]{1,0:T(8,128)(2,1)S(1)} %after.12.refs_1_), channel_id=1, source_target_pairs={{0,24},{1,17},{2,26},{3,19},{4,28},{5,21},{6,30},{7,23},{8,16},{9,... | collective-permute-start | bytes 1277960 | tf_op jit(solution)/shard_map/ppermute | solution.py:384
  11.9 24.1 %collective-permute-start.31 = (bf16[208,1024]{1,0:T(8,128)(2,1)S(1)}, bf16[208,1024]{1,0:T(8,128)(2,1)S(1)}, u32[]{:S(2)}, u32[]{:S(2)}) collective-permute-start(bf16[208,1024]{1,0:T(8,128)(2,1)S(1)} %after.14), channel_id=1, source_target_pairs={{0,2},{1,3},{2,0},{3,1},{4,6},{5,7},{6,4},{7,5},{8,10},{9,11},{10,... | collective-permute-start | bytes 1277960 | tf_op jit(solution)/shard_map/ppermute | solution.py:384
  27.6 8.4 %collective-permute-start.24 = (bf16[208,1024]{1,0:T(8,128)(2,1)S(1)}, bf16[208,1024]{1,0:T(8,128)(2,1)S(1)}, u32[]{:S(2)}, u32[]{:S(2)}) collective-permute-start(bf16[208,1024]{1,0:T(8,128)(2,1)S(1)} %collective-permute-done.21.refs_1_), channel_id=1, source_target_pairs={{0,8},{1,9},{2,10},{3,11},{4,12},{5,13},{6,14},{7,15},{8,0},{9,1},... | collective-permute-start | bytes 1277960 | tf_op jit(solution)/shard_map/ppermute | solution.py:384
  27.6 12.6 %collective-permute-start.23 = (bf16[208,1024]{1,0:T(8,128)(2,1)S(1)}, bf16[208,1024]{1,0:T(8,128)(2,1)S(1)}, u32[]{:S(2)}, u32[]{:S(2)}) collective-permute-start(bf16[208,1024]{1,0:T(8,128)(2,1)S(1)} %collective-permute-done.21.refs_1_), channel_id=1, source_target_pairs={{0,9},{1,0},{2,11},{3,2},{4,13},{5,4},{6,15},{7,6},{8,1},{9,8},{10... | collective-permute-start | bytes 1277960 | tf_op jit(solution)/shard_map/ppermute | solution.py:384
  29.3 12.7 %collective-permute-start.22 = (bf16[208,1024]{1,0:T(8,128)(2,1)S(1)}, bf16[208,1024]{1,0:T(8,128)(2,1)S(1)}, u32[]{:S(2)}, u32[]{:S(2)}) collective-permute-start(bf16[208,1024]{1,0:T(8,128)(2,1)S(1)} %collective-permute-done.21.refs_1_), channel_id=1, source_target_pairs={{0,24},{1,17},{2,26},{3,19},{4,28},{5,21},{6,30},{7,23},{8,16},{9,... | collective-permute-start | bytes 1277960 | tf_op jit(solution)/shard_map/ppermute | solution.py:384
  30.4 14.7 %collective-permute-start.20 = (bf16[208,1024]{1,0:T(8,128)(2,1)S(1)}, bf16[208,1024]{1,0:T(8,128)(2,1)S(1)}, u32[]{:S(2)}, u32[]{:S(2)}) collective-permute-start(bf16[208,1024]{1,0:T(8,128)(2,1)S(1)} %get-tuple-element.69), channel_id=1, source_target_pairs={{0,6},{1,7},{2,4},{3,5},{4,2},{5,3},{6,0},{7,1},{8,14},{9,15},{10,... | collective-permute-start | bytes 1277960 | tf_op jit(solution)/shard_map/ppermute | solution.py:384
  35.9 13.4 %collective-permute-start.34 = (bf16[208,1024]{1,0:T(8,128)(2,1)S(1)}, bf16[208,1024]{1,0:T(8,128)(2,1)S(1)}, u32[]{:S(2)}, u32[]{:S(2)}) collective-permute-start(bf16[208,1024]{1,0:T(8,128)(2,1)S(1)} %after.15.refs_1_), channel_id=1, source_target_pairs={{0,9},{1,0},{2,11},{3,2},{4,13},{5,4},{6,15},{7,6},{8,1},{9,8},{10... | collective-permute-start | bytes 1277960 | tf_op jit(solution)/shard_map/ppermute | solution.py:384
  36.0 14.1 %collective-permute-start.33 = (bf16[208,1024]{1,0:T(8,128)(2,1)S(1)}, bf16[208,1024]{1,0:T(8,128)(2,1)S(1)}, u32[]{:S(2)}, u32[]{:S(2)}) collective-permute-start(bf16[208,1024]{1,0:T(8,128)(2,1)S(1)} %after.15.refs_1_), channel_id=1, source_target_pairs={{0,24},{1,17},{2,26},{3,19},{4,28},{5,21},{6,30},{7,23},{8,16},{9,... | collective-permute-start | bytes 1277960 | tf_op jit(solution)/shard_map/ppermute | solution.py:384
  40.2 9.9 %collective-permute-start.32 = (bf16[208,1024]{1,0:T(8,128)(2,1)S(1)}, bf16[208,1024]{1,0:T(8,128)(2,1)S(1)}, u32[]{:S(2)}, u32[]{:S(2)}) collective-permute-start(bf16[208,1024]{1,0:T(8,128)(2,1)S(1)} %after.15.refs_1_), channel_id=1, source_target_pairs={{0,8},{1,9},{2,10},{3,11},{4,12},{5,13},{6,14},{7,15},{8,0},{9,1},... | collective-permute-start | bytes 1277960 | tf_op jit(solution)/shard_map/ppermute | solution.py:384
  45.2 9.8 %collective-permute-start.30 = (bf16[208,1024]{1,0:T(8,128)(2,1)S(1)}, bf16[208,1024]{1,0:T(8,128)(2,1)S(1)}, u32[]{:S(2)}, u32[]{:S(2)}) collective-permute-start(bf16[208,1024]{1,0:T(8,128)(2,1)S(1)} %after.13.refs_1_), channel_id=1, source_target_pairs={{0,8},{1,9},{2,10},{3,11},{4,12},{5,13},{6,14},{7,15},{8,0},{9,1},... | collective-permute-start | bytes 1277960 | tf_op jit(solution)/shard_map/ppermute | solution.py:384
  45.2 13.4 %collective-permute-start.29 = (bf16[208,1024]{1,0:T(8,128)(2,1)S(1)}, bf16[208,1024]{1,0:T(8,128)(2,1)S(1)}, u32[]{:S(2)}, u32[]{:S(2)}) collective-permute-start(bf16[208,1024]{1,0:T(8,128)(2,1)S(1)} %after.13.refs_1_), channel_id=1, source_target_pairs={{0,9},{1,0},{2,11},{3,2},{4,13},{5,4},{6,15},{7,6},{8,1},{9,8},{10... | collective-permute-start | bytes 1277960 | tf_op jit(solution)/shard_map/ppermute | solution.py:384
  49.4 11.1 %collective-permute-start.28 = (bf16[208,1024]{1,0:T(8,128)(2,1)S(1)}, bf16[208,1024]{1,0:T(8,128)(2,1)S(1)}, u32[]{:S(2)}, u32[]{:S(2)}) collective-permute-start(bf16[208,1024]{1,0:T(8,128)(2,1)S(1)} %after.13.refs_1_), channel_id=1, source_target_pairs={{0,24},{1,17},{2,26},{3,19},{4,28},{5,21},{6,30},{7,23},{8,16},{9,... | collective-permute-start | bytes 1277960 | tf_op jit(solution)/shard_map/ppermute | solution.py:384
  54.9 22.5 %copy-start = (bf16[768,1024]{1,0:T(8,128)(2,1)S(1)}, bf16[768,1024]{1,0:T(8,128)(2,1)}, u32[]{:S(2)}) copy-start(bf16[768,1024]{1,0:T(8,128)(2,1)} %emb.1) | copy-start | bytes 4718596
  54.9 22.5 %copy-start.1 = (s32[768]{0:T(1024)S(1)}, s32[768]{0:T(1024)}, u32[]{:S(2)}) copy-start(s32[768]{0:T(1024)} %param.6) | copy-start | bytes 9220
  54.9 22.5 %copy-start.2 = (s32[768]{0:T(1024)S(1)}, s32[768]{0:T(1024)}, u32[]{:S(2)}) copy-start(s32[768]{0:T(1024)} %param.7) | copy-start | bytes 9220
  63.3 3.3 %collective-permute-start.35 = (f32[1,1152]{1,0:T(1,128)S(1)}, f32[1,1152]{1,0:T(1,128)S(1)}, u32[]{:S(2)}, u32[]{:S(2)}) collective-permute-start(f32[1,1152]{1,0:T(1,128)S(1)} %get-tuple-element.87), channel_id=1, source_target_pairs={{0,1},{1,8},{2,3},{3,10},{4,5},{5,12},{6,7},{7,14},{8,9},{9,0},{10... | collective-permute-start | bytes 13832 | tf_op jit(solution)/shard_map/ppermute | solution.py:384
  64.8 3.1 %collective-permute-start.36 = (f32[1,1152]{1,0:T(1,128)S(1)}, f32[1,1152]{1,0:T(1,128)S(1)}, u32[]{:S(2)}, u32[]{:S(2)}) collective-permute-start(f32[1,1152]{1,0:T(1,128)S(1)} %get-tuple-element.88), channel_id=1, source_target_pairs={{0,16},{1,25},{2,18},{3,27},{4,20},{5,29},{6,22},{7,31},{8,24},{9,... | collective-permute-start | bytes 13832 | tf_op jit(solution)/shard_map/ppermute | solution.py:384
  67.9 7.1 %collective-permute-start.39 = (f32[1,1152]{1,0:T(1,128)S(1)}, f32[1,1152]{1,0:T(1,128)S(1)}, u32[]{:S(2)}, u32[]{:S(2)}) collective-permute-start(f32[1,1152]{1,0:T(1,128)S(1)} %maximum_maximum_fusion.1.refs_0_), channel_id=1, source_target_pairs={{0,6},{1,7},{2,4},{3,5},{4,2},{5,3},{6,0},{7,1},{8,14},{9,15},{10,... | collective-permute-start | bytes 13832 | tf_op jit(solution)/shard_map/ppermute | solution.py:384
  71.4 4.5 %collective-permute-start.38 = (f32[1,1152]{1,0:T(1,128)S(1)}, f32[1,1152]{1,0:T(1,128)S(1)}, u32[]{:S(2)}, u32[]{:S(2)}) collective-permute-start(f32[1,1152]{1,0:T(1,128)S(1)} %maximum_maximum_fusion.1.refs_0_), channel_id=1, source_target_pairs={{0,4},{1,5},{2,6},{3,7},{4,0},{5,1},{6,2},{7,3},{8,12},{9,13},{10,... | collective-permute-start | bytes 13832 | tf_op jit(solution)/shard_map/ppermute | solution.py:384
  73.7 3.6 %collective-permute-start.37 = (f32[1,1152]{1,0:T(1,128)S(1)}, f32[1,1152]{1,0:T(1,128)S(1)}, u32[]{:S(2)}, u32[]{:S(2)}) collective-permute-start(f32[1,1152]{1,0:T(1,128)S(1)} %maximum_maximum_fusion.1.refs_0_), channel_id=1, source_target_pairs={{0,2},{1,3},{2,0},{3,1},{4,6},{5,7},{6,4},{7,5},{8,10},{9,11},{10,... | collective-permute-start | bytes 13832 | tf_op jit(solution)/shard_map/ppermute | solution.py:384
  77.7 0.6 copy-start.3
